TPU v7x, 32 devices: a whole 2x2x4 slice. The times are simulated.
32 devices in a mesh: rep: 4 (over y, x), seq: 8 (over z, core).
Axes of the slice: x: 2, y: 2, z: 4, core: 2. Of those that a mesh axis runs over, the one named last changes fastest.
Arguments:
- tokens: bfloat16 [8, 2048, 2048], P('rep', 'seq'), may hold values from -6 to 6
- lengths: int32 [8], P('rep'), may hold values from 512 to 2048, as said below
- pre_gain: float32 [2048], replicated, may hold values from 0.5 to 1.5
- in_weight: bfloat16 [2048, 8512], P('seq'), may hold values from -0.125 to 0.125
- conv_weight: float32 [4, 4352], replicated, may hold values from -3 to 3
- conv_bias: float32 [4352], replicated, may hold values from -3 to 3
- step_bias: float32 [64], replicated, may hold values from -2 to 1
- decay_log: float32 [64], replicated, may hold values from -13 to -3
- skip_gain: float32 [64], replicated, may hold values from 0.5 to 1.5
- norm_gain: float32 [4096], replicated, may hold values from 0.5 to 1.5
- out_weight: bfloat16 [4096, 2048], P('seq'), may hold values from -0.09375 to 0.09375
- cotangent: bfloat16 [8, 2048, 2048], P('rep', 'seq'), may hold values from -6 to 6
Outputs:
- output: bfloat16 [8, 2048, 2048], P('rep', 'seq')
- tokens_grad: float32 [8, 2048, 2048], P('rep', 'seq')
- pre_gain_grad: float32 [2048], replicated
- in_weight_grad: float32 [2048, 8512], P('seq')
- conv_weight_grad: float32 [4, 4352], replicated
- conv_bias_grad: float32 [4352], replicated
- step_bias_grad: float32 [64], replicated
- decay_log_grad: float32 [64], replicated
- skip_gain_grad: float32 [64], replicated
- norm_gain_grad: float32 [4096], replicated
- out_weight_grad: float32 [4096, 2048], P('seq')
Inputs may be any that keep to these rules, and one draw needn't show every extreme that they name: `lengths`: each replica group's 2 slots hold one of length 2048; one slot of all has length 512; the others lie evenly between.
All inputs are finite; a program needn't handle non-finite values.
Results may differ from a plain program's by a relative error of at most 0.0091.
Values may be sent and summed in bfloat16 or wider, within the bound.
No kernel may reach another device: no remote copies, remote signals or barrier semaphores. Data moves between devices by JAX's collectives and lax.ppermute only.
A program may use at most 576 MiB of HBM per device.

v0:
```python
import jax
import jax.numpy as jnp
from jax import lax
from jax.sharding import PartitionSpec as P

HEADS = 64
HEAD_DIM = 64
STATE = 128
KCONV = 4


EPSILON = 1e-05
HIGHEST_PRECISION = lax.Precision.HIGHEST


def from_behind(shard, axis, by):
    size = lax.axis_size(axis)
    pairs = [(i, i + by) for i in range(size) if 0 <= i + by < size]
    return lax.ppermute(shard, axis, pairs)


def entering(part, axis, combine, identity, reverse):
    count = lax.axis_size(axis)
    place = lax.axis_index(axis)
    ahead = count - 1 - place if reverse else place
    gathered = jax.tree.map(lambda a: lax.all_gather(a, axis), part)
    state = jax.tree.map(lambda a, e: jnp.zeros_like(a) + jnp.asarray(e, a.dtype), part, identity)

    def one(turn, state):
        source = count - 1 - turn if reverse else turn
        return combine(
            state, jax.tree.map(lambda a: lax.dynamic_index_in_dim(a, source, 0, False), gathered)
        )

    return lax.fori_loop(0, ahead, one, state)


def rms_scale(values, gain):
    return values * lax.rsqrt(jnp.mean(values * values, axis=-1, keepdims=True) + EPSILON) * gain


def silu_apply(values):
    return values * jax.nn.sigmoid(values)


def state_terms(head_inputs, b_rows, step_size, decay_rate):
    log_decay = jnp.cumsum(-step_size * decay_rate, axis=1)
    last_log = log_decay[:, -1, :]
    to_end = jnp.exp(last_log[:, None, :] - log_decay) * step_size
    local_state = jnp.einsum(
        "msh,mshp,msn->mhpn", to_end, head_inputs, b_rows, precision=HIGHEST_PRECISION
    )
    return (jnp.exp(last_log), local_state)


def out_terms(head_inputs, b_rows, c_rows, step_size, decay_rate, skip_gain, carried):
    log_decay = jnp.cumsum(-step_size * decay_rate, axis=1)
    length = head_inputs.shape[1]
    causal = (
        jnp.arange(length, dtype=jnp.int32)[:, None] >= jnp.arange(length, dtype=jnp.int32)[None, :]
    )
    by_head = jnp.swapaxes(log_decay, 1, 2)
    log_gap = jnp.where(causal, by_head[:, :, :, None] - by_head[:, :, None, :], 0.0)
    decay_map = jnp.where(causal, jnp.exp(log_gap), 0.0)
    scores = jnp.einsum("mtn,msn->mts", c_rows, b_rows, precision=HIGHEST_PRECISION)
    weights = scores[:, None] * decay_map * jnp.swapaxes(step_size, 1, 2)[:, :, None, :]
    inside_group = jnp.einsum("mhts,mshp->mthp", weights, head_inputs, precision=HIGHEST_PRECISION)
    carry_in = (
        jnp.einsum("mtn,mhpn->mthp", c_rows, carried, precision=HIGHEST_PRECISION)
        * jnp.exp(log_decay)[..., None]
    )
    return inside_group + carry_in + skip_gain[:, None] * head_inputs


def front_mixer(extended, step_raw, conv_weight, conv_bias, step_bias, decay_log):
    length = step_raw.shape[1]
    conv_sum = conv_bias + conv_weight[0] * extended[:, 0:length]
    for offset in range(1, KCONV):
        conv_sum = conv_sum + conv_weight[offset] * extended[:, offset : offset + length]
    activated = silu_apply(conv_sum)
    inner_w = activated.shape[-1] - 2 * STATE
    head_inputs = activated[..., :inner_w].reshape(activated.shape[0], length, HEADS, HEAD_DIM)
    b_rows = activated[..., inner_w : inner_w + STATE]
    c_rows = activated[..., inner_w + STATE :]
    step_size = jax.nn.softplus(step_raw + step_bias)
    return (head_inputs, b_rows, c_rows, step_size, jnp.exp(decay_log))


def gated_norm(mixer_flat, gate_raw, norm_gain):
    return rms_scale(mixer_flat * silu_apply(gate_raw), norm_gain)


def chain_states(earlier, later):
    return (earlier[0] * later[0], later[1] + later[0][:, :, None, None] * earlier[1])


def per_device(
    tokens,
    lengths,
    pre_gain,
    in_weight,
    conv_weight,
    conv_bias,
    step_bias,
    decay_log,
    skip_gain,
    norm_gain,
    out_weight,
    cotangent,
):
    slot_count, length, model_width = tokens.shape
    inner_w = norm_gain.shape[0]
    channels = conv_bias.shape[0]
    position = lax.axis_index("seq") * length + jnp.arange(length, dtype=jnp.int32)
    valid_mask = position[None, :] < lengths[:, None]
    token_rows = tokens.astype(jnp.float32)
    normed_float, norm_pull = jax.vjp(rms_scale, token_rows, pre_gain)
    normed = normed_float.astype(jnp.bfloat16)
    in_full, out_full = (
        lax.all_gather(in_weight, "seq", axis=0, tiled=True),
        lax.all_gather(out_weight, "seq", axis=0, tiled=True),
    )
    projected = jnp.einsum(
        "msd,de->mse", normed, in_full, preferred_element_type=jnp.float32
    ).astype(jnp.bfloat16)
    gate_raw = projected[..., :inner_w].astype(jnp.float32)
    mixed = projected[..., inner_w : inner_w + channels]
    step_raw = projected[..., inner_w + channels :].astype(jnp.float32)
    tail_rows = from_behind(mixed[:, length - (KCONV - 1) :], "seq", 1)
    extended = jnp.concatenate([tail_rows, mixed], axis=1).astype(jnp.float32)
    front_values, front_pull = jax.vjp(
        front_mixer, extended, step_raw, conv_weight, conv_bias, step_bias, decay_log
    )
    head_inputs, b_rows, c_rows, step_size, decay_rate = front_values
    (fade_all, local_state), state_pull = jax.vjp(
        state_terms, head_inputs, b_rows, step_size, decay_rate
    )
    start_state = entering(
        (fade_all, local_state),
        "seq",
        chain_states,
        (jnp.ones_like(fade_all), jnp.zeros_like(local_state)),
        False,
    )[1]
    mixer_out, out_pull = jax.vjp(
        jax.checkpoint(out_terms),
        head_inputs,
        b_rows,
        c_rows,
        step_size,
        decay_rate,
        skip_gain,
        start_state,
    )
    mixer_flat = mixer_out.reshape(slot_count, length, inner_w)
    gated_float, gated_pull = jax.vjp(gated_norm, mixer_flat, gate_raw, norm_gain)
    gated_out = gated_float.astype(jnp.bfloat16)
    branch = jnp.einsum("msi,id->msd", gated_out, out_full, preferred_element_type=jnp.float32)
    output = jnp.where(valid_mask[..., None], token_rows + branch, 0.0).astype(jnp.bfloat16)
    in_back, out_back = (
        lax.all_gather(in_weight, "seq", axis=0, tiled=True),
        lax.all_gather(out_weight, "seq", axis=0, tiled=True),
    )
    masked = jnp.where(valid_mask[..., None], cotangent, jnp.zeros_like(cotangent))
    gated_grad = jnp.einsum("msd,id->msi", masked, out_back, preferred_element_type=jnp.float32)
    mixer_grad, gate_grad, norm_gain_part = gated_pull(gated_grad)
    inputs_one, b_one, c_grad, step_one, rate_one, skip_part, start_grad = out_pull(
        mixer_grad.reshape(mixer_out.shape)
    )
    later_grad = entering(
        (fade_all, start_grad),
        "seq",
        chain_states,
        (jnp.ones_like(fade_all), jnp.zeros_like(start_grad)),
        True,
    )[1]
    fade_grad = jnp.sum(later_grad * start_state, axis=(2, 3))
    inputs_two, b_two, step_two, rate_two = state_pull((fade_grad, later_grad))
    ext_grad, step_raw_grad, conv_w_part, conv_b_part, step_bias_part, decay_log_part = front_pull(
        (inputs_one + inputs_two, b_one + b_two, c_grad, step_one + step_two, rate_one + rate_two)
    )
    back_tail = from_behind(ext_grad[:, : KCONV - 1].astype(jnp.bfloat16), "seq", -1).astype(
        jnp.float32
    )
    mixed_grad = ext_grad[:, KCONV - 1 :] + jnp.pad(
        back_tail, ((0, 0), (length - (KCONV - 1), 0), (0, 0))
    )
    projected_grad = jnp.concatenate([gate_grad, mixed_grad, step_raw_grad], axis=-1).astype(
        jnp.bfloat16
    )
    normed_grad = jnp.einsum(
        "mse,de->msd", projected_grad, in_back, preferred_element_type=jnp.float32
    )
    rows_grad, pre_gain_part = norm_pull(normed_grad)
    tokens_grad = jnp.where(valid_mask[..., None], cotangent.astype(jnp.float32), 0.0) + rows_grad
    rows = normed
    in_shard = lax.psum_scatter(
        jnp.einsum("msd,mse->de", rows, projected_grad, preferred_element_type=jnp.float32),
        "seq",
        scatter_dimension=0,
        tiled=True,
    )
    rows = gated_out
    out_shard = lax.psum_scatter(
        jnp.einsum("msi,msd->id", rows, masked, preferred_element_type=jnp.float32),
        "seq",
        scatter_dimension=0,
        tiled=True,
    )
    in_weight_grad, out_weight_grad = lax.psum((in_shard, out_shard), "rep")
    summed_small = lax.psum(
        (
            pre_gain_part,
            conv_w_part,
            conv_b_part,
            step_bias_part,
            decay_log_part,
            skip_part,
            norm_gain_part,
        ),
        ("rep", "seq"),
    )
    return (
        output,
        tokens_grad,
        summed_small[0],
        in_weight_grad,
        summed_small[1],
        summed_small[2],
        summed_small[3],
        summed_small[4],
        summed_small[5],
        summed_small[6],
        out_weight_grad,
    )


def solution(mesh):
    in_specs = (
        P("rep", "seq", None),
        P("rep"),
        P(),
        P("seq", None),
        P(),
        P(),
        P(),
        P(),
        P(),
        P(),
        P("seq", None),
        P("rep", "seq", None),
    )
    out_specs = (
        P("rep", "seq", None),
        P("rep", "seq", None),
        P(),
        P("seq", None),
        P(),
        P(),
        P(),
        P(),
        P(),
        P(),
        P("seq", None),
    )
    return jax.shard_map(
        per_device, mesh=mesh, in_specs=in_specs, out_specs=out_specs, check_vma=False
    )
```

profile of v0, /device:TPU:0, one launch (start us, length us, event | category | flops | bytes accessed | tf_op | source)
XLA Modules:
  0.0 2666.8 jit_solution(646531954753342715)
XLA Ops:
  13.4 302.7 %all-gather.8.cloned.1.call-done = bf16[2048,8512]{0,1:T(8,128)(2,1)} async-done(((bf16[256,8512]{0,1:T(8,128)(2,1)}), bf16[2048,8512]{0,1:T(8,128)(2,1)}) %all-gather.8.cloned.1.call-update) | async-done | bytes 34865168 | tf_op jit(solution)/shard_map/all_gather | solution.py:120
  316.1 25.3 fusion.2
  341.4 22.7 copy.250
  386.1 18.5 fusion.122
  438.5 29.6 %all-gather.10.cloned.1.call-done = bf16[4096,2048]{1,0:T(8,128)(2,1)} async-done(((bf16[512,2048]{1,0:T(8,128)(2,1)}), bf16[4096,2048]{1,0:T(8,128)(2,1)}) %all-gather.10.cloned.1.call-update) | async-done | bytes 16777232 | tf_op jit(solution)/shard_map/all_gather | solution.py:121
  494.3 41.7 %fusion.9 = f32[2,64,64,256]{3,2,1,0:T(8,128)} fusion(f32[2,256,64,64]{1,3,2,0:T(8,128)} %bitcast.171, f32[2,64,256]{2,1,0:T(8,128)S(1)} %copy.258, f32[2,64,256]{2,1,0:T(8,128)S(1)} %copy.256, f32[2,256,256]{2,1,0:T(8,128)S(1)} %fusion.98, pred[256,256]{1,0:T(8,128)(4,1)S(1)} %iota_compare_fusion), kind=kOutput, calls=%fused_computation.17 | convolution fusion | flops 6484393984 | bytes 17629184 | tf_op jit(solution)/shard_map/jvp(mhts,mshp->mthp)/dot_general | solution.py:67
  536.0 221.7 %all-gather.12.cloned.1.call-done = f32[16,64,64,128]{3,2,1,0:T(8,128)} async-done(((f32[2,64,64,128]{3,2,1,0:T(8,128)}), f32[16,64,64,128]{3,2,1,0:T(8,128)}) %all-gather.12.cloned.1.call-update) | async-done | bytes 33554448 | tf_op jit(solution)/shard_map/all_gather | solution.py:26
  806.0 21.6 multiply_reduce_fusion.7
  827.9 34.4 %fusion.42 = (bf16[2,256,4096]{2,0,1:T(2,128)(2,1)}, f32[2,256,4096]{2,0,1:T(2,128)}, bf16[2,256,4096]{2,0,1:T(2,128)(2,1)}) fusion(f32[2,256,4096]{2,0,1:T(2,128)} %copy.264, f32[2,256,4096]{2,0,1:T(2,128)} %get-tuple-element.208, f32[2,256]{0,1:T(8,128)S(1)} %copy.270, f32[2,256,4096]{2,1,0:T(8,128)} %fusion.18, f32[4096]{0:T(1024)S(1)} %copy-done.26, ...), kind=kLoop, calls=%fused_computation.66 | loop fusion | flops 46137344 | bytes 46157824 | tf_op jit(solution)/shard_map/convert.2
  889.4 58.2 %fusion.17 = (f32[2,64,256]{2,1,0:T(8,128)S(1)}, f32[2,64,256]{2,1,0:T(8,128)S(1)}, f32[2,64,256]{2,1,0:T(8,128)S(1)}, f32[2,256,256]{2,1,0:T(8,128)S(1)}) fusion(f32[2,256,256]{2,1,0:T(8,128)S(1)} %fusion.106, f32[2,64,256]{2,1,0:T(8,128)S(1)} %copy_bitcast_fusion, f32[2,64,256]{2,1,0:T(8,128)S(1)} %copy.275, pred[256,256]{1,0:T(8,128)(4,1)S(1)} %iota_compare_fusion, ...), kind=kOutput, calls=%fused_computation.25 | convolution fusion | flops 6568050688 | bytes 18546688 | tf_op jit(solution)/shard_map/transpose(jvp(jvp()))/checkpoint/mhts,mshp->mthp/dot_general | solution.py:67
  967.3 18.0 convolution_bitcast_fusion.1
  1009.7 274.4 %all-gather.14.cloned.1.call-done = f32[16,64,64,128]{3,2,1,0:T(8,128)} async-done(((f32[2,64,64,128]{3,2,1,0:T(8,128)}), f32[16,64,64,128]{3,2,1,0:T(8,128)}) %all-gather.14.cloned.1.call-update) | async-done | bytes 33554448 | tf_op jit(solution)/shard_map/all_gather | solution.py:26
  1286.7 42.2 %while.27 = (s32[]{:T(128)}, f32[2,64,64,128]{3,2,1,0:T(8,128)}, s32[]{:T(128)}, f32[8,2,64,64,128]{4,3,2,1,0:T(8,128)}, f32[8,2,64]{2,1,0:T(2,128)S(1)}, /*index=5*/s32[]{:T(128)}, s32[]{:T(128)}, s32[]{:T(128)}, s32[]{:T(128)}) while((s32[]{:T(128)}, f32[2,64,64,128]{3,2,1,0:T(8,128)}, s32[]{:T(128)}, f32[8,2,64,64,128]{4,3,2,1,0:T(8,128)}, ...), condition=%wide.region_11.12_spmd, body=%wide.region_10.11_spmd.sunk | while | flops 2097158 | bytes 12584603 | solution.py:35
  1351.3 34.5 %fusion.43 = f32[2,256,64,64]{1,3,2,0:T(8,128)} fusion(f32[2,256,64,64]{1,3,2,0:T(8,128)} %get-tuple-element.233, f32[2,256,64,64]{1,3,2,0:T(8,128)} %bitcast.178, f32[64]{0:T(128)S(1)} %copy-done.43, f32[2,256,64]{1,2,0:T(8,128)S(1)} %copy-done.14, f32[2,256,256]{2,1,0:T(8,128)} %copy-done.16, f32[2,64,256]{2,1,0:T(8,128)S(1)} %copy_bitcast_fusion, ...), kind=kOutput, calls=%fused_computation.68 | convolution fusion | flops 6492782592 | bytes 26149120 | tf_op jit(solution)/shard_map/transpose(jvp(jvp()))/checkpoint/mhts,mshp->mthp/dot_general | solution.py:67
  1416.3 34.1 %multiply_reduce_fusion.5 = (f32[4352]{0:T(1024)S(1)}, f32[4352]{0:T(1024)S(1)}, f32[4352]{0:T(1024)S(1)}, f32[4352]{0:T(1024)S(1)}, f32[4352]{0:T(1024)S(1)}, /*index=5*/f32[2,256,4352]{2,0,1:T(2,128)}) fusion(f32[2,259,4352]{2,0,1:T(2,128)} %copy-done, f32[2,256,4352]{2,0,1:T(2,128)} %get-tuple-element.212, f32[2,256,4096]{2,0,1:T(2,128)S(1)} %copy-done.2, ...), kind=kLoop, calls=%fused_computation.57 | loop fusion | flops 44542720 | bytes 62477312 | tf_op jit(solution)/shard_map/transpose(jvp())/reduce_sum | solution.py:79
  1488.2 30.8 %pad_maximum_fusion = bf16[2,256,8512]{2,0,1:T(2,128)(2,1)} fusion(bf16[2,256,64]{2,0,1:T(2,128)(2,1)S(1)} %get-tuple-element.203, bf16[2,256,4352]{2,0,1:T(2,128)(2,1)S(1)} %fusion.36, bf16[2,256,4096]{2,0,1:T(2,128)(2,1)S(1)} %copy-done.3), kind=kLoop, calls=%fused_computation.60 | loop fusion | flops 26148864 | bytes 17432576 | tf_op jit(solution)/shard_map/concatenate | solution.py:188
  1519.1 22.4 copy.294
  1541.5 30.6 %convolution_bitcast_fusion = f32[2048,8512]{0,1:T(8,128)} fusion(bf16[2,256,8512]{1,2,0:T(8,128)(2,1)} %copy.294, bf16[2,256,2048]{2,1,0:T(8,128)(2,1)S(1)} %copy-done.5, f32[2048]{0:T(1024)S(1)} %copy-done.36, f32[2,256]{1,0:T(2,128)S(1)} %copy-done.38), kind=kOutput, calls=%fused_computation.4 | convolution fusion | flops 17855152128 | bytes 80553984 | tf_op jit(solution)/shard_map/msd,mse->de/dot_general | solution.py:198
  1573.3 37.4 %reduce-scatter.5.cloned.1.call-done = f32[512,2048]{1,0:T(8,128)} async-done(((f32[4096,2048]{1,0:T(8,128)}), f32[512,2048]{1,0:T(8,128)}) %reduce-scatter.5.cloned.1.call-update) | async-done | bytes 4194320 | tf_op jit(solution)/shard_map/reduce_scatter | solution.py:204
  1610.7 665.3 %reduce-scatter.3.cloned.1.call-done = f32[256,8512]{0,1:T(8,128)} async-done(((f32[2048,8512]{0,1:T(8,128)}), f32[256,8512]{0,1:T(8,128)}) %reduce-scatter.3.cloned.1.call-update) | async-done | bytes 8716304 | tf_op jit(solution)/shard_map/reduce_scatter | solution.py:197
  2297.0 24.3 fusion.61
  2321.3 39.1 %all-reduce.13 = (f32[2048]{0:T(1024)}, f32[4352]{0:T(1024)}, f32[64]{0:T(128)}, f32[64]{0:T(128)}, f32[64]{0:T(128)}, /*index=5*/f32[4096]{0:T(1024)}) all-reduce(f32[2048]{0:T(1024)S(1)} %get-tuple-element.168, f32[4352]{0:T(1024)S(1)} %get-tuple-element.167, ...), channel_id=1, replica_groups=mesh['rep'=4,'seq'=8] {'rep','seq'}, use_global_device_ids=true, to_apply=%region_24.25 | all-reduce | flops 10688 | bytes 85504 | tf_op jit(solution)/shard_map/psum | solution.py:211
  2365.3 33.1 %all-reduce.18.cloned.1.call-done = f32[4,4352]{1,0:T(4,128)} async-done(((f32[4,4352]{1,0:T(4,128)}), f32[4,4352]{1,0:T(4,128)}) %all-reduce.18.cloned.1.call-update) | async-done | bytes 69648 | tf_op jit(solution)/shard_map/psum | solution.py:211
  2398.4 251.9 %all-reduce.20.cloned.1.call-done = (f32[256,8512]{0,1:T(8,128)}, f32[512,2048]{1,0:T(8,128)}) async-done(((f32[256,8512]{0,1:T(8,128)}, f32[512,2048]{1,0:T(8,128)}), (f32[256,8512]{0,1:T(8,128)}, f32[512,2048]{1,0:T(8,128)})) %all-reduce.20.cloned.1.call-update) | async-done | bytes 12910608 | tf_op jit(solution)/shard_map/psum | solution.py:210
  (245 shorter events, 379.3 us)
Async XLA Ops:
  7.2 308.9 %copy-start.4 = (bf16[2,256,2048]{2,1,0:T(8,128)(2,1)S(1)}, bf16[2,256,2048]{2,1,0:T(8,128)(2,1)}, u32[]{:S(2)}) copy-start(bf16[2,256,2048]{2,1,0:T(8,128)(2,1)} %param.16) | copy-start | bytes 6291460
  7.2 308.9 %copy-start.35 = (f32[2048]{0:T(1024)S(1)}, f32[2048]{0:T(1024)}, u32[]{:S(2)}) copy-start(f32[2048]{0:T(1024)} %param.18) | copy-start | bytes 24580
  7.2 308.9 %all-gather.8.cloned.1.call-start = ((), (), s32[]{:S(2)}) async-start(), calls=%async_computation.2 | async-start | bytes 39223296 | tf_op jit(solution)/shard_map/all_gather | solution.py:120
  7.9 460.2 %all-gather.10.cloned.1.call-start = ((), (), s32[]{:S(2)}) async-start(), calls=%async_computation.3 | async-start | bytes 18874368 | tf_op jit(solution)/shard_map/all_gather | solution.py:121
  8.7 749.0 %all-gather.12.cloned.1.call-start = ((), (), s32[]{:S(2)}) async-start(), calls=%async_computation.7 | async-start | bytes 37748736 | tf_op jit(solution)/shard_map/all_gather | solution.py:26
  9.4 866.0 %copy-start.33 = (f32[64]{0:T(128)}, f32[64]{0:T(128)S(1)}, u32[]{:S(2)}) copy-start(f32[64]{0:T(128)S(1)} %exp.52) | copy-start | bytes 772
  10.6 375.4 %copy-start.17 = (f32[4352]{0:T(1024)}, f32[4352]{0:T(1024)S(1)}, u32[]{:S(2)}) copy-start(f32[4352]{0:T(1024)S(1)} %get-tuple-element.170) | copy-start | bytes 52228
  10.6 375.4 %copy-start.19 = (f32[4352]{0:T(1024)}, f32[4352]{0:T(1024)S(1)}, u32[]{:S(2)}) copy-start(f32[4352]{0:T(1024)S(1)} %get-tuple-element.171) | copy-start | bytes 52228
  10.7 375.4 %copy-start.21 = (f32[4352]{0:T(1024)}, f32[4352]{0:T(1024)S(1)}, u32[]{:S(2)}) copy-start(f32[4352]{0:T(1024)S(1)} %get-tuple-element.172) | copy-start | bytes 52228
  10.7 375.4 %copy-start.23 = (f32[4352]{0:T(1024)}, f32[4352]{0:T(1024)S(1)}, u32[]{:S(2)}) copy-start(f32[4352]{0:T(1024)S(1)} %get-tuple-element.173) | copy-start | bytes 52228
  13.4 328.0 %copy-start.37 = (f32[2,256]{1,0:T(2,128)}, f32[2,256]{1,0:T(2,128)S(1)}, u32[]{:S(2)}) copy-start(f32[2,256]{1,0:T(2,128)S(1)} %fusion.116) | copy-start | bytes 6148
  364.9 14.4 collective-permute-start
  370.7 112.4 %copy-start.6 = (f32[2,64,2,128]{1,0,3,2:T(2,128)}, f32[2,64,2,128]{1,0,3,2:T(2,128)S(1)}, u32[]{:S(2)}) copy-start(f32[2,64,2,128]{1,0,3,2:T(2,128)S(1)} %copy.255) | copy-start | bytes 393220
  379.3 47.6 %copy-start.13 = (f32[2,256,64]{1,2,0:T(8,128)}, f32[2,256,64]{1,2,0:T(8,128)S(1)}, u32[]{:S(2)}) copy-start(f32[2,256,64]{1,2,0:T(8,128)S(1)} %copy.259) | copy-start | bytes 393220
  427.6 40.6 %copy-start.12 = (bf16[2,256,2048]{2,1,0:T(8,128)(2,1)S(1)}, bf16[2,256,2048]{2,1,0:T(8,128)(2,1)}, u32[]{:S(2)}) copy-start(bf16[2,256,2048]{2,1,0:T(8,128)(2,1)} %param.27) | copy-start | bytes 6291460
  438.1 846.0 %all-gather.14.cloned.1.call-start = ((), (), s32[]{:S(2)}) async-start(), calls=%async_computation.8 | async-start | bytes 37748736 | tf_op jit(solution)/shard_map/all_gather | solution.py:26
  438.5 44.4 %copy-start.39 = (pred[2,256]{1,0:T(4,128)(4,1)}, pred[2,256]{1,0:T(4,128)(4,1)S(1)}, u32[]{:S(2)}) copy-start(pred[2,256]{1,0:T(4,128)(4,1)S(1)} %broadcast_compare_fusion) | copy-start | bytes 1540
  956.2 654.5 %reduce-scatter.5.cloned.1.call-start = ((), (), s32[]{:S(2)}) async-start(), calls=%async_computation.6 | async-start | bytes 37748736 | tf_op jit(solution)/shard_map/reduce_scatter | solution.py:204
  985.3 1290.7 %reduce-scatter.3.cloned.1.call-start = ((), (), s32[]{:S(2)}) async-start(), calls=%async_computation.4 | async-start | bytes 78446592 | tf_op jit(solution)/shard_map/reduce_scatter | solution.py:197
  1286.7 42.2 %copy-start.11 = (f32[2,256,128,1]{2,0,1,3:T(2,128)S(1)}, f32[2,256,128,1]{2,0,1,3:T(2,128)}, u32[]{:S(2)}) copy-start(f32[2,256,128,1]{2,0,1,3:T(2,128)} %copy-done.10) | copy-start | bytes 786436
  1476.5 4.1 collective-permute-start.1
  1572.2 826.2 %all-reduce.18.cloned.1.call-start = ((), (), s32[]{:S(2)}) async-start(), calls=%async_computation.5 | async-start | bytes 139264 | tf_op jit(solution)/shard_map/psum | solution.py:211
  1573.0 1077.2 %all-reduce.20.cloned.1.call-start = ((), (), s32[]{:S(2)}) async-start(), calls=%async_computation.9 | async-start | bytes 25821184 | tf_op jit(solution)/shard_map/psum | solution.py:210
  2297.0 63.3 %copy-start.30 = (f32[2,256]{1,0:T(2,128)S(1)}, f32[2,256]{1,0:T(2,128)}, u32[]{:S(2)}) copy-start(f32[2,256]{1,0:T(2,128)} %copy-done.29) | copy-start | bytes 6148
  (39 other events, 569.9 us)
Sparse Core Ops, SparseCore 0:
  9.6 306.3 all-gather.7
  317.7 150.4 all-gather.9
  470.3 287.3 all-gather.11
  956.3 327.7 all-gather.13
  1286.3 324.2 reduce-scatter.4
  1613.1 662.8 reduce-scatter.2
  2282.1 116.1 all-reduce.17
  2402.1 248.0 all-reduce.19
where the time goes:
time: 2670 us
  waiting for transfers between devices  1820 us (68%)
  matrix products  352 us (13%)
  other arithmetic  278 us (10%)
  local copies, waits for them, and re-layouts  149 us (6%)
  blocking collectives  48.5 us (2%)
    reduce_scatter x1, waiting for transfers between devices, per_device(): lax.psum_scatter(jnp.einsum('msd,mse->de', rows, projected_grad, preferre...  665 us
    all_gather x2, waiting for transfers between devices, entering(): gathered = jax.tree.map(lambda a: lax.all_gather(a, axis), part)  496 us
    all_gather x1, waiting for transfers between devices, per_device(): lax.all_gather(in_weight, 'seq', axis=0, tiled=True)  303 us
    psum x1, waiting for transfers between devices, per_device(): in_weight_grad, out_weight_grad = lax.psum((in_shard, out_shard), 'rep')  252 us
    dot_general x3, matrix products, out_terms(): jnp.einsum('mhts,mshp->mthp', weights, head_inputs, precision=HIGHEST_PRE...  134 us
    another operation x14, other arithmetic  55.7 us
  transfers between devices with their start and end apart: 10, of which 8 were waited for; matrix products, arithmetic and copies ran while one was open for 21% of the time, Pallas kernels for 0%

commit v1 on v0

v1 whole, which is shorter than its diff:
```python
import functools

import jax
import jax.numpy as jnp
from jax import lax
from jax.experimental import pallas as pl
from jax.experimental.pallas import tpu as pltpu
from jax.sharding import PartitionSpec as P

HEADS = 64
HEAD_DIM = 64
STATE = 128
KCONV = 4
LANES = 128
PAD = 8
COST = 1.0
LOW = 1.0
MARK = 16
EPSILON = 1e-05
NEVER = -1e30
BF16 = jnp.bfloat16
F32 = jnp.float32


def swap(value, axis, bit):
    return lax.ppermute(value, axis, [(i, i ^ bit) for i in range(lax.axis_size(axis))])


def after(value, *others):
    return lax.optimization_barrier((value,) + others)[0]


def gather_near(own):
    return own, swap(own, "rep", 1), swap(own, "rep", 2)


def to_far(near):
    own, one, two = near
    half = own.shape[0] // 2
    return one[:half], two[half:]


def far_parts(near, sent):
    return list(near) + [swap(sent[0], "rep", 2), swap(sent[1], "rep", 1)]


def gather_direct(own):
    return [own] + [swap(own, "rep", j) for j in (1, 2, 3)]


def scatter_direct(parts):
    total = parts[0].astype(F32)
    for j in (1, 2, 3):
        total = total + swap(parts[j], "rep", j).astype(F32)
    return total


def in_order(blocks):
    stack = jnp.stack(blocks)
    place = lax.axis_index("rep")
    return [lax.dynamic_index_in_dim(stack, place ^ q, 0, False) for q in range(len(blocks))]


def sum_seq(value):
    bit = 1
    while bit < lax.axis_size("seq"):
        value = value + swap(value, "seq", bit)
        bit *= 2
    return value


class SmallSums:
    def __init__(self, value):
        self.value, self.bit = value, 1

    def hop(self):
        if self.bit < lax.axis_size("seq"):
            sent = self.value
            self.value = sent + swap(sent, "seq", self.bit)
            self.bit *= 2
        return sent

    def rest(self):
        while self.bit < lax.axis_size("seq"):
            self.hop()
        return self.value


def sum_aligned(blocks):
    total = blocks
    for bit in (1, 2, 3):
        other = swap(blocks, "rep", bit)
        total = total + jnp.stack([other[j ^ bit] for j in range(blocks.shape[0])])
    return total


class Chain:
    def __init__(self, fade, part, message, reverse):
        count = lax.axis_size("seq")
        self.chips = count // 2
        first, lead = (1, 0) if reverse else (0, 1)
        hop = -1 if reverse else 1
        chips = range(self.chips)
        self.fade, self.part = fade, part
        self.homeward = [(2 * c + lead, 2 * c + first) for c in chips]
        onward = [(2 * c + lead, 2 * (c + hop) + lead) for c in chips if 0 <= c + hop < self.chips]
        self.onward = onward[::hop]
        self.leads = lax.axis_index("seq") % 2 == lead
        self.got = lax.ppermute(message, "seq", [(2 * c + first, 2 * c + lead) for c in chips])
        self.total = None
        self.enters = 0.0

    def hop(self):
        if self.total is None:
            got = self.got
            self.mate = got[:, :STATE].astype(F32)
            self.mate_fade = got[:, STATE : STATE + 1].astype(F32) + got[:, STATE + 1 : STATE + 2].astype(F32)
            self.total = self.part + self.fade * self.mate
            self.total_fade = self.fade * self.mate_fade
            onto = self.total.astype(BF16)
        else:
            onto = (self.total + self.total_fade * self.enters.astype(F32)).astype(BF16)
        self.enters = self.enters + lax.ppermute(onto, "seq", [self.onward.pop(0)])
        return onto

    def rest(self):
        while self.onward:
            self.hop()

    def back(self):
        self.handed = lax.ppermute(self.enters, "seq", self.homeward)
        return self.enters

    def end(self):
        own = (self.mate + self.mate_fade * self.enters.astype(F32)).astype(BF16)
        return jnp.where(self.leads, own, self.handed)


def nt(a, b):
    return lax.dot_general(a, b, (((1,), (1,)), ((), ())), preferred_element_type=F32)


def tn(a, b):
    return lax.dot_general(a, b, (((0,), (0,)), ((), ())), preferred_element_type=F32)


def nn(a, b):
    return jnp.dot(a, b, preferred_element_type=F32)


def col(p):
    return slice(p * LANES, (p + 1) * LANES)


def two_parts(value):
    heads = LANES // 4
    high = value.astype(BF16)
    low = (value - high.astype(F32)).astype(BF16).astype(F32)
    lane = lax.broadcasted_iota(jnp.int32, value.shape, 1)
    both = jnp.where(
        lane < heads, high.astype(F32), jnp.where(lane < 2 * heads, pltpu.roll(low, heads, 1), 0.0)
    )
    return both.astype(BF16)


def running(value, reverse):
    rows = value.shape[0]
    place = lax.broadcasted_iota(jnp.int32, value.shape, 0)
    shift = 1
    while shift < rows:
        if reverse:
            moved = jnp.where(place < rows - shift, pltpu.roll(value, rows - shift, 0), 0.0)
        else:
            moved = jnp.where(place >= shift, pltpu.roll(value, shift, 0), 0.0)
        value = value + moved
        shift *= 2
    return value


def head_sums(product, fold):
    high = product.astype(BF16)
    low = (product - high.astype(F32)).astype(BF16)
    return nn(high, fold) + nn(low, fold)


def softplus(v):
    return jnp.maximum(v, 0.0) + jnp.log1p(jnp.exp(-jnp.abs(v)))


def sigmoid(v):
    return 1.0 / (1.0 + jnp.exp(-v))


def split(value):
    high = value.astype(BF16)
    return high, (value - high.astype(F32)).astype(BF16)


def nt_fine(a, b):
    half = a.shape[1] // 2
    return nt(
        jnp.concatenate([a, a[:, :half]], axis=1),
        jnp.concatenate([b[:, :half], b[:, :half], b[:, half:]], axis=1),
    )


def nn_fine(a_high, a_low, b):
    half = b.shape[1] // 2
    return nn(
        jnp.concatenate([a_high, a_low, a_high], axis=1),
        jnp.concatenate([b[:, :half], b[:, :half], b[:, half:]], axis=0),
    )


def twice(value):
    return jnp.concatenate([value, value], axis=0)


def tn_sum(a, b):
    both = tn(a, b)
    half = both.shape[0] // 2
    return both[:half] + both[half:]


def message_of(out, p, part, fade):
    out[0, 0:STATE, col(p)] = part.astype(BF16)
    high, low = split(fade)
    place = lax.broadcasted_iota(jnp.int32, (MARK, LANES), 0)
    rows = jnp.where(place == 0, high.astype(F32), jnp.where(place == 1, low.astype(F32), 0.0))
    out[0, STATE : STATE + MARK, col(p)] = rows.astype(BF16)


def front_kernel(
    proj, halo, cw, cb, sb, dl, spread, x_out, bc_out, sl_out, st_out, msg_out, fade_out, ext
):
    rows = proj.shape[0]
    pairs = x_out.shape[1] // LANES
    raw_step = proj[:, (pairs + 2) * LANES :].astype(F32) + sb[...]
    step = softplus(raw_step)
    log_decay = running(-step * jnp.exp(dl[...]), False)
    last = log_decay[rows - 1 : rows, :]
    sl_out[:, :LANES] = step
    sl_out[:, LANES:] = log_decay
    weight = two_parts(jnp.exp(last - log_decay) * step)
    ending = two_parts(jnp.broadcast_to(jnp.exp(last), (PAD, LANES)))
    ext_rows = pl.ds(PAD, rows)

    def activated(p):
        ext[0:PAD, :] = halo[0, :, col(p)]
        ext[ext_rows, :] = proj[:, col(p)].astype(F32)
        z = cb[:, col(p)] + cw[0:1, col(p)] * ext[pl.ds(PAD - 3, rows), :]
        for k in range(1, KCONV):
            z = z + cw[k : k + 1, col(p)] * ext[pl.ds(PAD - 3 + k, rows), :]
        return z * sigmoid(z)

    b_rows = jnp.concatenate(split(activated(pairs)), axis=1)
    bc_out[:, : 2 * STATE] = b_rows
    bc_out[:, 2 * STATE :] = jnp.concatenate(split(activated(pairs + 1)), axis=1)
    for p in range(pairs):
        x = activated(p)
        x_out[:, col(p)] = x
        scaled = (x * nn(weight, spread[:, col(p)])).astype(BF16)
        part = tn_sum(b_rows, scaled)
        fade = nn(ending, spread[:, col(p)])[0:1, :]
        st_out[0, :, col(p)] = part
        fade_out[0, :, col(p)] = fade
        message_of(msg_out, p, part, fade)


def inside_kernel(x, bc, sl, spread, y_out):
    rows = x.shape[0]
    pairs = x.shape[1] // LANES
    scores = nt_fine(bc[:, 2 * STATE :], bc[:, : 2 * STATE])
    log_decay = sl[:, LANES:]
    across = log_decay.T
    step = two_parts(sl[:, :LANES])
    t = lax.broadcasted_iota(jnp.int32, (rows, rows), 0)
    s = lax.broadcasted_iota(jnp.int32, (rows, rows), 1)
    causal = t >= s
    low_lanes = lax.broadcasted_iota(jnp.int32, (rows, LANES), 1) < HEAD_DIM
    for p in range(pairs):
        scaled = (x[:, col(p)] * nn(step, spread[:, col(p)])).astype(BF16)
        outs = []
        for h in (2 * p, 2 * p + 1):
            gap = log_decay[:, h : h + 1] - across[h : h + 1, :]
            weights = (scores * jnp.exp(jnp.where(causal, gap, NEVER))).astype(BF16)
            outs.append(nn(weights, scaled))
        y_out[:, col(p)] = jnp.where(low_lanes, outs[0], outs[1])


def gate_kernel(y, x, bc, sl, start, gate, grad, gain, skip, spread, y_out, sums_out):
    rows = x.shape[0]
    pairs = x.shape[1] // LANES
    c_rows = bc[:, 2 * STATE :]
    decay = two_parts(jnp.exp(sl[:, LANES:]))
    squares = jnp.zeros((rows, LANES), F32)
    cross = jnp.zeros((rows, LANES), F32)
    for p in range(pairs):
        plain = y[:, col(p)] + nn(decay, spread[:, col(p)]) * nn(c_rows, twice(start[0, :, col(p)]))
        y_out[:, col(p)] = plain
        g = gate[:, col(p)].astype(F32)
        v = (plain + skip[:, col(p)] * x[:, col(p)]) * (g * sigmoid(g))
        squares = squares + v * v
        cross = cross + grad[:, col(p)].astype(F32) * gain[:, col(p)] * v
    lane = lax.broadcasted_iota(jnp.int32, (rows, LANES), 1)
    both = jnp.where(
        lane == 0,
        jnp.sum(squares, axis=1, keepdims=True),
        jnp.where(lane == 1, jnp.sum(cross, axis=1, keepdims=True), 0.0),
    )
    sums_out[0] = both.T[0:PAD, :]


def norm_kernel(
    inner, y, x, bc, sl, gate, grad, gain, skip, fade, sums, spread,
    gated_out, dy_out, dgate_out, dstart_out, msg_out, gain_out, skip_out,
):
    rows = x.shape[0]
    pairs = x.shape[1] // LANES

    @pl.when(pl.program_id(0) == 0)
    def _():
        gain_out[...] = jnp.zeros_like(gain_out)
        skip_out[...] = jnp.zeros_like(skip_out)

    c_rows = bc[:, 2 * STATE :]
    decay = two_parts(jnp.exp(sl[:, LANES:]))
    padded = jnp.concatenate([sums[0], jnp.zeros((LANES - PAD, rows), F32)], axis=0).T
    scale = lax.rsqrt(padded[:, 0:1] / inner + EPSILON)
    back = scale * scale * (padded[:, 1:2] / inner)
    for p in range(pairs):
        g = gate[:, col(p)].astype(F32)
        sg = sigmoid(g)
        silu = g * sg
        xp = x[:, col(p)]
        yp = y[:, col(p)] + skip[:, col(p)] * xp
        v = yp * silu
        gp = grad[:, col(p)].astype(F32)
        normal = v * scale
        gated_out[:, col(p)] = (normal * gain[:, col(p)]).astype(BF16)
        gain_out[0:1, col(p)] += jnp.sum(gp * normal, axis=0, keepdims=True)
        dv = scale * (gp * gain[:, col(p)] - v * back)
        dy = (dv * silu).astype(BF16)
        dy_out[:, col(p)] = dy
        dyf = dy.astype(F32)
        dgate_out[:, col(p)] = (dv * yp * (sg * (1.0 + g * (1.0 - sg)))).astype(BF16)
        skip_out[0:1, col(p)] += jnp.sum(dyf * xp, axis=0, keepdims=True)
        faded = (dyf * nn(decay, spread[:, col(p)])).astype(BF16)
        dstart = tn_sum(c_rows, faded)
        dstart_out[0, :, col(p)] = dstart
        message_of(msg_out, p, dstart, fade[0, :, col(p)])


def inside_back_kernel(x, bc, sl, dy, start, spread, dxs_out, dbc_out):
    rows = x.shape[0]
    pairs = x.shape[1] // LANES
    b_rows = bc[:, : 2 * STATE]
    c_rows = bc[:, 2 * STATE :]
    scores = nt_fine(b_rows, c_rows)
    log_decay = sl[:, LANES:]
    across = log_decay.T
    step = two_parts(sl[:, :LANES])
    decay = two_parts(jnp.exp(log_decay))
    s = lax.broadcasted_iota(jnp.int32, (rows, rows), 0)
    t = lax.broadcasted_iota(jnp.int32, (rows, rows), 1)
    causal = t >= s
    low_lanes = lax.broadcasted_iota(jnp.int32, (rows, LANES), 1) < HEAD_DIM
    score_grad = jnp.zeros((rows, rows), F32)
    dc = jnp.zeros((rows, LANES), F32)
    for p in range(pairs):
        scaled = x[:, col(p)] * nn(step, spread[:, col(p)])
        dyp = dy[:, col(p)]
        faded = (dyp.astype(F32) * nn(decay, spread[:, col(p)])).astype(BF16)
        dc = dc + nt(faded, start[0, :, col(p)])
        outs = []
        for h in (2 * p, 2 * p + 1):
            gap = across[h : h + 1, :] - log_decay[:, h : h + 1]
            fall = jnp.exp(jnp.where(causal, gap, NEVER))
            weights = (scores * fall).astype(BF16)
            outs.append(nn(weights, dyp))
            mine = low_lanes if h % 2 == 0 else jnp.logical_not(low_lanes)
            score_grad = score_grad + fall * nt(jnp.where(mine, scaled, 0.0).astype(BF16), dyp)
        dxs_out[:, col(p)] = jnp.where(low_lanes, outs[0], outs[1])
    dbc_out[:, col(0)] = nn_fine(*split(score_grad), c_rows)
    dbc_out[:, col(1)] = dc + nn_fine(*split(score_grad.T), b_rows)


def back_kernel(
    proj, halo, cw, cb, sb, dl, skip, spread, fold, x, bc, sl, y, dy, dxs, dbc, start, part, fade, later,
    pg_out, halo_out, tail_out, cw_out, cb_out, sb_out, dl_out, ext, dext,
):
    rows = x.shape[0]
    pairs = x.shape[1] // LANES

    @pl.when(pl.program_id(0) == 0)
    def _():
        for out in (cw_out, cb_out, sb_out, dl_out):
            out[...] = jnp.zeros_like(out)

    rate = jnp.exp(dl[...])
    step_f = sl[:, :LANES]
    log_decay = sl[:, LANES:]
    last = log_decay[rows - 1 : rows, :]
    step = two_parts(step_f)
    to_end = two_parts(jnp.exp(last - log_decay))
    b_rows = bc[:, : 2 * STATE]
    dext[0:PAD, :] = jnp.zeros((PAD, LANES), F32)
    dext[pl.ds(PAD + rows, PAD), :] = jnp.zeros((PAD, LANES), F32)

    def through_conv(p, grad):
        ext[0:PAD, :] = halo[0, :, col(p)]
        ext[pl.ds(PAD, rows), :] = proj[:, col(p)].astype(F32)
        taps = [ext[pl.ds(PAD - 3 + k, rows), :] for k in range(KCONV)]
        z = cb[:, col(p)] + cw[0:1, col(p)] * taps[0]
        for k in range(1, KCONV):
            z = z + cw[k : k + 1, col(p)] * taps[k]
        sg = sigmoid(z)
        dz = grad * (sg * (1.0 + z * (1.0 - sg)))
        cb_out[0:1, col(p)] += jnp.sum(dz, axis=0, keepdims=True)
        for k in range(KCONV):
            cw_out[k : k + 1, col(p)] += jnp.sum(dz * taps[k], axis=0, keepdims=True)
        dext[pl.ds(PAD, rows), :] = dz
        whole = rows + PAD
        dm = cw[KCONV - 1 : KCONV, col(p)] * dext[pl.ds(0, whole), :]
        for k in range(KCONV - 1):
            dm = dm + cw[k : k + 1, col(p)] * dext[pl.ds(KCONV - 1 - k, whole), :]
        halo_out[0, :, col(p)] = dm[0:PAD, :]
        pg_out[:, col(p)] = dm[PAD:, :].astype(BF16)
        tail_out[0, :, col(p)] = dm[rows:, :]

    db = dbc[:, col(0)]
    dstep = jnp.zeros((rows, LANES), F32)
    dlog = jnp.zeros((rows, LANES), F32)
    dlast = jnp.zeros((PAD, LANES), F32)
    for p in range(pairs):
        xp = x[:, col(p)]
        step_p = nn(step, spread[:, col(p)])
        end_p = nn(to_end, spread[:, col(p)])
        later_p = later[0, :, col(p)]
        dyf = dy[:, col(p)].astype(F32)
        scaled = xp * step_p
        dxs_p = dxs[:, col(p)] + end_p * nn(b_rows, twice(later_p))
        db = db + nt((end_p * scaled).astype(BF16), later_p)
        dstep = dstep + head_sums(xp * dxs_p, fold[col(p), :])
        dlog = dlog + head_sums(dyf * y[:, col(p)] - scaled * dxs_p, fold[col(p), :])
        end_state = fade[0, :, col(p)] * start[0, :, col(p)].astype(F32) + part[0, :, col(p)]
        ends = jnp.sum(later_p.astype(F32) * end_state, axis=0, keepdims=True)
        dlast = dlast + head_sums(jnp.broadcast_to(ends, (PAD, LANES)), fold[col(p), :])
        through_conv(p, step_p * dxs_p + skip[:, col(p)] * dyf)
    through_conv(pairs, db)
    through_conv(pairs + 1, dbc[:, col(1)])
    place = lax.broadcasted_iota(jnp.int32, (rows, LANES), 0)
    dlog = dlog + jnp.where(place == rows - 1, dlast[0:1, :], 0.0)
    da = running(dlog, True)
    dstep = dstep - rate * da
    raw_step = proj[:, (pairs + 2) * LANES :].astype(F32) + sb[...]
    draw = dstep * sigmoid(raw_step)
    pg_out[:, (pairs + 2) * LANES :] = draw.astype(BF16)
    sb_out[0:1, :] += jnp.sum(draw, axis=0, keepdims=True)
    dl_out[0:1, :] += -rate * jnp.sum(step_f * da, axis=0, keepdims=True)


def rows_kernel(product, left, right, out):
    out[...] = product(left[...], right[...]).astype(BF16)


def gathered_kernel(product, own, one, two, low, high, right, out, left):
    half = low.shape[0]
    for j, block in enumerate((own, one, two)):

        @pl.when(pl.program_id(0) == j)
        def _():
            left[...] = block[...]

    @pl.when(pl.program_id(0) == 3)
    def _():
        left[:half, :] = low[...]
        left[half:, :] = high[...]

    out[...] = product(left[...], right[...]).astype(BF16)


def weight_kernel(*refs):
    count = len(refs) // 2
    total = tn(refs[0][...], refs[count][...])
    for m in range(1, count):
        total = total + tn(refs[m][...], refs[count + m][...])
    refs[-1][...] = total.astype(BF16)


def both_weights_kernel(count, *refs):
    normed, gates, gated, cots = (refs[i * count : (i + 1) * count] for i in range(4))
    out = refs[-1]
    gate = sum(tn(a[...], b[...]) for a, b in zip(normed, gates))
    back = sum(tn(a[...], b[...]) for a, b in zip(gated, cots))
    rows, width = gate.shape
    half = back.shape[0]
    out[0, :rows] = gate.astype(BF16)
    for part in range(back.shape[1] // width):
        out[0, rows + part * half : rows + (part + 1) * half] = back[:, part * width : (part + 1) * width].astype(BF16)


def branch_kernel(left, right, *outs):
    value = nn(left[...], right[...]).astype(BF16)
    for q, out in enumerate(outs):

        @pl.when(pl.program_id(0) == q)
        def _():
            out[...] = value


def grad_kernel(mix, gate, w_mix, w_gate, normed, o0, o1, o2, o3, pre):
    @pl.when(pl.program_id(0) == 0)
    def _():
        pre[...] = jnp.zeros_like(pre)

    grad = nt(mix[...], w_mix[...]) + nt(gate[...], w_gate[...])
    pre[0:1, :] += jnp.sum(grad * normed[...].astype(F32), axis=0, keepdims=True)
    grad = grad.astype(BF16)
    for q, out in enumerate((o0, o1, o2, o3)):

        @pl.when(pl.program_id(0) == q)
        def _():
            out[...] = grad


def ordered(place, blocks):
    odd = (place & 1) == 1
    high = (place & 2) == 2
    a, b, c, d = blocks
    a, b = jnp.where(odd, b, a), jnp.where(odd, a, b)
    c, d = jnp.where(odd, d, c), jnp.where(odd, c, d)
    return [jnp.where(high, c, a), jnp.where(high, d, b), jnp.where(high, a, c), jnp.where(high, b, d)]


def turned(place, blocks, out):
    unit = blocks[0].shape[1]
    for q, block in enumerate(ordered(place[0], [b[...].astype(F32) for b in blocks])):
        out[q * unit : (q + 1) * unit, :] = block.T


def gate_grad_kernel(place, g0, g1, g2, g3, out):
    turned(place, (g0, g1, g2, g3), out)


def mix_grad_kernel(groups, heads, before, place, *refs):
    mixes, lasts, (where_heads, out) = refs[:4], refs[4:8], refs[8:]
    step = pl.program_id(0)

    @pl.when(step < groups)
    def _():
        turned(place, mixes, out)

    @pl.when(step == groups)
    def _():
        both = ordered(place[0], [b[:, : 2 * STATE].astype(F32) for b in lasts])
        out[: 2 * STATE, :] = ((both[0] + both[1]) + (both[2] + both[3])).T
        steps = ordered(place[0], [b[:, 2 * STATE :] for b in lasts])
        placed = nn(steps[0], where_heads[0])
        for q in range(1, 4):
            placed = placed + nn(steps[q], where_heads[q])
        out[2 * STATE : 2 * STATE + 4 * heads, :] = placed.T[: 4 * heads, :]


def out_grad_kernel(rows, place, b0, b1, b2, b3, out):
    from_rep = place[0] ^ pl.program_id(0)
    count = out.shape[0]
    for j, block in enumerate((b0, b1, b2, b3)):

        @pl.when(from_rep == j)
        def _():
            width = block.shape[1]
            for part in range(out.shape[1] // width):
                first = rows + part * count
                out[:, part * width : (part + 1) * width] = block[first : first + count, :].astype(F32)


def each(*shape):
    return pl.BlockSpec((1,) + shape, lambda i: (i, 0, 0))


def whole(*shape):
    return pl.BlockSpec(shape, lambda i: (0,) * len(shape))


def call(kernel, slots, ins, outs, scratch, us, held=None, alias=None):
    arrays = [a for a, _ in ins]
    if held is not None:
        arrays[0] = held(arrays[0])
    out_shape = [o for o, _ in outs]
    return pl.pallas_call(
        kernel,
        grid=(slots,),
        in_specs=[s for _, s in ins],
        out_specs=[s for _, s in outs],
        out_shape=out_shape,
        scratch_shapes=scratch,
        input_output_aliases=alias or {},
        compiler_params=pltpu.CompilerParams(
            dimension_semantics=("arbitrary",), vmem_limit_bytes=56 * 1024 * 1024
        ),
        cost_estimate=pl.CostEstimate(
            flops=int(us * slots * 1.1e9 * COST), bytes_accessed=int(us * slots * 1e6 * COST), transcendentals=0
        ),
    )(*arrays)


def sds(shape, dtype):
    return jax.ShapeDtypeStruct(shape, dtype)


def rows_times(left, right, product, block, held):
    rows, depth = left.shape
    width = right.shape[1] if product is nn else right.shape[0]
    (out,) = call(
        functools.partial(rows_kernel, product),
        rows // block,
        [(left, pl.BlockSpec((block, depth), lambda i: (i, 0))), (right, whole(*right.shape))],
        [(sds((rows, width), BF16), pl.BlockSpec((block, width), lambda i: (i, 0)))],
        [],
        2.0,
        held,
    )
    return out


def gathered_times(parts, right, product, held):
    rows, depth = parts[0].shape
    width = right.shape[1] if product is nn else right.shape[0]
    block = lambda w: (sds((4 * rows, w), BF16), pl.BlockSpec((rows, w), lambda i: (i, 0)))
    return call(
        functools.partial(gathered_kernel, product),
        4,
        [(v, whole(*v.shape)) for v in parts] + [(right, whole(*right.shape))],
        [block(width), block(depth)],
        [],
        2.7,
        held,
    )


def weight_sum(lefts, rights, held, us=2.0):
    rows, width = lefts[0].shape
    depth = rights[0].shape[1]
    block = min(256, width)
    (out,) = call(
        weight_kernel,
        width // block,
        [(v, pl.BlockSpec((rows, block), lambda i: (0, i))) for v in lefts] + [(v, whole(*v.shape)) for v in rights],
        [(sds((width, depth), BF16), pl.BlockSpec((block, depth), lambda i: (i, 0)))],
        [],
        us,
        held,
    )
    return out


def per_device(
    tokens, lengths, pre_gain, in_weight, conv_weight, conv_bias, step_bias, decay_log, skip_gain,
    norm_gain, out_weight, cotangent,
):
    micro, length, model = tokens.shape
    reps = lax.axis_size("rep")
    pieces = lax.axis_size("seq")
    rep = lax.axis_index("rep")
    inner = norm_gain.shape[0]
    heads = HEADS // reps
    width = heads * HEAD_DIM
    rows = reps * length
    xbc = width + 2 * STATE
    cols = xbc + LANES
    groups = pieces if HEADS % (pieces * reps) == 0 else 1
    strided = groups == pieces

    def pick(v, unit):
        each_group = heads // groups * unit
        v = v.reshape(v.shape[:-1] + (groups, reps, each_group))
        v = lax.dynamic_index_in_dim(v, rep, v.ndim - 2, False)
        return v.reshape(v.shape[:-2] + (groups * each_group,))

    def unpick(parts, unit):
        each_group = heads // groups * unit
        lead = parts[0].shape[:-1]
        v = jnp.stack([q.reshape(lead + (groups, each_group)) for q in parts], axis=-2)
        return v.reshape(lead + (HEADS * unit,))

    def lanes_of(v):
        return jnp.pad(v, [(0, 0)] * (v.ndim - 1) + [(0, LANES - v.shape[-1])])

    def conv_share(v):
        return jnp.concatenate([pick(v[..., :inner], HEAD_DIM), v[..., inner:]], axis=-1)

    position = lax.axis_index("seq") * length + jnp.arange(length, dtype=jnp.int32)
    valid = (position[None, :] < lengths[:, None])[..., None]
    token_rows = tokens.astype(F32)
    inverse = lax.rsqrt(jnp.mean(token_rows * token_rows, axis=-1, keepdims=True) + EPSILON)
    normed = (token_rows * inverse * pre_gain).astype(BF16)
    masked = jnp.where(valid, cotangent, jnp.zeros_like(cotangent))

    w_mix = jnp.concatenate(
        [
            pick(in_weight[:, inner : 2 * inner], HEAD_DIM),
            in_weight[:, 2 * inner : 2 * inner + 2 * STATE],
            lanes_of(pick(in_weight[:, 2 * inner + 2 * STATE :], 1)),
        ],
        axis=1,
    )
    w_gate = pick(in_weight[:, :inner], HEAD_DIM)
    w_mix = lax.all_gather(w_mix, "seq", axis=0, tiled=True)
    w_gate = lax.all_gather(w_gate, "seq", axis=0, tiled=True)
    if strided:
        share = out_weight.shape[0] // reps
        w_out = lax.dynamic_slice_in_dim(out_weight, rep * share, share, 0)
        w_out = lax.all_gather(w_out, "seq", axis=0, tiled=True)
    else:
        w_out = lax.all_gather(out_weight, "seq", axis=0, tiled=True)
        w_out = lax.dynamic_slice_in_dim(w_out, rep * width, width, 0)

    spread_row = jnp.arange(LANES, dtype=jnp.int32)[:, None]
    spread = (
        (spread_row < LANES // 2)
        & (spread_row % (LANES // 4) == jnp.arange(width, dtype=jnp.int32)[None, :] // HEAD_DIM)
    ).astype(BF16)
    fold = (
        jnp.arange(width, dtype=jnp.int32)[:, None] // HEAD_DIM
        == jnp.arange(LANES, dtype=jnp.int32)[None, :]
    ).astype(BF16)

    cw = conv_share(conv_weight)
    cb = conv_share(conv_bias)[None, :]
    sb = lanes_of(pick(step_bias, 1))[None, :]
    dl = lanes_of(pick(decay_log, 1))[None, :]
    skip = jnp.repeat(pick(skip_gain, 1), HEAD_DIM)[None, :]
    gain = pick(norm_gain, HEAD_DIM)[None, :]

    line = []

    def held(*others):
        return lambda value: after(value, *line, *others)

    def later(values):
        return list(after(tuple(values), *line))

    def ran(out):
        line[:] = [out]
        return out

    row_spec = lambda w: pl.BlockSpec((length, w), lambda i: (i, 0))
    small = [
        (cw, whole(KCONV, xbc)),
        (cb, whole(1, xbc)),
        (sb, whole(1, LANES)),
        (dl, whole(1, LANES)),
    ]
    spread_in = (spread, whole(LANES, width))
    gain_in = (gain, whole(1, width))
    skip_in = (skip, whole(1, width))
    wide = lambda v: (v, row_spec(width))
    state = lambda v: (v, each(STATE, width))
    out_wide = lambda t: (sds((rows, width), t), row_spec(width))
    out_state = (sds((reps, STATE, width), F32), each(STATE, width))
    out_message = (sds((reps, STATE + MARK, width), BF16), each(STATE + MARK, width))
    out_gain = (sds((PAD, width), F32), whole(PAD, width))
    ext = pltpu.VMEM((length + PAD, LANES), F32)

    proj_in, halo_in, x_in, bc_in, sl_in, part_in, fade_in, start_in = ([None] * micro for _ in range(8))
    gate_in, grad_in, y_in, sums, inside = ([None] * micro for _ in range(5))
    forward_chain = [None] * micro

    def project(m, *others):
        proj, normed_all[m] = gathered_times(normed_parts[m], w_mix, nn, held(*others))
        ran(proj)
        tail = proj.reshape(reps, length, cols)[:, length - (KCONV - 1) :, :xbc]
        halo = lax.ppermute(tail, "seq", [(i, i + 1) for i in range(pieces - 1)])
        halo = jnp.pad(halo.astype(F32), ((0, 0), (PAD - (KCONV - 1), 0), (0, 0)))
        proj_in[m], halo_in[m] = (proj, row_spec(cols)), (halo, each(PAD, xbc))

    def front(m, *others):
        x, bc, sl, part, message, fade = call(
            front_kernel,
            reps,
            [proj_in[m], halo_in[m]] + small + [spread_in],
            [
                out_wide(F32),
                (sds((rows, 4 * STATE), BF16), row_spec(4 * STATE)),
                (sds((rows, 2 * LANES), F32), row_spec(2 * LANES)),
                out_state,
                out_message,
                (sds((reps, 1, width), F32), each(1, width)),
            ],
            [ext],
            2.3,
            held(*others),
        )
        ran(fade)
        x_in[m], bc_in[m], sl_in[m] = wide(x), (bc, row_spec(4 * STATE)), (sl, row_spec(2 * LANES))
        part_in[m], fade_in[m] = state(part), (fade, each(1, width))
        forward_chain[m] = Chain(fade, part, message, False)

    def within(m, *others):
        (inside[m],) = call(
            inside_kernel, reps, [x_in[m], bc_in[m], sl_in[m], spread_in], [out_wide(F32)], [], 2.2, held(*others)
        )
        ran(inside[m])

    def gate_of(m, *others):
        gate_in[m] = wide(ran(rows_times(normed_all[m], w_gate, nn, length, held(*others))))

    def grad_of(m, *others):
        grad, cot_all[m] = gathered_times(later(cot_parts[m]), w_out, nt, held(*others))
        grad_in[m] = wide(ran(grad))

    def gating(m, *others):
        start_in[m] = state(forward_chain[m].end())
        y, partial = call(
            gate_kernel,
            reps,
            [wide(inside[m]), x_in[m], bc_in[m], sl_in[m], start_in[m], gate_in[m], grad_in[m], gain_in, skip_in, spread_in],
            [out_wide(F32), (sds((reps, PAD, length), F32), each(PAD, length))],
            [],
            2.8,
            held(*others),
        )
        ran(partial)
        y_in[m] = wide(y)
        partial = sum_aligned(partial[:, :2])
        sums[m] = (jnp.pad(partial, ((0, 0), (0, PAD - 2), (0, 0))), each(PAD, length))

    near = [gather_near(normed[0])]
    far = [to_far(near[0])]
    normed_all, cot_all = [None] * micro, [None] * micro
    normed_parts = [far_parts(near[0], far[0])]
    near.append(gather_near(after(normed[1], *normed_parts[0][3:])))
    project(0, near[1][0])
    near[1] = later(near[1])
    far.append(to_far(near[1]))
    normed_parts.append(far_parts(near[1], far[1]))
    front(0, *far[1])
    cot_near = [gather_near(after(masked[0], *line))]
    project(1, cot_near[0][0])
    front(1, forward_chain[0].hop())
    gate_of(0)
    cot_near[0] = later(cot_near[0])
    cot_far = [to_far(cot_near[0])]
    cot_near.append(gather_near(after(masked[1], *line, *cot_far[0])))
    cot_parts = [far_parts(cot_near[0], cot_far[0])]
    within(0, forward_chain[0].hop(), forward_chain[1].hop(), cot_near[1][0])
    gate_of(1)
    within(1, forward_chain[0].hop(), forward_chain[1].hop())
    cot_near[1] = later(cot_near[1])
    cot_far.append(to_far(cot_near[1]))
    cot_parts.append(far_parts(cot_near[1], cot_far[1]))
    grad_of(0, *cot_far[1])
    forward_chain[0].rest()
    grad_of(1, forward_chain[0].back(), forward_chain[1].hop())
    forward_chain[1].rest()
    gating(0, forward_chain[1].back())
    gating(1)

    gated, dy_in, dgate, later_in, gains, skips = ([None] * micro for _ in range(6))
    backward_chain = [None] * micro

    def normalise(m, *others):
        gated[m], dy, dgate[m], dstart, message, gains[m], skips[m] = call(
            functools.partial(norm_kernel, float(inner)),
            reps,
            [y_in[m], x_in[m], bc_in[m], sl_in[m], gate_in[m], grad_in[m], gain_in, skip_in, fade_in[m], sums[m], spread_in],
            [out_wide(BF16), out_wide(BF16), out_wide(BF16), out_state, out_message, out_gain, out_gain],
            [],
            3.1,
            held(*others),
        )
        ran(gains[m])
        dy_in[m] = wide(dy)
        backward_chain[m] = Chain(fade_in[m][0], dstart, message, True)

    inner_back = [None] * micro

    def within_back(m, *others):
        inner_back[m] = call(
            inside_back_kernel,
            reps,
            [x_in[m], bc_in[m], sl_in[m], dy_in[m], start_in[m], spread_in],
            [out_wide(F32), (sds((rows, 2 * STATE), F32), row_spec(2 * STATE))],
            [],
            3.6 * LOW,
            held(*others),
        )
        ran(inner_back[m][1])

    pgs, smalls = [None] * micro, [None] * micro

    def back(m, *others):
        dxs, dbc = inner_back[m]
        later_in[m] = state(backward_chain[m].end())
        pg, halo_grad, tail_grad, *smalls[m] = call(
            back_kernel,
            reps,
            [proj_in[m], halo_in[m]] + small
            + [skip_in, spread_in, (fold, whole(width, LANES)), x_in[m], bc_in[m], sl_in[m], y_in[m], dy_in[m]]
            + [wide(dxs), (dbc, row_spec(2 * STATE)), start_in[m], part_in[m], fade_in[m], later_in[m]],
            [
                (sds((rows, cols), BF16), row_spec(cols)),
                (sds((reps, PAD, xbc), F32), each(PAD, xbc)),
                (sds((reps, PAD, xbc), F32), each(PAD, xbc)),
                (sds((PAD, xbc), F32), whole(PAD, xbc)),
                (sds((PAD, xbc), F32), whole(PAD, xbc)),
                (sds((PAD, LANES), F32), whole(PAD, LANES)),
                (sds((PAD, LANES), F32), whole(PAD, LANES)),
            ],
            [ext, pltpu.VMEM((length + 2 * PAD, LANES), F32)],
            5.1 * LOW,
            held(*others),
        )
        ran(smalls[m][0])
        from_next = lax.ppermute(
            halo_grad[:, PAD - (KCONV - 1) :].astype(BF16), "seq", [(i, i - 1) for i in range(1, pieces)]
        )
        pgs[m] = pg, tail_grad[:, PAD - (KCONV - 1) :], from_next

    def complete(m):
        pg, last_rows, from_next = pgs[m]
        last_rows = last_rows + later([from_next])[0].astype(F32)
        pgs[m] = lax.dynamic_update_slice(
            pg.reshape(reps, length, cols), last_rows.astype(BF16), (0, length - (KCONV - 1), 0)
        ).reshape(rows, cols)

    normed_grad, pre_parts = [None] * micro, [None] * micro

    def grad_through(m, *others):
        *blocks, pre = call(
            grad_kernel,
            reps,
            [(pgs[m], row_spec(cols)), wide(dgate[m]), (w_mix, whole(*w_mix.shape)), (w_gate, whole(*w_gate.shape))]
            + [(normed_all[m], row_spec(model))],
            [(sds((length, model), BF16), whole(length, model))] * reps + [(sds((PAD, model), F32), whole(PAD, model))],
            [],
            30.0 if m == micro - 1 else 10.0,
            held(*others),
        )
        pre_parts[m] = ran(pre)[0]
        normed_grad[m] = blocks[:1] + [swap(blocks[q], "rep", q) for q in (1, 2, 3)]

    def over_seq(parts):
        return lax.psum_scatter(parts, "seq", scatter_dimension=0, tiled=True)

    def project_out(m, *others):
        blocks = call(
            branch_kernel,
            reps,
            [wide(gated[m]), (w_out, whole(*w_out.shape))],
            [(sds((length, model), BF16), whole(length, model))] * reps,
            [],
            1.9,
            held(*others),
        )
        ran(blocks[0])
        return list(blocks[:1]) + [swap(blocks[q], "rep", q) for q in (1, 2, 3)]

    normalise(0)
    branch = [project_out(0)]
    normalise(1, backward_chain[0].hop())
    branch.append(project_out(1))
    within_back(0, backward_chain[0].hop(), backward_chain[1].hop())
    within_back(1, backward_chain[0].hop(), backward_chain[1].hop())
    backward_chain[0].rest()
    back(0, backward_chain[0].back(), backward_chain[1].hop())
    backward_chain[1].rest()
    if strided:
        k_rows, out_share = model // pieces, width // pieces
        both_rows = k_rows + out_share * model // width
        columns = lambda w: pl.BlockSpec((rows, w), lambda i: (0, i))
        (both_part,) = call(
            functools.partial(both_weights_kernel, micro),
            pieces,
            [(v, columns(k_rows)) for v in normed_all]
            + [(v, whole(*v.shape)) for v in dgate]
            + [(v, columns(out_share)) for v in gated]
            + [(v, whole(*v.shape)) for v in cot_all],
            [(sds((pieces, both_rows, width), BF16), each(both_rows, width))],
            [],
            3.2,
            held(backward_chain[1].back()),
        )
        ran(both_part)
        gate_sums = out_sums = over_seq(both_part)[0]
    else:
        gate_sums = over_seq(ran(weight_sum(normed_all, dgate, held(backward_chain[1].back()))))
        out_part = ran(weight_sum(gated, cot_all, held()))
        out_sums = over_seq(
            lax.dynamic_update_slice(jnp.zeros((inner, model), BF16), out_part, (rep * width, 0))
        )
    complete(0)
    back(1)
    grad_through(0, *branch[0])
    complete(1)
    gain_part, skip_part = sum(g[0] for g in gains), sum(v[0] for v in skips)
    cw_part, cb_part, sb_part, dl_part = (sum(v) for v in zip(*smalls))
    skip_heads = skip_part.reshape(heads, HEAD_DIM).sum(axis=1)
    packed = jnp.concatenate(
        [cw_part[:KCONV].reshape(-1), cb_part[0], gain_part, lanes_of(skip_heads), sb_part[0], dl_part[0]]
    )
    branch = [later(b) for b in branch]
    output = jnp.stack([sum(v.astype(F32) for v in b) for b in branch])
    output = jnp.where(valid, token_rows + output, 0.0).astype(BF16)
    mix_part = ran(weight_sum(normed_all, pgs, held(output), 5.0))
    mix_sums = over_seq(after(mix_part, gate_sums, out_sums))
    gate_rows = gather_direct(gate_sums)
    out_rows = gate_rows if strided else gather_direct(out_sums)
    grad_through(1, *normed_grad[0])
    pre_part = sum(pre_parts)
    small_sums = SmallSums(jnp.concatenate([packed, pre_part]).reshape(-1, LANES)).rest()
    normed_grad = [list(after(tuple(v), mix_sums)) for v in normed_grad]

    normed_grad = jnp.stack([sum(v.astype(F32) for v in n) for n in normed_grad])
    xhat = token_rows * inverse
    scaled = normed_grad * pre_gain
    rows_grad = inverse * (scaled - xhat * jnp.mean(scaled * xhat, axis=-1, keepdims=True))
    tokens_grad = jnp.where(valid, cotangent.astype(F32), 0.0) + rows_grad

    rep_scalar = rep.astype(jnp.int32).reshape(1)
    place_in = (rep_scalar, pl.BlockSpec(memory_space=pltpu.SMEM))
    local = jnp.arange(LANES, dtype=jnp.int32)
    a_group = heads // groups
    head_of = (local[None, :] // a_group * reps + jnp.arange(reps, dtype=jnp.int32)[:, None]) * a_group + local % a_group
    head_of = jnp.where(local < heads, head_of, -1)
    where_heads = (head_of[:, :, None] == local[None, None, :]).astype(BF16)
    unit = width // groups
    k_rows = in_weight.shape[0]
    lanes_spec = lambda index: pl.BlockSpec((k_rows, unit), lambda i: (0, index(i)))
    column = lambda first: (
        sds(in_weight.shape[::-1], F32),
        pl.BlockSpec((reps * unit, k_rows), lambda i: (i + first, 0)),
    )
    finished = []
    if strided:
        (out_weight_grad,) = call(
            functools.partial(out_grad_kernel, k_rows),
            reps,
            [place_in] + [(b, whole(*b.shape)) for b in out_rows],
            [(sds(out_weight.shape, F32), pl.BlockSpec((out_share, model), lambda i: (i, 0)))],
            [],
            0.9,
        )
        (gate_done,) = call(
            gate_grad_kernel,
            groups,
            [place_in] + [(b, lanes_spec(lambda i: i)) for b in gate_rows],
            [column(0)],
            [],
            0.8,
        )
        finished = [out_weight_grad, gate_done]
    mix_rows = gather_direct(after(mix_sums, *finished))
    packed = gather_direct(after(small_sums, mix_sums))
    if strided:
        (in_weight_grad,) = call(
            functools.partial(mix_grad_kernel, groups, heads),
            groups + 1,
            [(gate_done, pl.BlockSpec(memory_space=pl.ANY)), place_in]
            + [(b, lanes_spec(lambda i: jnp.minimum(i, groups - 1))) for b in mix_rows]
            + [(b[:, width:], whole(k_rows, cols - width)) for b in mix_rows]
            + [(where_heads, whole(reps, LANES, LANES))],
            [column(groups)],
            [],
            0.5,
            alias={0: 0},
        )
        in_weight_grad = in_weight_grad.T
    else:
        out_weight_grad = sum(v.astype(F32) for v in in_order(out_rows))
        gates, mixes = in_order(gate_rows), in_order(mix_rows)
        in_weight_grad = jnp.concatenate(
            [
                unpick(gates, HEAD_DIM).astype(F32),
                unpick([v[:, :width] for v in mixes], HEAD_DIM).astype(F32),
                sum(v[:, width:xbc].astype(F32) for v in mixes),
                unpick([v[:, xbc : xbc + heads] for v in mixes], 1).astype(F32),
            ],
            axis=1,
        )
    flat = [v.reshape(-1) for v in in_order(packed)]
    def conv_join(values):
        return jnp.concatenate(
            [unpick([v[..., :width] for v in values], HEAD_DIM), sum(v[..., width:] for v in values)], axis=-1
        )

    conv_weight_grad = conv_join([v[: KCONV * xbc].reshape(KCONV, xbc) for v in flat])
    at = KCONV * xbc
    conv_bias_grad = conv_join([v[at : at + xbc] for v in flat])
    at += xbc
    norm_gain_grad = unpick([v[at : at + width] for v in flat], HEAD_DIM)
    at += width
    by_head = [lax.optimization_barrier(v[at : at + 3 * LANES]).reshape(3, LANES)[:, :heads] for v in flat]
    skip_gain_grad, step_bias_grad, decay_log_grad = unpick(by_head, 1)

    at += 3 * LANES
    pre_gain_grad = sum(v[at : at + model] for v in flat) / pre_gain

    return (
        output, tokens_grad, pre_gain_grad, in_weight_grad, conv_weight_grad, conv_bias_grad,
        step_bias_grad, decay_log_grad, skip_gain_grad, norm_gain_grad, out_weight_grad,
    )


def solution(mesh):
    rows = P("rep", "seq", None)
    shard = P("seq", None)
    in_specs = (rows, P("rep"), P(), shard, P(), P(), P(), P(), P(), P(), shard, rows)
    out_specs = (rows, rows, P(), shard, P(), P(), P(), P(), P(), P(), shard)
    return jax.shard_map(per_device, mesh=mesh, in_specs=in_specs, out_specs=out_specs, check_vma=False)
```

time: 2670 us -> 772 us (0.29)
  waiting for transfers between devices: 1820 us -> 175 us
  matrix products: 352 us -> 0 us
  Pallas kernels: 0 us -> 339 us
  other arithmetic: 278 us -> 76.5 us
  starting transfers between devices: 5.01 us -> 97.3 us
  local copies, waits for them, and re-layouts: 149 us -> 57.8 us
  blocking collectives: 48.5 us -> 0 us
    all_gather x4 -> x3, waiting for transfers between devices: 828 us -> 13 us  [the longest x1 13 us: per_device(): w_mix = lax.all_gather(w_mix, 'seq', axis=0, tiled=True)]
    reduce_scatter x2, waiting for transfers between devices: 703 us -> 0.01 us  [over_seq(): return lax.psum_scatter(parts, 'seq', scatter_dimension=0, tiled=True)]
    dot_general x20 -> x0, matrix products: 352 us -> none  [the longest x3 134 us: out_terms(): jnp.einsum('mhts,mshp->mthp', weights, head_inputs, precision=HIGHEST_PRE...]
    pallas_call x0 -> x27, Pallas kernels: none -> 339 us  [call(): pl.pallas_call(kernel, grid=(slots,), in_specs=[s for _, s in ins], out_s...]
    psum x2 -> x0, waiting for transfers between devices: 285 us -> none  [the longest x1 252 us: per_device(): in_weight_grad, out_weight_grad = lax.psum((in_shard, out_shard), 'rep')]
    ppermute x2 -> x70, waiting for transfers between devices: 0.01 us -> 161 us  [the longest x46 161 us: swap(): lax.ppermute(value, axis, [(i, i ^ bit) for i in range(lax.axis_size(axis...]
    ppermute x2 -> x70, starting transfers between devices: 4.3 us -> 97.1 us  [the longest x46 50.7 us: swap(): lax.ppermute(value, axis, [(i, i ^ bit) for i in range(lax.axis_size(axis...]
    reduce_sum x8 -> x3, other arithmetic: 89.3 us -> 3.17 us  [the longest x1 2.22 us: per_device(): jnp.mean(token_rows * token_rows, axis=-1, keepdims=True) + EPSILON]
  transfers between devices with their start and end apart: 10 -> 75, of which waited for: 8 -> 19; matrix products, arithmetic and copies ran while one was open for 21% -> 15% of each run, Pallas kernels for 0% -> 39%
where the time goes in v1:
time: 772 us; the launch traced here: 761 us
  Pallas kernels  339 us (44%)
  waiting for transfers between devices  175 us (23%)
  starting transfers between devices  97.3 us (13%)
  other arithmetic  76.5 us (10%)
  local copies, waits for them, and re-layouts  57.8 us (7%)
  between operations  15.8 us (2%)
    pallas_call x27, Pallas kernels, call(): pl.pallas_call(kernel, grid=(slots,), in_specs=[s for _, s in ins], out_s...  339 us
    ppermute x46, waiting for transfers between devices, swap(): lax.ppermute(value, axis, [(i, i ^ bit) for i in range(lax.axis_size(axis...  161 us
    ppermute x46, starting transfers between devices, swap(): lax.ppermute(value, axis, [(i, i ^ bit) for i in range(lax.axis_size(axis...  50.7 us
    convert_element_type x8, other arithmetic, hop(): onto = (self.total + self.total_fade * self.enters.astype(F32)).astype(BF16)  22 us
    ppermute x12, starting transfers between devices, hop(): self.enters = self.enters + lax.ppermute(onto, 'seq', [self.onward.pop(0)])  15.9 us
  transfers between devices with their start and end apart: 75, of which 19 were waited for; matrix products, arithmetic and copies ran while one was open for 15% of the time, Pallas kernels for 39%

profile of v1, /device:TPU:0, one launch (start us, length us, event | category | flops | bytes accessed | tf_op | source)
XLA Modules:
  0.0 760.6 jit_solution(17183427638637535403)
XLA Ops:
  31.7 16.4 %collective-permute-done.one = bf16[256,2048]{1,0:T(8,128)(2,1)} collective-permute-done((bf16[256,2048]{1,0:T(8,128)(2,1)}, bf16[256,2048]{1,0:T(8,128)(2,1)}, u32[]{:S(2)}, u32[]{:S(2)}) %collective-permute-start) | collective-permute-done | bytes 1048608 | tf_op jit(solution)/shard_map/ppermute | solution.py:26
  66.7 13.0 %all-gather.4.cloned.1.call-done.right.w_mix = bf16[2048,1408]{1,0:T(8,128)(2,1)} async-done(((bf16[256,1408]{1,0:T(8,128)(2,1)}), bf16[2048,1408]{1,0:T(8,128)(2,1)}) %all-gather.4.cloned.1.call-update) | async-done | bytes 5767184 | tf_op jit(solution)/shard_map/all_gather | solution.py:709
  79.8 12.4 %shard_map.203 = (bf16[1024,1408]{1,0:T(8,128)(2,1)}, bf16[1024,2048]{1,0:T(8,128)(2,1)}) custom-call(bf16[256,2048]{1,0:T(8,128)(2,1)} %get-tuple-element.153.own, bf16[256,2048]{1,0:T(8,128)(2,1)} %collective-permute-done.one, bf16[256,2048]{1,0:T(8,128)(2,1)} %collective-permute-done.2.two, bf16[128,2048]{1,0:T(8,128)(2,1)} %copy-done.60, ...), custom_call_target="tpu_custom_call" | custom-call | flops 11879999488 | bytes 10800000 | tf_op jit(solution)/shard_map/pallas_call | solution.py:591
  112.5 12.5 %shard_map.205 = (bf16[1024,1408]{1,0:T(8,128)(2,1)}, bf16[1024,2048]{1,0:T(8,128)(2,1)}) custom-call(bf16[256,2048]{1,0:T(8,128)(2,1)} %copy-done.25, bf16[256,2048]{1,0:T(8,128)(2,1)} %copy-done.32, bf16[256,2048]{1,0:T(8,128)(2,1)} %copy-done.33, bf16[128,2048]{1,0:T(8,128)(2,1)} %copy-done.61, bf16[128,2048]{1,0:T(8,128)(2,1)} %copy-done.63, ...), custom_call_target="tpu_custom_call" | custom-call | flops 11879999488 | bytes 10800000 | tf_op jit(solution)/shard_map/pallas_call | solution.py:591
  174.9 11.5 %shard_map.208.y = f32[1024,1024]{1,0:T(8,128)} custom-call(f32[1024,1024]{1,0:T(8,128)} %get-tuple-element.225.x, bf16[1024,512]{1,0:T(8,128)(2,1)} %get-tuple-element.176.bc, f32[1024,256]{1,0:T(8,128)} %get-tuple-element.177.sl, bf16[128,1024]{1,0:T(8,128)(2,1)} %and_convert_fusion.spread), custom_call_target="tpu_custom_call" | custom-call | flops 9680000000 | bytes 8800000 | tf_op jit(solution)/shard_map/pallas_call | solution.py:591
  205.2 11.5 %shard_map.210.y = f32[1024,1024]{1,0:T(8,128)} custom-call(f32[1024,1024]{1,0:T(8,128)} %get-tuple-element.228.x, bf16[1024,512]{1,0:T(8,128)(2,1)} %get-tuple-element.182.bc, f32[1024,256]{1,0:T(8,128)} %get-tuple-element.183.sl, bf16[128,1024]{1,0:T(8,128)(2,1)} %and_convert_fusion.spread), custom_call_target="tpu_custom_call" | custom-call | flops 9680000000 | bytes 8800000 | tf_op jit(solution)/shard_map/pallas_call | solution.py:591
  289.0 12.2 %shard_map.215 = (bf16[1024,1024]{1,0:T(8,128)(2,1)}, bf16[1024,1024]{1,0:T(8,128)(2,1)}, bf16[1024,1024]{1,0:T(8,128)(2,1)}, f32[4,128,1024]{2,1,0:T(8,128)}, b...) custom-call(f32[1024,1024]{1,0:T(8,128)} %get-tuple-element.207.y, ...), custom_call_target="tpu_custom_call" | custom-call | flops 13639999488 | bytes 12400000 | tf_op jit(solution)/shard_map/pallas_call | solution.py:591
  302.9 10.1 %shard_map.216 = (bf16[256,2048]{1,0:T(8,128)(2,1)}, bf16[256,2048]{1,0:T(8,128)(2,1)}, bf16[256,2048]{1,0:T(8,128)(2,1)}, bf16[256,2048]{1,0:T(8,128)(2,1)}) custom-call(bf16[1024,1024]{1,0:T(8,128)(2,1)} %get-tuple-element.210.left.refs_4_, bf16[1024,2048]{1,0:T(8,128)(2,1)} %all-gather.8.cloned.1.call-done.right), custom_call_target="tpu_custom_call" | custom-call | flops 8360000000 | bytes 7600000 | tf_op jit(solution)/shard_map/pallas_call | solution.py:591
  315.5 12.2 %shard_map.217 = (bf16[1024,1024]{1,0:T(8,128)(2,1)}, bf16[1024,1024]{1,0:T(8,128)(2,1)}, bf16[1024,1024]{1,0:T(8,128)(2,1)}, f32[4,128,1024]{2,1,0:T(8,128)}, b...) custom-call(f32[1024,1024]{1,0:T(8,128)} %get-tuple-element.218.y, ...), custom_call_target="tpu_custom_call" | custom-call | flops 13639999488 | bytes 12400000 | tf_op jit(solution)/shard_map/pallas_call | solution.py:591
  332.5 10.0 %shard_map.218 = (bf16[256,2048]{1,0:T(8,128)(2,1)}, bf16[256,2048]{1,0:T(8,128)(2,1)}, bf16[256,2048]{1,0:T(8,128)(2,1)}, bf16[256,2048]{1,0:T(8,128)(2,1)}) custom-call(bf16[1024,1024]{1,0:T(8,128)(2,1)} %get-tuple-element.221.left.refs_5_, bf16[1024,2048]{1,0:T(8,128)(2,1)} %all-gather.8.cloned.1.call-done.right), custom_call_target="tpu_custom_call" | custom-call | flops 8360000000 | bytes 7600000 | tf_op jit(solution)/shard_map/pallas_call | solution.py:591
  350.4 14.1 %shard_map.219 = (f32[1024,1024]{1,0:T(8,128)}, f32[1024,256]{1,0:T(8,128)}) custom-call(f32[1024,1024]{1,0:T(8,128)} %get-tuple-element.225.x, bf16[1024,512]{1,0:T(8,128)(2,1)} %get-tuple-element.176.bc, f32[1024,256]{1,0:T(8,128)} %get-tuple-element.177.sl, bf16[1024,1024]{1,0:T(8,128)(2,1)} %get-tuple-element.226.dy, ...), custom_call_target="tpu_custom_call" | custom-call | flops 15840000000 | bytes 14400000 | tf_op jit(solution)/shard_map/pallas_call | solution.py:591
  379.4 14.1 %shard_map.220 = (f32[1024,1024]{1,0:T(8,128)}, f32[1024,256]{1,0:T(8,128)}) custom-call(f32[1024,1024]{1,0:T(8,128)} %get-tuple-element.228.x, bf16[1024,512]{1,0:T(8,128)(2,1)} %get-tuple-element.182.bc, f32[1024,256]{1,0:T(8,128)} %get-tuple-element.183.sl, bf16[1024,1024]{1,0:T(8,128)(2,1)} %get-tuple-element.229.dy, ...), custom_call_target="tpu_custom_call" | custom-call | flops 15840000000 | bytes 14400000 | tf_op jit(solution)/shard_map/pallas_call | solution.py:591
  399.0 20.5 %shard_map.221 = (bf16[1024,1408]{1,0:T(8,128)(2,1)}, f32[4,8,1280]{2,1,0:T(8,128)}, f32[4,8,1280]{2,1,0:T(8,128)}, f32[8,1280]{1,0:T(8,128)}, f32[8,1280]{1,0:T...) custom-call(bf16[1024,1408]{1,0:T(8,128)(2,1)} %get-tuple-element.231.proj, f32[4,8,1280]{2,1,0:T(8,128)} %pad_convert_fusion.1.halo, ...), custom_call_target="tpu_custom_call" | custom-call | flops 22439999488 | bytes 20400000 | tf_op jit(solution)/shard_map/pallas_call | solution.py:591
  419.9 25.5 %shard_map.222 = bf16[8,512,1024]{2,1,0:T(8,128)(2,1)} custom-call(bf16[1024,2048]{1,0:T(8,128)(2,1)} %get-tuple-element.263.left.refs_0_.normed, bf16[1024,2048]{1,0:T(8,128)(2,1)} %get-tuple-element.180.left.refs_1_.normed, bf16[1024,1024]{1,0:T(8,128)(2,1)} %get-tuple-element.238.refs_2_.gate, bf16[1024,1024]{1,0:T(8,128)(2,1)} %get-tuple-element.239.refs_3_.gate, ...), custom_call_target="tpu_custom_call" | custom-call | flops 28160000000 | bytes 25600000 | tf_op jit(solution)/shard_map/pallas_call | solution.py:591
  461.0 20.6 %shard_map.223 = (bf16[1024,1408]{1,0:T(8,128)(2,1)}, f32[4,8,1280]{2,1,0:T(8,128)}, f32[4,8,1280]{2,1,0:T(8,128)}, f32[8,1280]{1,0:T(8,128)}, f32[8,1280]{1,0:T...) custom-call(bf16[1024,1408]{1,0:T(8,128)(2,1)} %get-tuple-element.243.proj, f32[4,8,1280]{2,1,0:T(8,128)} %pad_convert_fusion.halo, ...), custom_call_target="tpu_custom_call" | custom-call | flops 22439999488 | bytes 20400000 | tf_op jit(solution)/shard_map/pallas_call | solution.py:591
  483.9 12.2 %collective-permute-done.32 = bf16[256,2048]{1,0:T(8,128)(2,1)} collective-permute-done((bf16[256,2048]{1,0:T(8,128)(2,1)}, bf16[256,2048]{1,0:T(8,128)(2,1)}, u32[]{:S(2)}, u32[]{:S(2)}) %collective-permute-start.32) | collective-permute-done | bytes 1048608 | tf_op jit(solution)/shard_map/ppermute | solution.py:26
  496.2 19.2 %shard_map.224 = (bf16[256,2048]{1,0:T(8,128)(2,1)}, bf16[256,2048]{1,0:T(8,128)(2,1)}, bf16[256,2048]{1,0:T(8,128)(2,1)}, bf16[256,2048]{1,0:T(8,128)(2,1)}, f32[8,2048]{1,0:T(8,128)}) custom-call(bf16[1024,1408]{1,0:T(8,128)(2,1)} %bitcast.224, bf16[1024,1024]{1,0:T(8,128)(2,1)} %get-tuple-element.238.refs_2_.gate, ...), custom_call_target="tpu_custom_call" | custom-call | flops 44000002048 | bytes 40000000 | tf_op jit(solution)/shard_map/pallas_call | solution.py:591
  518.4 20.4 %collective-permute-done.50 = bf16[256,2048]{1,0:T(8,128)(2,1)S(1)} collective-permute-done((bf16[256,2048]{1,0:T(8,128)(2,1)S(1)}, bf16[256,2048]{1,0:T(8,128)(2,1)S(1)}, u32[]{:S(2)}, u32[]{:S(2)}) %collective-permute-start.50) | collective-permute-done | bytes 1048608 | tf_op jit(solution)/shard_map/ppermute | solution.py:26
  561.9 18.7 %shard_map.225 = bf16[2048,1408]{1,0:T(8,128)(2,1)} custom-call(bf16[1024,2048]{1,0:T(8,128)(2,1)} %get-tuple-element.263.left.refs_0_.normed, bf16[1024,2048]{1,0:T(8,128)(2,1)} %get-tuple-element.180.left.refs_1_.normed, bf16[1024,1408]{1,0:T(8,128)(2,1)} %bitcast.225, bf16[1024,1408]{1,0:T(8,128)(2,1)} %bitcast.221), custom_call_target="tpu_custom_call" | custom-call | flops 44000002048 | bytes 40000000 | tf_op jit(solution)/shard_map/pallas_call | solution.py:591
  580.6 11.0 %collective-permute-done.52 = bf16[256,2048]{1,0:T(8,128)(2,1)} collective-permute-done((bf16[256,2048]{1,0:T(8,128)(2,1)}, bf16[256,2048]{1,0:T(8,128)(2,1)}, u32[]{:S(2)}, u32[]{:S(2)}) %collective-permute-start.52) | collective-permute-done | bytes 1048608 | tf_op jit(solution)/shard_map/ppermute | solution.py:26
  591.7 19.6 %shard_map.226 = (bf16[256,2048]{1,0:T(8,128)(2,1)}, bf16[256,2048]{1,0:T(8,128)(2,1)}, bf16[256,2048]{1,0:T(8,128)(2,1)}, bf16[256,2048]{1,0:T(8,128)(2,1)}, f32[8,2048]{1,0:T(8,128)}) custom-call(bf16[1024,1408]{1,0:T(8,128)(2,1)} %bitcast.222, bf16[1024,1024]{1,0:T(8,128)(2,1)} %get-tuple-element.239.refs_3_.gate, ...), custom_call_target="tpu_custom_call" | custom-call | flops 131999997952 | bytes 120000000 | tf_op jit(solution)/shard_map/pallas_call | solution.py:591
  640.6 21.5 %collective-permute-done.65.g2.b2 = bf16[512,1024]{1,0:T(8,128)(2,1)} collective-permute-done((bf16[512,1024]{1,0:T(8,128)(2,1)S(1)}, bf16[512,1024]{1,0:T(8,128)(2,1)}, u32[]{:S(2)}, u32[]{:S(2)}) %collective-permute-start.65) | collective-permute-done | bytes 1048608 | tf_op jit(solution)/shard_map/ppermute | solution.py:26
  683.3 24.6 %collective-permute-done.56 = bf16[256,2048]{1,0:T(8,128)(2,1)} collective-permute-done((bf16[256,2048]{1,0:T(8,128)(2,1)}, bf16[256,2048]{1,0:T(8,128)(2,1)}, u32[]{:S(2)}, u32[]{:S(2)}) %collective-permute-start.56) | collective-permute-done | bytes 1048608 | tf_op jit(solution)/shard_map/ppermute | solution.py:26
  728.7 14.1 %collective-permute-done.68.refs_2_ = bf16[256,1408]{1,0:T(8,128)(2,1)} collective-permute-done((bf16[256,1408]{1,0:T(8,128)(2,1)}, bf16[256,1408]{1,0:T(8,128)(2,1)}, u32[]{:S(2)}, u32[]{:S(2)}) %collective-permute-start.68) | collective-permute-done | bytes 720928 | tf_op jit(solution)/shard_map/ppermute | solution.py:26
  (485 shorter events, 366.9 us)
Async XLA Ops:
  7.2 72.6 %all-gather.4.cloned.1.call-start = ((), (), s32[]{:S(2)}) async-start(), calls=%async_computation.2 | async-start | bytes 6488064 | tf_op jit(solution)/shard_map/all_gather | solution.py:709
  16.5 134.8 %all-gather.6.cloned.1.call-start = ((), (), s32[]{:S(2)}) async-start(), calls=%async_computation.3 | async-start | bytes 4718592 | tf_op jit(solution)/shard_map/all_gather | solution.py:710
  17.6 206.4 %all-gather.8.cloned.1.call-start = ((), (), s32[]{:S(2)}) async-start(), calls=%async_computation.4 | async-start | bytes 4718592 | tf_op jit(solution)/shard_map/all_gather | solution.py:714
  27.1 564.5 %reduce-scatter.3.cloned.1.call-start = ((), (), s32[]{:S(2)}) async-start(), calls=%async_computation.5 | async-start | bytes 9437184 | tf_op jit(solution)/shard_map/reduce_scatter | solution.py:945
  163.1 53.6 %collective-permute-start.21 = (bf16[128,2048]{1,0:T(8,128)(2,1)}, bf16[128,2048]{1,0:T(8,128)(2,1)}, u32[]{:S(2)}, u32[]{:S(2)}) collective-permute-start(bf16[128,2048]{1,0:T(8,128)(2,1)} %slice.413), channel_id=1, source_target_pairs={{0,16},{8,24},{16,0},{24,8},{1,17},{9,25},{17,1},{25,9},{2,18},{10... | collective-permute-start | bytes 1572872 | tf_op jit(solution)/shard_map/ppermute | solution.py:26
  163.9 54.6 %collective-permute-start.22 = (bf16[128,2048]{1,0:T(8,128)(2,1)S(1)}, bf16[128,2048]{1,0:T(8,128)(2,1)}, u32[]{:S(2)}, u32[]{:S(2)}) collective-permute-start(bf16[128,2048]{1,0:T(8,128)(2,1)S(1)} %slice.414), channel_id=1, source_target_pairs={{0,8},{8,0},{16,24},{24,16},{1,9},{9,1},{17,25},{25,17},{2,10},{10... | collective-permute-start | bytes 1572872 | tf_op jit(solution)/shard_map/ppermute | solution.py:26
  164.8 53.8 %collective-permute-start.15 = (bf16[256,2048]{1,0:T(8,128)(2,1)}, bf16[256,2048]{1,0:T(8,128)(2,1)}, u32[]{:S(2)}, u32[]{:S(2)}) collective-permute-start(bf16[256,2048]{1,0:T(8,128)(2,1)} %get-tuple-element.196.own), channel_id=1, source_target_pairs={{0,8},{8,0},{16,24},{24,16},{1,9},{9,1},{17,25},{25,17},{2,10},{10... | collective-permute-start | bytes 3145736 | tf_op jit(solution)/shard_map/ppermute | solution.py:26
  445.5 228.0 %reduce-scatter.5.cloned.1.call-start = ((), (), s32[]{:S(2)}) async-start(), calls=%async_computation.6 | async-start | bytes 6488064 | tf_op jit(solution)/shard_map/reduce_scatter | solution.py:945
  447.3 48.9 %collective-permute-start.32 = (bf16[256,2048]{1,0:T(8,128)(2,1)}, bf16[256,2048]{1,0:T(8,128)(2,1)}, u32[]{:S(2)}, u32[]{:S(2)}) collective-permute-start(bf16[256,2048]{1,0:T(8,128)(2,1)} %get-tuple-element.213), channel_id=1, source_target_pairs={{0,16},{8,24},{16,0},{24,8},{1,17},{9,25},{17,1},{25,9},{2,18},{10... | collective-permute-start | bytes 3145736 | tf_op jit(solution)/shard_map/ppermute | solution.py:26
  448.2 47.9 %collective-permute-start.33 = (bf16[256,2048]{1,0:T(8,128)(2,1)}, bf16[256,2048]{1,0:T(8,128)(2,1)}, u32[]{:S(2)}, u32[]{:S(2)}) collective-permute-start(bf16[256,2048]{1,0:T(8,128)(2,1)} %get-tuple-element.214), channel_id=1, source_target_pairs={{0,24},{8,16},{16,8},{24,0},{1,25},{9,17},{17,9},{25,1},{2,26},{10... | collective-permute-start | bytes 3145736 | tf_op jit(solution)/shard_map/ppermute | solution.py:26
  456.1 62.3 %collective-permute-start.48 = (bf16[256,2048]{1,0:T(8,128)(2,1)}, bf16[256,2048]{1,0:T(8,128)(2,1)}, u32[]{:S(2)}, u32[]{:S(2)}) collective-permute-start(bf16[256,2048]{1,0:T(8,128)(2,1)} %get-tuple-element.252), channel_id=1, source_target_pairs={{0,8},{8,0},{16,24},{24,16},{1,9},{9,1},{17,25},{25,17},{2,10},{10... | collective-permute-start | bytes 3145736 | tf_op jit(solution)/shard_map/ppermute | solution.py:26
  458.4 60.0 %collective-permute-start.49 = (bf16[256,2048]{1,0:T(8,128)(2,1)}, bf16[256,2048]{1,0:T(8,128)(2,1)S(1)}, u32[]{:S(2)}, u32[]{:S(2)}) collective-permute-start(bf16[256,2048]{1,0:T(8,128)(2,1)} %get-tuple-element.253), channel_id=1, source_target_pairs={{0,16},{8,24},{16,0},{24,8},{1,17},{9,25},{17,1},{25,9},{2,18},{10... | collective-permute-start | bytes 3145736 | tf_op jit(solution)/shard_map/ppermute | solution.py:26
  481.6 57.2 %collective-permute-start.50 = (bf16[256,2048]{1,0:T(8,128)(2,1)S(1)}, bf16[256,2048]{1,0:T(8,128)(2,1)S(1)}, u32[]{:S(2)}, u32[]{:S(2)}) collective-permute-start(bf16[256,2048]{1,0:T(8,128)(2,1)S(1)} %copy-done.58), channel_id=1, source_target_pairs={{0,24},{8,16},{16,8},{24,0},{1,25},{9,17},{17,9},{25,1},{2,26},{10... | collective-permute-start | bytes 3145736 | tf_op jit(solution)/shard_map/ppermute | solution.py:26
  541.2 39.4 %collective-permute-start.51 = (bf16[256,2048]{1,0:T(8,128)(2,1)}, bf16[256,2048]{1,0:T(8,128)(2,1)S(1)}, u32[]{:S(2)}, u32[]{:S(2)}) collective-permute-start(bf16[256,2048]{1,0:T(8,128)(2,1)} %get-tuple-element.260), channel_id=1, source_target_pairs={{0,8},{8,0},{16,24},{24,16},{1,9},{9,1},{17,25},{25,17},{2,10},{10... | collective-permute-start | bytes 3145736 | tf_op jit(solution)/shard_map/ppermute | solution.py:26
  542.9 48.7 %collective-permute-start.52 = (bf16[256,2048]{1,0:T(8,128)(2,1)}, bf16[256,2048]{1,0:T(8,128)(2,1)}, u32[]{:S(2)}, u32[]{:S(2)}) collective-permute-start(bf16[256,2048]{1,0:T(8,128)(2,1)} %get-tuple-element.261), channel_id=1, source_target_pairs={{0,16},{8,24},{16,0},{24,8},{1,17},{9,25},{17,1},{25,9},{2,18},{10... | collective-permute-start | bytes 3145736 | tf_op jit(solution)/shard_map/ppermute | solution.py:26
  543.5 48.1 %collective-permute-start.53 = (bf16[256,2048]{1,0:T(8,128)(2,1)}, bf16[256,2048]{1,0:T(8,128)(2,1)}, u32[]{:S(2)}, u32[]{:S(2)}) collective-permute-start(bf16[256,2048]{1,0:T(8,128)(2,1)} %get-tuple-element.262), channel_id=1, source_target_pairs={{0,24},{8,16},{16,8},{24,0},{1,25},{9,17},{17,9},{25,1},{2,26},{10... | collective-permute-start | bytes 3145736 | tf_op jit(solution)/shard_map/ppermute | solution.py:26
  613.6 48.5 %collective-permute-start.65 = (bf16[512,1024]{1,0:T(8,128)(2,1)S(1)}, bf16[512,1024]{1,0:T(8,128)(2,1)}, u32[]{:S(2)}, u32[]{:S(2)}) collective-permute-start(bf16[512,1024]{1,0:T(8,128)(2,1)S(1)} %bitcast.229), channel_id=1, source_target_pairs={{0,16},{8,24},{16,0},{24,8},{1,17},{9,25},{17,1},{25,9},{2,18},{10... | collective-permute-start | bytes 3145736 | tf_op jit(solution)/shard_map/ppermute | solution.py:26
  614.9 47.2 %collective-permute-start.66 = (bf16[512,1024]{1,0:T(8,128)(2,1)S(1)}, bf16[512,1024]{1,0:T(8,128)(2,1)}, u32[]{:S(2)}, u32[]{:S(2)}) collective-permute-start(bf16[512,1024]{1,0:T(8,128)(2,1)S(1)} %bitcast.230), channel_id=1, source_target_pairs={{0,24},{8,16},{16,8},{24,0},{1,25},{9,17},{17,9},{25,1},{2,26},{10... | collective-permute-start | bytes 3145736 | tf_op jit(solution)/shard_map/ppermute | solution.py:26
  624.5 57.9 %collective-permute-start.55 = (bf16[256,2048]{1,0:T(8,128)(2,1)}, bf16[256,2048]{1,0:T(8,128)(2,1)S(1)}, u32[]{:S(2)}, u32[]{:S(2)}) collective-permute-start(bf16[256,2048]{1,0:T(8,128)(2,1)} %get-tuple-element.275), channel_id=1, source_target_pairs={{0,8},{8,0},{16,24},{24,16},{1,9},{9,1},{17,25},{25,17},{2,10},{10... | collective-permute-start | bytes 3145736 | tf_op jit(solution)/shard_map/ppermute | solution.py:26
  631.2 76.8 %collective-permute-start.56 = (bf16[256,2048]{1,0:T(8,128)(2,1)}, bf16[256,2048]{1,0:T(8,128)(2,1)}, u32[]{:S(2)}, u32[]{:S(2)}) collective-permute-start(bf16[256,2048]{1,0:T(8,128)(2,1)} %get-tuple-element.276), channel_id=1, source_target_pairs={{0,16},{8,24},{16,0},{24,8},{1,17},{9,25},{17,1},{25,9},{2,18},{10... | collective-permute-start | bytes 3145736 | tf_op jit(solution)/shard_map/ppermute | solution.py:26
  638.3 71.6 %collective-permute-start.57 = (bf16[256,2048]{1,0:T(8,128)(2,1)}, bf16[256,2048]{1,0:T(8,128)(2,1)}, u32[]{:S(2)}, u32[]{:S(2)}) collective-permute-start(bf16[256,2048]{1,0:T(8,128)(2,1)} %get-tuple-element.277), channel_id=1, source_target_pairs={{0,24},{8,16},{16,8},{24,0},{1,25},{9,17},{17,9},{25,1},{2,26},{10... | collective-permute-start | bytes 3145736 | tf_op jit(solution)/shard_map/ppermute | solution.py:26
  673.4 46.8 %collective-permute-start.61 = (f32[77,128]{1,0:T(8,128)}, f32[77,128]{1,0:T(8,128)S(1)}, u32[]{:S(2)}, u32[]{:S(2)}) collective-permute-start(f32[77,128]{1,0:T(8,128)} %add.469), channel_id=1, source_target_pairs={{0,8},{8,0},{16,24},{24,16},{1,9},{9,1},{17,25},{25,17},{2,10},{10... | collective-permute-start | bytes 118280 | tf_op jit(solution)/shard_map/ppermute | solution.py:26
  675.4 45.9 %collective-permute-start.62 = (f32[77,128]{1,0:T(8,128)}, f32[77,128]{1,0:T(8,128)S(1)}, u32[]{:S(2)}, u32[]{:S(2)}) collective-permute-start(f32[77,128]{1,0:T(8,128)} %add.469), channel_id=1, source_target_pairs={{0,16},{8,24},{16,0},{24,8},{1,17},{9,25},{17,1},{25,9},{2,18},{10... | collective-permute-start | bytes 118280 | tf_op jit(solution)/shard_map/ppermute | solution.py:26
  682.3 39.0 %collective-permute-start.63 = (f32[77,128]{1,0:T(8,128)}, f32[77,128]{1,0:T(8,128)S(1)}, u32[]{:S(2)}, u32[]{:S(2)}) collective-permute-start(f32[77,128]{1,0:T(8,128)} %add.469), channel_id=1, source_target_pairs={{0,24},{8,16},{16,8},{24,0},{1,25},{9,17},{17,9},{25,1},{2,26},{10... | collective-permute-start | bytes 118280 | tf_op jit(solution)/shard_map/ppermute | solution.py:26
  (121 other events, 1894.2 us)
Sparse Core Ops, SparseCore 0:
  16.6 63.1 all-gather.3
  81.3 45.8 all-gather.5
  128.8 52.4 all-gather.7
  445.6 88.6 reduce-scatter.2
  591.8 63.6 reduce-scatter.4

commit v2 on v1

--- a/solution.py
+++ b/solution.py
@@ -42,6 +42,23 @@
 
 def far_parts(near, sent):
     return list(near) + [swap(sent[0], "rep", 2), swap(sent[1], "rep", 1)]
+
+
+def gather_halves(own):
+    near = gather_near(own)
+    return far_parts(near, to_far(near))
+
+
+def scatter_far(far):
+    half = far.shape[0] // 2
+    return swap(far[:half], "rep", 1), swap(far[half:], "rep", 2)
+
+
+def scatter_near(own, one, two, low, high):
+    half = low.shape[0]
+    two = jnp.concatenate([(two[:half].astype(F32) + low.astype(F32)).astype(BF16), two[half:]], axis=0)
+    one = jnp.concatenate([one[:half], (one[half:].astype(F32) + high.astype(F32)).astype(BF16)], axis=0)
+    return [own, swap(one, "rep", 1), swap(two, "rep", 2)]
 
 
 def gather_direct(own):
@@ -535,43 +552,83 @@
 
 def turned(place, blocks, out):
     unit = blocks[0].shape[1]
-    for q, block in enumerate(ordered(place[0], [b[...].astype(F32) for b in blocks])):
+    for q, block in enumerate(ordered(place[0], [b.astype(F32) for b in blocks])):
         out[q * unit : (q + 1) * unit, :] = block.T
 
 
 def gate_grad_kernel(place, g0, g1, g2, g3, out):
-    turned(place, (g0, g1, g2, g3), out)
-
-
-def mix_grad_kernel(groups, heads, before, place, *refs):
-    mixes, lasts, (where_heads, out) = refs[:4], refs[4:8], refs[8:]
+    turned(place, [g[...] for g in (g0, g1, g2, g3)], out)
+
+
+def mix_grad_kernel(groups, heads, before, place, m0, m1, m2, low, high, where_heads, out):
     step = pl.program_id(0)
+    width = heads * HEAD_DIM
+    unit = width // groups
+
+    def columns(at, count):
+        whole_blocks = [m[:, pl.ds(at, count)] for m in (m0, m1, m2)]
+        return whole_blocks + [jnp.concatenate([low[:, pl.ds(at, count)], high[:, pl.ds(at, count)]], axis=0)]
 
     @pl.when(step < groups)
     def _():
-        turned(place, mixes, out)
+        turned(place, columns(pl.multiple_of(step * unit, LANES), unit), out)
 
     @pl.when(step == groups)
     def _():
-        both = ordered(place[0], [b[:, : 2 * STATE].astype(F32) for b in lasts])
+        both = ordered(place[0], [b.astype(F32) for b in columns(width, 2 * STATE)])
         out[: 2 * STATE, :] = ((both[0] + both[1]) + (both[2] + both[3])).T
-        steps = ordered(place[0], [b[:, 2 * STATE :] for b in lasts])
+        steps = ordered(place[0], columns(width + 2 * STATE, LANES))
         placed = nn(steps[0], where_heads[0])
         for q in range(1, 4):
             placed = placed + nn(steps[q], where_heads[q])
         out[2 * STATE : 2 * STATE + 4 * heads, :] = placed.T[: 4 * heads, :]
 
 
+def small_kernel(groups, heads, blocks, place, gain, where_heads, *refs):
+    ins, (cw_out, cb_out, norm_out, head_out, pre_out) = refs[:4], refs[4:]
+    parts = ordered(place[0], [b[...] for b in ins])
+    total = (parts[0] + parts[1]) + (parts[2] + parts[3])
+    width = groups * blocks
+
+    def spread(out, row, first):
+        for g in range(groups):
+            for q in range(4):
+                for k in range(blocks):
+                    at = ((g * 4 + q) * blocks + k) * LANES
+                    out[row : row + 1, at : at + LANES] = parts[q][first + g * blocks + k :][:1, :]
+
+    first = 0
+    for k in range(KCONV + 1):
+        out, row = (cw_out, k) if k < KCONV else (cb_out, 0)
+        spread(out, row, first)
+        for c in (0, 1):
+            at = (4 * width + c) * LANES
+            out[row : row + 1, at : at + LANES] = total[first + width + c :][:1, :]
+        first += width + 2
+    spread(norm_out, 0, first)
+    first += width
+    placed = 0.0
+    for q in range(4):
+        rows = jnp.concatenate([parts[q][first : first + 3, :], jnp.zeros((PAD - 3, LANES), F32)], axis=0)
+        placed = placed + jnp.dot(
+            rows, where_heads[q].astype(F32), preferred_element_type=F32, precision=lax.Precision.HIGHEST
+        )
+    head_out[...] = placed
+    first += 3
+    for k in range(pre_out.shape[1] // LANES):
+        pre_out[:, col(k)] = total[first + k :][:1, :] / gain[:, col(k)]
+
+
 def out_grad_kernel(rows, place, b0, b1, b2, b3, out):
     from_rep = place[0] ^ pl.program_id(0)
     count = out.shape[0]
-    for j, block in enumerate((b0, b1, b2, b3)):
+    for j, (block, skip) in enumerate(((b0, rows), (b1, rows), (b2, rows), (b3, 0))):
 
         @pl.when(from_rep == j)
         def _():
             width = block.shape[1]
             for part in range(out.shape[1] // width):
-                first = rows + part * count
+                first = skip + part * count
                 out[:, part * width : (part + 1) * width] = block[first : first + count, :].astype(F32)
 
 
@@ -935,11 +992,14 @@
             + [(normed_all[m], row_spec(model))],
             [(sds((length, model), BF16), whole(length, model))] * reps + [(sds((PAD, model), F32), whole(PAD, model))],
             [],
-            30.0 if m == micro - 1 else 10.0,
+            40.0,
             held(*others),
         )
         pre_parts[m] = ran(pre)[0]
-        normed_grad[m] = blocks[:1] + [swap(blocks[q], "rep", q) for q in (1, 2, 3)]
+        if m == 0:
+            normed_grad[m] = list(blocks[:1]) + [swap(blocks[q], "rep", q) for q in (1, 2, 3)]
+        else:
+            normed_grad[m] = list(blocks[:3]) + list(scatter_far(blocks[3]))
 
     def over_seq(parts):
         return lax.psum_scatter(parts, "seq", scatter_dimension=0, tiled=True)
@@ -962,7 +1022,7 @@
     normalise(1, backward_chain[0].hop())
     branch.append(project_out(1))
     within_back(0, backward_chain[0].hop(), backward_chain[1].hop())
-    within_back(1, backward_chain[0].hop(), backward_chain[1].hop())
+    within_back(1, backward_chain[0].hop(), backward_chain[1].hop(), *branch[0])
     backward_chain[0].rest()
     back(0, backward_chain[0].back(), backward_chain[1].hop())
     backward_chain[1].rest()
@@ -992,8 +1052,9 @@
         )
     complete(0)
     back(1)
-    grad_through(0, *branch[0])
+    grad_through(0)
     complete(1)
+    grad_through(1)
     gain_part, skip_part = sum(g[0] for g in gains), sum(v[0] for v in skips)
     cw_part, cb_part, sb_part, dl_part = (sum(v) for v in zip(*smalls))
     skip_heads = skip_part.reshape(heads, HEAD_DIM).sum(axis=1)
@@ -1003,14 +1064,15 @@
     branch = [later(b) for b in branch]
     output = jnp.stack([sum(v.astype(F32) for v in b) for b in branch])
     output = jnp.where(valid, token_rows + output, 0.0).astype(BF16)
-    mix_part = ran(weight_sum(normed_all, pgs, held(output), 5.0))
-    mix_sums = over_seq(after(mix_part, gate_sums, out_sums))
-    gate_rows = gather_direct(gate_sums)
+    mix_part = ran(weight_sum(normed_all, pgs, held(output), 0.1))
+    mix_sums = over_seq(after(mix_part, gate_sums, out_sums, *normed_grad[0], *normed_grad[1][3:]))
+    normed_grad[0] = later(normed_grad[0])
+    gate_near = gather_near(gate_sums)
+    normed_grad[1] = scatter_near(*normed_grad[1][:3], *after(tuple(normed_grad[1][3:]), *line, *gate_near[1:]))
+    gate_rows = far_parts(gate_near, to_far(gate_near)) if strided else gather_direct(gate_sums)
     out_rows = gate_rows if strided else gather_direct(out_sums)
-    grad_through(1, *normed_grad[0])
     pre_part = sum(pre_parts)
     small_sums = SmallSums(jnp.concatenate([packed, pre_part]).reshape(-1, LANES)).rest()
-    normed_grad = [list(after(tuple(v), mix_sums)) for v in normed_grad]
 
     normed_grad = jnp.stack([sum(v.astype(F32) for v in n) for n in normed_grad])
     xhat = token_rows * inverse
@@ -1037,7 +1099,7 @@
         (out_weight_grad,) = call(
             functools.partial(out_grad_kernel, k_rows),
             reps,
-            [place_in] + [(b, whole(*b.shape)) for b in out_rows],
+            [place_in] + [(b, whole(*b.shape)) for b in gate_rows[:3] + gate_rows[4:]],
             [(sds(out_weight.shape, F32), pl.BlockSpec((out_share, model), lambda i: (i, 0)))],
             [],
             0.9,
@@ -1045,21 +1107,22 @@
         (gate_done,) = call(
             gate_grad_kernel,
             groups,
-            [place_in] + [(b, lanes_spec(lambda i: i)) for b in gate_rows],
+            [place_in] + [(b, lanes_spec(lambda i: i)) for b in gate_rows[:4]],
             [column(0)],
             [],
             0.8,
         )
         finished = [out_weight_grad, gate_done]
-    mix_rows = gather_direct(after(mix_sums, *finished))
-    packed = gather_direct(after(small_sums, mix_sums))
+    mix_rows = (gather_halves if strided else gather_direct)(after(mix_sums, tokens_grad, *finished))
+    both_packed = jnp.stack([small_sums, swap(small_sums, "rep", 1)])
+    far_packed = swap(both_packed, "rep", 2)
+    packed = [both_packed[0], both_packed[1], far_packed[0], far_packed[1]]
     if strided:
         (in_weight_grad,) = call(
             functools.partial(mix_grad_kernel, groups, heads),
             groups + 1,
             [(gate_done, pl.BlockSpec(memory_space=pl.ANY)), place_in]
-            + [(b, lanes_spec(lambda i: jnp.minimum(i, groups - 1))) for b in mix_rows]
-            + [(b[:, width:], whole(k_rows, cols - width)) for b in mix_rows]
+            + [(b, whole(*b.shape)) for b in mix_rows]
             + [(where_heads, whole(reps, LANES, LANES))],
             [column(groups)],
             [],
@@ -1079,23 +1142,24 @@
             ],
             axis=1,
         )
-    flat = [v.reshape(-1) for v in in_order(packed)]
-    def conv_join(values):
-        return jnp.concatenate(
-            [unpick([v[..., :width] for v in values], HEAD_DIM), sum(v[..., width:] for v in values)], axis=-1
-        )
-
-    conv_weight_grad = conv_join([v[: KCONV * xbc].reshape(KCONV, xbc) for v in flat])
-    at = KCONV * xbc
-    conv_bias_grad = conv_join([v[at : at + xbc] for v in flat])
-    at += xbc
-    norm_gain_grad = unpick([v[at : at + width] for v in flat], HEAD_DIM)
-    at += width
-    by_head = [lax.optimization_barrier(v[at : at + 3 * LANES]).reshape(3, LANES)[:, :heads] for v in flat]
-    skip_gain_grad, step_bias_grad, decay_log_grad = unpick(by_head, 1)
-
-    at += 3 * LANES
-    pre_gain_grad = sum(v[at : at + model] for v in flat) / pre_gain
+    channels = conv_bias.shape[0]
+    conv_weight_grad, conv_bias_grad, norm_gain_grad, by_head, pre_gain_grad = call(
+        functools.partial(small_kernel, groups, heads, width // groups // LANES),
+        1,
+        [place_in, (pre_gain[None, :], whole(1, model)), (where_heads, whole(reps, LANES, LANES))]
+        + [(v, whole(*v.shape)) for v in packed],
+        [
+            (sds((KCONV, channels), F32), whole(KCONV, channels)),
+            (sds((1, channels), F32), whole(1, channels)),
+            (sds((1, inner), F32), whole(1, inner)),
+            (sds((PAD, LANES), F32), whole(PAD, LANES)),
+            (sds((1, model), F32), whole(1, model)),
+        ],
+        [],
+        3.0,
+    )
+    conv_bias_grad, norm_gain_grad, pre_gain_grad = conv_bias_grad[0], norm_gain_grad[0], pre_gain_grad[0]
+    skip_gain_grad, step_bias_grad, decay_log_grad = by_head[0, :HEADS], by_head[1, :HEADS], by_head[2, :HEADS]
 
     return (
         output, tokens_grad, pre_gain_grad, in_weight_grad, conv_weight_grad, conv_bias_grad,

time: 772 us -> 690 us (0.89)
  waiting for transfers between devices: 175 us -> 87.1 us
  starting transfers between devices: 97.3 us -> 106 us
  local copies, waits for them, and re-layouts: 57.8 us -> 50 us
    ppermute x46 -> x48, waiting for transfers between devices: 161 us -> 73.3 us  [swap(): lax.ppermute(value, axis, [(i, i ^ bit) for i in range(lax.axis_size(axis...]
    ppermute x46 -> x48, starting transfers between devices: 50.7 us -> 62.2 us  [swap(): lax.ppermute(value, axis, [(i, i ^ bit) for i in range(lax.axis_size(axis...]
    pallas_call x27 -> x28, Pallas kernels: 339 us -> 339 us  [call(): pl.pallas_call(kernel, grid=(slots,), in_specs=[s for _, s in ins], out_s...]
  transfers between devices with their start and end apart: 75 -> 77, of which waited for: 19 -> 18; matrix products, arithmetic and copies ran while one was open for 15% -> 16% of each run, Pallas kernels for 39% -> 48%
where the time goes in v2:
time: 690 us; the launch traced here: 677 us
  Pallas kernels  339 us (49%)
  starting transfers between devices  106 us (15%)
  waiting for transfers between devices  87.1 us (13%)
  other arithmetic  79.6 us (12%)
  local copies, waits for them, and re-layouts  50 us (7%)
  between operations  15.4 us (2%)
    pallas_call x28, Pallas kernels, call(): pl.pallas_call(kernel, grid=(slots,), in_specs=[s for _, s in ins], out_s...  339 us
    ppermute x48, waiting for transfers between devices, swap(): lax.ppermute(value, axis, [(i, i ^ bit) for i in range(lax.axis_size(axis...  73.3 us
    ppermute x48, starting transfers between devices, swap(): lax.ppermute(value, axis, [(i, i ^ bit) for i in range(lax.axis_size(axis...  62.2 us
    convert_element_type x8, other arithmetic, hop(): onto = (self.total + self.total_fade * self.enters.astype(F32)).astype(BF16)  21.2 us
    ppermute x12, starting transfers between devices, hop(): self.enters = self.enters + lax.ppermute(onto, 'seq', [self.onward.pop(0)])  15.1 us
  transfers between devices with their start and end apart: 77, of which 18 were waited for; matrix products, arithmetic and copies ran while one was open for 16% of the time, Pallas kernels for 48%

profile of v2, /device:TPU:0, one launch (start us, length us, event | category | flops | bytes accessed | tf_op | source)
XLA Modules:
  0.0 677.2 jit_solution(198076455488198688)
XLA Ops:
  31.8 16.4 %collective-permute-done.2.two = bf16[256,2048]{1,0:T(8,128)(2,1)} collective-permute-done((bf16[256,2048]{1,0:T(8,128)(2,1)}, bf16[256,2048]{1,0:T(8,128)(2,1)}, u32[]{:S(2)}, u32[]{:S(2)}) %collective-permute-start.2) | collective-permute-done | bytes 1048608 | tf_op jit(solution)/shard_map/ppermute | solution.py:26
  66.8 13.0 %all-gather.4.cloned.1.call-done.right.w_mix = bf16[2048,1408]{1,0:T(8,128)(2,1)} async-done(((bf16[256,1408]{1,0:T(8,128)(2,1)}), bf16[2048,1408]{1,0:T(8,128)(2,1)}) %all-gather.4.cloned.1.call-update) | async-done | bytes 5767184 | tf_op jit(solution)/shard_map/all_gather | solution.py:766
  79.7 12.4 %shard_map.203 = (bf16[1024,1408]{1,0:T(8,128)(2,1)}, bf16[1024,2048]{1,0:T(8,128)(2,1)}) custom-call(bf16[256,2048]{1,0:T(8,128)(2,1)} %get-tuple-element.155.own, bf16[256,2048]{1,0:T(8,128)(2,1)} %collective-permute-done.one, bf16[256,2048]{1,0:T(8,128)(2,1)} %collective-permute-done.2.two, bf16[128,2048]{1,0:T(8,128)(2,1)} %copy-done.57, ...), custom_call_target="tpu_custom_call" | custom-call | flops 11879999488 | bytes 10800000 | tf_op jit(solution)/shard_map/pallas_call | solution.py:648
  112.7 12.5 %shard_map.205 = (bf16[1024,1408]{1,0:T(8,128)(2,1)}, bf16[1024,2048]{1,0:T(8,128)(2,1)}) custom-call(bf16[256,2048]{1,0:T(8,128)(2,1)} %copy-done.26, bf16[256,2048]{1,0:T(8,128)(2,1)} %copy-done.31, bf16[256,2048]{1,0:T(8,128)(2,1)} %copy-done.30, bf16[128,2048]{1,0:T(8,128)(2,1)} %copy-done.58, bf16[128,2048]{1,0:T(8,128)(2,1)} %copy-done.56, ...), custom_call_target="tpu_custom_call" | custom-call | flops 11879999488 | bytes 10800000 | tf_op jit(solution)/shard_map/pallas_call | solution.py:648
  135.7 9.6 %shard_map.206 = (f32[1024,1024]{1,0:T(8,128)}, bf16[1024,512]{1,0:T(8,128)(2,1)}, f32[1024,256]{1,0:T(8,128)}, f32[4,128,1024]{2,1,0:T(8,128)}, bf16[4,144,1024]{2,1,0:T(8,128)(2,1)}, /*index=5*/f32[4,1,1024]{2,1,0:T(1,128)}) custom-call(bf16[1024,1408]{1,0:T(8,128)(2,1)} %get-tuple-element.241.proj, f32[4,8,1280]{2,1,0:T(8,128)} %pad_convert_fusion.halo, ...), custom_call_target="tpu_custom_call" | custom-call | flops 10119999488 | bytes 9200000 | tf_op jit(solution)/shard_map/pallas_call | solution.py:648
  173.4 11.5 %shard_map.208.y = f32[1024,1024]{1,0:T(8,128)} custom-call(f32[1024,1024]{1,0:T(8,128)} %get-tuple-element.227.x, bf16[1024,512]{1,0:T(8,128)(2,1)} %get-tuple-element.178.bc, f32[1024,256]{1,0:T(8,128)} %get-tuple-element.179.sl, bf16[128,1024]{1,0:T(8,128)(2,1)} %and_convert_fusion.spread), custom_call_target="tpu_custom_call" | custom-call | flops 9680000000 | bytes 8800000 | tf_op jit(solution)/shard_map/pallas_call | solution.py:648
  203.6 11.5 %shard_map.210.y = f32[1024,1024]{1,0:T(8,128)} custom-call(f32[1024,1024]{1,0:T(8,128)} %get-tuple-element.230.x, bf16[1024,512]{1,0:T(8,128)(2,1)} %get-tuple-element.184.bc, f32[1024,256]{1,0:T(8,128)} %get-tuple-element.185.sl, bf16[128,1024]{1,0:T(8,128)(2,1)} %and_convert_fusion.spread), custom_call_target="tpu_custom_call" | custom-call | flops 9680000000 | bytes 8800000 | tf_op jit(solution)/shard_map/pallas_call | solution.py:648
  222.6 9.8 %shard_map.211 = (bf16[1024,1024]{1,0:T(8,128)(2,1)}, bf16[1024,2048]{1,0:T(8,128)(2,1)}) custom-call(bf16[256,2048]{1,0:T(8,128)(2,1)} %get-tuple-element.191.own, bf16[256,2048]{1,0:T(8,128)(2,1)} %collective-permute-done.13.one, bf16[256,2048]{1,0:T(8,128)(2,1)} %collective-permute-done.14.two, bf16[128,2048]{1,0:T(8,128)(2,1)} %collective-permute-done.21.low, ...), custom_call_target="tpu_custom_call" | custom-call | flops 11879999488 | bytes 10800000 | tf_op jit(solution)/shard_map/pallas_call | solution.py:648
  239.1 9.8 %shard_map.212 = (bf16[1024,1024]{1,0:T(8,128)(2,1)}, bf16[1024,2048]{1,0:T(8,128)(2,1)}) custom-call(bf16[256,2048]{1,0:T(8,128)(2,1)} %get-tuple-element.198.own, bf16[256,2048]{1,0:T(8,128)(2,1)} %collective-permute-done.15.one, bf16[256,2048]{1,0:T(8,128)(2,1)} %collective-permute-done.16.two, bf16[128,2048]{1,0:T(8,128)(2,1)} %collective-permute-done.19.low, ...), custom_call_target="tpu_custom_call" | custom-call | flops 11879999488 | bytes 10800000 | tf_op jit(solution)/shard_map/pallas_call | solution.py:648
  252.3 9.7 %shard_map.213 = (f32[1024,1024]{1,0:T(8,128)}, f32[4,8,256]{2,1,0:T(8,128)}) custom-call(f32[1024,1024]{1,0:T(8,128)} %shard_map.208.y, f32[1024,1024]{1,0:T(8,128)} %get-tuple-element.227.x, bf16[1024,512]{1,0:T(8,128)(2,1)} %get-tuple-element.178.bc, f32[1024,256]{1,0:T(8,128)} %get-tuple-element.179.sl, bf16[4,128,1024]{2,1,0:T(8,128)(2,1)} %fusion.23.start, ...), custom_call_target="tpu_custom_call" | custom-call | flops 12320000000 | bytes 11200000 | tf_op jit(solution)/shard_map/pallas_call | solution.py:648
  287.9 12.2 %shard_map.215 = (bf16[1024,1024]{1,0:T(8,128)(2,1)}, bf16[1024,1024]{1,0:T(8,128)(2,1)}, bf16[1024,1024]{1,0:T(8,128)(2,1)}, f32[4,128,1024]{2,1,0:T(8,128)}, b...) custom-call(f32[1024,1024]{1,0:T(8,128)} %get-tuple-element.209.y, ...), custom_call_target="tpu_custom_call" | custom-call | flops 13639999488 | bytes 12400000 | tf_op jit(solution)/shard_map/pallas_call | solution.py:648
  301.7 9.9 %shard_map.216 = (bf16[256,2048]{1,0:T(8,128)(2,1)}, bf16[256,2048]{1,0:T(8,128)(2,1)}, bf16[256,2048]{1,0:T(8,128)(2,1)}, bf16[256,2048]{1,0:T(8,128)(2,1)}) custom-call(bf16[1024,1024]{1,0:T(8,128)(2,1)} %get-tuple-element.212.left.refs_4_, bf16[1024,2048]{1,0:T(8,128)(2,1)} %all-gather.8.cloned.1.call-done.right), custom_call_target="tpu_custom_call" | custom-call | flops 8360000000 | bytes 7600000 | tf_op jit(solution)/shard_map/pallas_call | solution.py:648
  317.6 12.2 %shard_map.217 = (bf16[1024,1024]{1,0:T(8,128)(2,1)}, bf16[1024,1024]{1,0:T(8,128)(2,1)}, bf16[1024,1024]{1,0:T(8,128)(2,1)}, f32[4,128,1024]{2,1,0:T(8,128)}, b...) custom-call(f32[1024,1024]{1,0:T(8,128)} %get-tuple-element.220.y, ...), custom_call_target="tpu_custom_call" | custom-call | flops 13639999488 | bytes 12400000 | tf_op jit(solution)/shard_map/pallas_call | solution.py:648
  334.6 9.9 %shard_map.218 = (bf16[256,2048]{1,0:T(8,128)(2,1)}, bf16[256,2048]{1,0:T(8,128)(2,1)}, bf16[256,2048]{1,0:T(8,128)(2,1)}, bf16[256,2048]{1,0:T(8,128)(2,1)}) custom-call(bf16[1024,1024]{1,0:T(8,128)(2,1)} %get-tuple-element.223.left.refs_5_, bf16[1024,2048]{1,0:T(8,128)(2,1)} %all-gather.8.cloned.1.call-done.right), custom_call_target="tpu_custom_call" | custom-call | flops 8360000000 | bytes 7600000 | tf_op jit(solution)/shard_map/pallas_call | solution.py:648
  351.4 14.1 %shard_map.219 = (f32[1024,1024]{1,0:T(8,128)}, f32[1024,256]{1,0:T(8,128)}) custom-call(f32[1024,1024]{1,0:T(8,128)} %get-tuple-element.227.x, bf16[1024,512]{1,0:T(8,128)(2,1)} %get-tuple-element.178.bc, f32[1024,256]{1,0:T(8,128)} %get-tuple-element.179.sl, bf16[1024,1024]{1,0:T(8,128)(2,1)} %get-tuple-element.228.dy, ...), custom_call_target="tpu_custom_call" | custom-call | flops 15840000000 | bytes 14400000 | tf_op jit(solution)/shard_map/pallas_call | solution.py:648
  382.2 14.1 %shard_map.220 = (f32[1024,1024]{1,0:T(8,128)}, f32[1024,256]{1,0:T(8,128)}) custom-call(f32[1024,1024]{1,0:T(8,128)} %get-tuple-element.230.x, bf16[1024,512]{1,0:T(8,128)(2,1)} %get-tuple-element.184.bc, f32[1024,256]{1,0:T(8,128)} %get-tuple-element.185.sl, bf16[1024,1024]{1,0:T(8,128)(2,1)} %get-tuple-element.231.dy, ...), custom_call_target="tpu_custom_call" | custom-call | flops 15840000000 | bytes 14400000 | tf_op jit(solution)/shard_map/pallas_call | solution.py:648
  402.4 20.5 %shard_map.221 = (bf16[1024,1408]{1,0:T(8,128)(2,1)}, f32[4,8,1280]{2,1,0:T(8,128)}, f32[4,8,1280]{2,1,0:T(8,128)}, f32[8,1280]{1,0:T(8,128)}, f32[8,1280]{1,0:T...) custom-call(bf16[1024,1408]{1,0:T(8,128)(2,1)} %get-tuple-element.233.proj, f32[4,8,1280]{2,1,0:T(8,128)} %pad_convert_fusion.1.halo, ...), custom_call_target="tpu_custom_call" | custom-call | flops 22439999488 | bytes 20400000 | tf_op jit(solution)/shard_map/pallas_call | solution.py:648
  428.6 25.5 %shard_map.222 = bf16[8,512,1024]{2,1,0:T(8,128)(2,1)} custom-call(bf16[1024,2048]{1,0:T(8,128)(2,1)} %get-tuple-element.271.left.refs_0_.normed, bf16[1024,2048]{1,0:T(8,128)(2,1)} %get-tuple-element.182.left.refs_1_.normed, bf16[1024,1024]{1,0:T(8,128)(2,1)} %get-tuple-element.237.refs_2_.gate, bf16[1024,1024]{1,0:T(8,128)(2,1)} %get-tuple-element.238.refs_3_.gate, ...), custom_call_target="tpu_custom_call" | custom-call | flops 28160000000 | bytes 25600000 | tf_op jit(solution)/shard_map/pallas_call | solution.py:648
  458.7 20.5 %shard_map.223 = (bf16[1024,1408]{1,0:T(8,128)(2,1)}, f32[4,8,1280]{2,1,0:T(8,128)}, f32[4,8,1280]{2,1,0:T(8,128)}, f32[8,1280]{1,0:T(8,128)}, f32[8,1280]{1,0:T...) custom-call(bf16[1024,1408]{1,0:T(8,128)(2,1)} %get-tuple-element.241.proj, f32[4,8,1280]{2,1,0:T(8,128)} %pad_convert_fusion.halo, ...), custom_call_target="tpu_custom_call" | custom-call | flops 22439999488 | bytes 20400000 | tf_op jit(solution)/shard_map/pallas_call | solution.py:648
  482.2 19.1 %shard_map.224 = (bf16[256,2048]{1,0:T(8,128)(2,1)}, bf16[256,2048]{1,0:T(8,128)(2,1)}, bf16[256,2048]{1,0:T(8,128)(2,1)}, bf16[256,2048]{1,0:T(8,128)(2,1)}, f32[8,2048]{1,0:T(8,128)}) custom-call(bf16[1024,1408]{1,0:T(8,128)(2,1)} %bitcast.110, bf16[1024,1024]{1,0:T(8,128)(2,1)} %get-tuple-element.237.refs_2_.gate, ...), custom_call_target="tpu_custom_call" | custom-call | flops 176000008192 | bytes 160000000 | tf_op jit(solution)/shard_map/pallas_call | solution.py:648
  506.8 19.1 %shard_map.225 = (bf16[256,2048]{1,0:T(8,128)(2,1)}, bf16[256,2048]{1,0:T(8,128)(2,1)}, bf16[256,2048]{1,0:T(8,128)(2,1)}, bf16[256,2048]{1,0:T(8,128)(2,1)}, f32[8,2048]{1,0:T(8,128)}) custom-call(bf16[1024,1408]{1,0:T(8,128)(2,1)} %bitcast.113, bf16[1024,1024]{1,0:T(8,128)(2,1)} %get-tuple-element.238.refs_3_.gate, ...), custom_call_target="tpu_custom_call" | custom-call | flops 176000008192 | bytes 160000000 | tf_op jit(solution)/shard_map/pallas_call | solution.py:648
  539.0 18.7 %shard_map.226 = bf16[2048,1408]{1,0:T(8,128)(2,1)} custom-call(bf16[1024,2048]{1,0:T(8,128)(2,1)} %get-tuple-element.271.left.refs_0_.normed, bf16[1024,2048]{1,0:T(8,128)(2,1)} %get-tuple-element.182.left.refs_1_.normed, bf16[1024,1408]{1,0:T(8,128)(2,1)} %bitcast.111, bf16[1024,1408]{1,0:T(8,128)(2,1)} %bitcast.114), custom_call_target="tpu_custom_call" | custom-call | flops 880000000 | bytes 800000 | tf_op jit(solution)/shard_map/pallas_call | solution.py:648
  620.6 9.9 %collective-permute-done.60 = bf16[256,2048]{1,0:T(8,128)(2,1)S(1)} collective-permute-done((bf16[256,2048]{1,0:T(8,128)(2,1)}, bf16[256,2048]{1,0:T(8,128)(2,1)S(1)}, u32[]{:S(2)}, u32[]{:S(2)}) %collective-permute-start.60) | collective-permute-done | bytes 1048608 | tf_op jit(solution)/shard_map/ppermute | solution.py:26
  641.3 12.5 %collective-permute-done.65 = f32[2,77,128]{2,1,0:T(8,128)S(1)} collective-permute-done((f32[2,77,128]{2,1,0:T(8,128)S(1)}, f32[2,77,128]{2,1,0:T(8,128)S(1)}, u32[]{:S(2)}, u32[]{:S(2)}) %collective-permute-start.65) | collective-permute-done | bytes 78880 | tf_op jit(solution)/shard_map/ppermute | solution.py:26
  (448 shorter events, 327.2 us)
Async XLA Ops:
  7.2 72.6 %all-gather.4.cloned.1.call-start = ((), (), s32[]{:S(2)}) async-start(), calls=%async_computation.2 | async-start | bytes 6488064 | tf_op jit(solution)/shard_map/all_gather | solution.py:766
  16.5 135.6 %all-gather.6.cloned.1.call-start = ((), (), s32[]{:S(2)}) async-start(), calls=%async_computation.3 | async-start | bytes 4718592 | tf_op jit(solution)/shard_map/all_gather | solution.py:767
  17.6 205.0 %all-gather.8.cloned.1.call-start = ((), (), s32[]{:S(2)}) async-start(), calls=%async_computation.4 | async-start | bytes 4718592 | tf_op jit(solution)/shard_map/all_gather | solution.py:771
  27.0 537.1 %reduce-scatter.3.cloned.1.call-start = ((), (), s32[]{:S(2)}) async-start(), calls=%async_computation.5 | async-start | bytes 9437184 | tf_op jit(solution)/shard_map/reduce_scatter | solution.py:1005
  64.7 31.6 %collective-permute-start.5 = (bf16[256,2048]{1,0:T(8,128)(2,1)S(1)}, bf16[256,2048]{1,0:T(8,128)(2,1)S(1)}, u32[]{:S(2)}, u32[]{:S(2)}) collective-permute-start(bf16[256,2048]{1,0:T(8,128)(2,1)S(1)} %get-tuple-element.165.own), channel_id=1, source_target_pairs={{0,16},{8,24},{16,0},{24,8},{1,17},{9,25},{17,1},{25,9},{2,18},{10... | collective-permute-start | bytes 3145736 | tf_op jit(solution)/shard_map/ppermute | solution.py:26
  133.8 32.6 %collective-permute-start.11 = (bf16[4,128,1024]{2,1,0:T(8,128)(2,1)}, bf16[4,128,1024]{2,1,0:T(8,128)(2,1)}, u32[]{:S(2)}, u32[]{:S(2)}) collective-permute-start(bf16[4,128,1024]{2,1,0:T(8,128)(2,1)} %fusion.29), channel_id=1, source_target_pairs={{1,3},{9,11},{17,19},{25,27}} | collective-permute-start | bytes 3145736 | tf_op jit(solution)/shard_map/ppermute | solution.py:140
  163.7 51.4 %collective-permute-start.22 = (bf16[128,2048]{1,0:T(8,128)(2,1)}, bf16[128,2048]{1,0:T(8,128)(2,1)}, u32[]{:S(2)}, u32[]{:S(2)}) collective-permute-start(bf16[128,2048]{1,0:T(8,128)(2,1)} %slice.288), channel_id=1, source_target_pairs={{0,8},{8,0},{16,24},{24,16},{1,9},{9,1},{17,25},{25,17},{2,10},{10... | collective-permute-start | bytes 1572872 | tf_op jit(solution)/shard_map/ppermute | solution.py:26
  164.4 52.7 %collective-permute-start.21 = (bf16[128,2048]{1,0:T(8,128)(2,1)S(1)}, bf16[128,2048]{1,0:T(8,128)(2,1)}, u32[]{:S(2)}, u32[]{:S(2)}) collective-permute-start(bf16[128,2048]{1,0:T(8,128)(2,1)S(1)} %slice.287), channel_id=1, source_target_pairs={{0,16},{8,24},{16,0},{24,8},{1,17},{9,25},{17,1},{25,9},{2,18},{10... | collective-permute-start | bytes 1572872 | tf_op jit(solution)/shard_map/ppermute | solution.py:26
  165.3 51.9 %collective-permute-start.16 = (bf16[256,2048]{1,0:T(8,128)(2,1)}, bf16[256,2048]{1,0:T(8,128)(2,1)}, u32[]{:S(2)}, u32[]{:S(2)}) collective-permute-start(bf16[256,2048]{1,0:T(8,128)(2,1)} %get-tuple-element.198.own), channel_id=1, source_target_pairs={{0,16},{8,24},{16,0},{24,8},{1,17},{9,25},{17,1},{25,9},{2,18},{10... | collective-permute-start | bytes 3145736 | tf_op jit(solution)/shard_map/ppermute | solution.py:26
  199.2 33.2 %collective-permute-start.23 = (bf16[4,128,1024]{2,1,0:T(8,128)(2,1)}, bf16[4,128,1024]{2,1,0:T(8,128)(2,1)}, u32[]{:S(2)}, u32[]{:S(2)}) collective-permute-start(bf16[4,128,1024]{2,1,0:T(8,128)(2,1)} %get-tuple-element.309), channel_id=1, source_target_pairs={{5,7},{13,15},{21,23},{29,31}} | collective-permute-start | bytes 3145736 | tf_op jit(solution)/shard_map/ppermute | solution.py:140
  311.6 56.7 %collective-permute-start.31 = (bf16[256,2048]{1,0:T(8,128)(2,1)}, bf16[256,2048]{1,0:T(8,128)(2,1)}, u32[]{:S(2)}, u32[]{:S(2)}) collective-permute-start(bf16[256,2048]{1,0:T(8,128)(2,1)} %get-tuple-element.214), channel_id=1, source_target_pairs={{0,8},{8,0},{16,24},{24,16},{1,9},{9,1},{17,25},{25,17},{2,10},{10... | collective-permute-start | bytes 3145736 | tf_op jit(solution)/shard_map/ppermute | solution.py:26
  312.6 56.8 %collective-permute-start.32 = (bf16[256,2048]{1,0:T(8,128)(2,1)}, bf16[256,2048]{1,0:T(8,128)(2,1)}, u32[]{:S(2)}, u32[]{:S(2)}) collective-permute-start(bf16[256,2048]{1,0:T(8,128)(2,1)} %get-tuple-element.215), channel_id=1, source_target_pairs={{0,16},{8,24},{16,0},{24,8},{1,17},{9,25},{17,1},{25,9},{2,18},{10... | collective-permute-start | bytes 3145736 | tf_op jit(solution)/shard_map/ppermute | solution.py:26
  313.8 56.9 %collective-permute-start.33 = (bf16[256,2048]{1,0:T(8,128)(2,1)}, bf16[256,2048]{1,0:T(8,128)(2,1)}, u32[]{:S(2)}, u32[]{:S(2)}) collective-permute-start(bf16[256,2048]{1,0:T(8,128)(2,1)} %get-tuple-element.216), channel_id=1, source_target_pairs={{0,24},{8,16},{16,8},{24,0},{1,25},{9,17},{17,9},{25,1},{2,26},{10... | collective-permute-start | bytes 3145736 | tf_op jit(solution)/shard_map/ppermute | solution.py:26
  365.6 160.4 %collective-permute-start.49 = (bf16[256,2048]{1,0:T(8,128)(2,1)}, bf16[256,2048]{1,0:T(8,128)(2,1)}, u32[]{:S(2)}, u32[]{:S(2)}) collective-permute-start(bf16[256,2048]{1,0:T(8,128)(2,1)} %get-tuple-element.260), channel_id=1, source_target_pairs={{0,8},{8,0},{16,24},{24,16},{1,9},{9,1},{17,25},{25,17},{2,10},{10... | collective-permute-start | bytes 3145736 | tf_op jit(solution)/shard_map/ppermute | solution.py:26
  368.2 158.5 %collective-permute-start.50 = (bf16[256,2048]{1,0:T(8,128)(2,1)}, bf16[256,2048]{1,0:T(8,128)(2,1)}, u32[]{:S(2)}, u32[]{:S(2)}) collective-permute-start(bf16[256,2048]{1,0:T(8,128)(2,1)} %get-tuple-element.261), channel_id=1, source_target_pairs={{0,16},{8,24},{16,0},{24,8},{1,17},{9,25},{17,1},{25,9},{2,18},{10... | collective-permute-start | bytes 3145736 | tf_op jit(solution)/shard_map/ppermute | solution.py:26
  369.4 157.3 %collective-permute-start.51 = (bf16[256,2048]{1,0:T(8,128)(2,1)}, bf16[256,2048]{1,0:T(8,128)(2,1)}, u32[]{:S(2)}, u32[]{:S(2)}) collective-permute-start(bf16[256,2048]{1,0:T(8,128)(2,1)} %get-tuple-element.262), channel_id=1, source_target_pairs={{0,24},{8,16},{16,8},{24,0},{1,25},{9,17},{17,9},{25,1},{2,26},{10... | collective-permute-start | bytes 3145736 | tf_op jit(solution)/shard_map/ppermute | solution.py:26
  454.2 181.4 %reduce-scatter.5.cloned.1.call-start = ((), (), s32[]{:S(2)}) async-start(), calls=%async_computation.6 | async-start | bytes 6488064 | tf_op jit(solution)/shard_map/reduce_scatter | solution.py:1005
  501.3 62.8 %collective-permute-start.52 = (bf16[256,2048]{1,0:T(8,128)(2,1)}, bf16[256,2048]{1,0:T(8,128)(2,1)}, u32[]{:S(2)}, u32[]{:S(2)}) collective-permute-start(bf16[256,2048]{1,0:T(8,128)(2,1)} %get-tuple-element.268), channel_id=1, source_target_pairs={{0,8},{8,0},{16,24},{24,16},{1,9},{9,1},{17,25},{25,17},{2,10},{10... | collective-permute-start | bytes 3145736 | tf_op jit(solution)/shard_map/ppermute | solution.py:26
  502.5 61.6 %collective-permute-start.53 = (bf16[256,2048]{1,0:T(8,128)(2,1)}, bf16[256,2048]{1,0:T(8,128)(2,1)}, u32[]{:S(2)}, u32[]{:S(2)}) collective-permute-start(bf16[256,2048]{1,0:T(8,128)(2,1)} %get-tuple-element.269), channel_id=1, source_target_pairs={{0,16},{8,24},{16,0},{24,8},{1,17},{9,25},{17,1},{25,9},{2,18},{10... | collective-permute-start | bytes 3145736 | tf_op jit(solution)/shard_map/ppermute | solution.py:26
  525.9 38.2 %collective-permute-start.54 = (bf16[256,2048]{1,0:T(8,128)(2,1)}, bf16[256,2048]{1,0:T(8,128)(2,1)S(1)}, u32[]{:S(2)}, u32[]{:S(2)}) collective-permute-start(bf16[256,2048]{1,0:T(8,128)(2,1)} %get-tuple-element.270), channel_id=1, source_target_pairs={{0,24},{8,16},{16,8},{24,0},{1,25},{9,17},{17,9},{25,1},{2,26},{10... | collective-permute-start | bytes 3145736 | tf_op jit(solution)/shard_map/ppermute | solution.py:26
  529.0 35.1 %collective-permute-start.56 = (bf16[128,2048]{1,0:T(8,128)(2,1)}, bf16[128,2048]{1,0:T(8,128)(2,1)}, u32[]{:S(2)}, u32[]{:S(2)}) collective-permute-start(bf16[128,2048]{1,0:T(8,128)(2,1)} %get-tuple-element.319), channel_id=1, source_target_pairs={{0,16},{8,24},{16,0},{24,8},{1,17},{9,25},{17,1},{25,9},{2,18},{10... | collective-permute-start | bytes 1572872 | tf_op jit(solution)/shard_map/ppermute | solution.py:26
  530.3 33.8 %collective-permute-start.55 = (bf16[128,2048]{1,0:T(8,128)(2,1)}, bf16[128,2048]{1,0:T(8,128)(2,1)}, u32[]{:S(2)}, u32[]{:S(2)}) collective-permute-start(bf16[128,2048]{1,0:T(8,128)(2,1)} %get-tuple-element.320), channel_id=1, source_target_pairs={{0,8},{8,0},{16,24},{24,16},{1,9},{9,1},{17,25},{25,17},{2,10},{10... | collective-permute-start | bytes 1572872 | tf_op jit(solution)/shard_map/ppermute | solution.py:26
  588.4 50.0 %collective-permute-start.64 = (f32[77,128]{1,0:T(8,128)}, f32[77,128]{1,0:T(8,128)}, u32[]{:S(2)}, u32[]{:S(2)}) collective-permute-start(f32[77,128]{1,0:T(8,128)} %add.443.refs_0_), channel_id=1, source_target_pairs={{0,8},{8,0},{16,24},{24,16},{1,9},{9,1},{17,25},{25,17},{2,10},{10... | collective-permute-start | bytes 118280 | tf_op jit(solution)/shard_map/ppermute | solution.py:26
  598.7 31.7 %collective-permute-start.60 = (bf16[256,2048]{1,0:T(8,128)(2,1)}, bf16[256,2048]{1,0:T(8,128)(2,1)S(1)}, u32[]{:S(2)}, u32[]{:S(2)}) collective-permute-start(bf16[256,2048]{1,0:T(8,128)(2,1)} %pad_maximum_fusion.1), channel_id=1, source_target_pairs={{0,16},{8,24},{16,0},{24,8},{1,17},{9,25},{17,1},{25,9},{2,18},{10... | collective-permute-start | bytes 3145736 | tf_op jit(solution)/shard_map/ppermute | solution.py:26
  (118 other events, 1417.8 us)
Sparse Core Ops, SparseCore 0:
  16.6 63.1 all-gather.3
  81.3 45.8 all-gather.5
  128.8 52.4 all-gather.7
  454.3 93.1 reduce-scatter.2
  565.3 69.4 reduce-scatter.4

commit v3 on v2

--- a/solution.py
+++ b/solution.py
@@ -44,11 +44,6 @@
     return list(near) + [swap(sent[0], "rep", 2), swap(sent[1], "rep", 1)]
 
 
-def gather_halves(own):
-    near = gather_near(own)
-    return far_parts(near, to_far(near))
-
-
 def scatter_far(far):
     half = far.shape[0] // 2
     return swap(far[:half], "rep", 1), swap(far[half:], "rep", 2)
@@ -58,7 +53,7 @@
     half = low.shape[0]
     two = jnp.concatenate([(two[:half].astype(F32) + low.astype(F32)).astype(BF16), two[half:]], axis=0)
     one = jnp.concatenate([one[:half], (one[half:].astype(F32) + high.astype(F32)).astype(BF16)], axis=0)
-    return [own, swap(one, "rep", 1), swap(two, "rep", 2)]
+    return [own, swap(one, "rep", 1), swap(two, "rep", 2)], (one, two)
 
 
 def gather_direct(own):
@@ -132,11 +127,10 @@
             got = self.got
             self.mate = got[:, :STATE].astype(F32)
             self.mate_fade = got[:, STATE : STATE + 1].astype(F32) + got[:, STATE + 1 : STATE + 2].astype(F32)
-            self.total = self.part + self.fade * self.mate
+            onto = self.total = (self.part + self.fade * self.mate).astype(BF16)
             self.total_fade = self.fade * self.mate_fade
-            onto = self.total.astype(BF16)
         else:
-            onto = (self.total + self.total_fade * self.enters.astype(F32)).astype(BF16)
+            onto = (self.total.astype(F32) + self.total_fade * self.enters.astype(F32)).astype(BF16)
         self.enters = self.enters + lax.ppermute(onto, "seq", [self.onward.pop(0)])
         return onto
 
@@ -263,7 +257,7 @@
     ext_rows = pl.ds(PAD, rows)
 
     def activated(p):
-        ext[0:PAD, :] = halo[0, :, col(p)]
+        ext[0:PAD, :] = halo[0, :, col(p)].astype(F32)[MARK - PAD :]
         ext[ext_rows, :] = proj[:, col(p)].astype(F32)
         z = cb[:, col(p)] + cw[0:1, col(p)] * ext[pl.ds(PAD - 3, rows), :]
         for k in range(1, KCONV):
@@ -286,22 +280,30 @@
 
 def inside_kernel(x, bc, sl, spread, y_out):
     rows = x.shape[0]
+    half = rows // 2
     pairs = x.shape[1] // LANES
     scores = nt_fine(bc[:, 2 * STATE :], bc[:, : 2 * STATE])
     log_decay = sl[:, LANES:]
     across = log_decay.T
     step = two_parts(sl[:, :LANES])
-    t = lax.broadcasted_iota(jnp.int32, (rows, rows), 0)
-    s = lax.broadcasted_iota(jnp.int32, (rows, rows), 1)
+    t = lax.broadcasted_iota(jnp.int32, (half, half), 0)
+    s = lax.broadcasted_iota(jnp.int32, (half, half), 1)
     causal = t >= s
     low_lanes = lax.broadcasted_iota(jnp.int32, (rows, LANES), 1) < HEAD_DIM
+
+    def weights(h, later, earlier, masked):
+        gap = log_decay[later, h : h + 1] - across[h : h + 1, earlier]
+        gap = jnp.where(causal, gap, NEVER) if masked else gap
+        return (scores[later, earlier] * jnp.exp(gap)).astype(BF16)
+
+    first, second = slice(0, half), slice(half, rows)
     for p in range(pairs):
         scaled = (x[:, col(p)] * nn(step, spread[:, col(p)])).astype(BF16)
         outs = []
         for h in (2 * p, 2 * p + 1):
-            gap = log_decay[:, h : h + 1] - across[h : h + 1, :]
-            weights = (scores * jnp.exp(jnp.where(causal, gap, NEVER))).astype(BF16)
-            outs.append(nn(weights, scaled))
+            above = nn(weights(h, first, first, True), scaled[:half])
+            below = jnp.concatenate([weights(h, second, first, False), weights(h, second, second, True)], axis=1)
+            outs.append(jnp.concatenate([above, nn(below, scaled)], axis=0))
         y_out[:, col(p)] = jnp.where(low_lanes, outs[0], outs[1])
 
 
@@ -370,6 +372,7 @@
 
 def inside_back_kernel(x, bc, sl, dy, start, spread, dxs_out, dbc_out):
     rows = x.shape[0]
+    half = rows // 2
     pairs = x.shape[1] // LANES
     b_rows = bc[:, : 2 * STATE]
     c_rows = bc[:, 2 * STATE :]
@@ -378,11 +381,18 @@
     across = log_decay.T
     step = two_parts(sl[:, :LANES])
     decay = two_parts(jnp.exp(log_decay))
-    s = lax.broadcasted_iota(jnp.int32, (rows, rows), 0)
-    t = lax.broadcasted_iota(jnp.int32, (rows, rows), 1)
+    s = lax.broadcasted_iota(jnp.int32, (half, half), 0)
+    t = lax.broadcasted_iota(jnp.int32, (half, half), 1)
     causal = t >= s
     low_lanes = lax.broadcasted_iota(jnp.int32, (rows, LANES), 1) < HEAD_DIM
-    score_grad = jnp.zeros((rows, rows), F32)
+
+    def falls(h, earlier, later, masked):
+        gap = across[h : h + 1, later] - log_decay[earlier, h : h + 1]
+        return jnp.exp(jnp.where(causal, gap, NEVER) if masked else gap)
+
+    first, second = slice(0, half), slice(half, rows)
+    above_grad = jnp.zeros((half, rows), F32)
+    below_grad = jnp.zeros((half, half), F32)
     dc = jnp.zeros((rows, LANES), F32)
     for p in range(pairs):
         scaled = x[:, col(p)] * nn(step, spread[:, col(p)])
@@ -391,13 +401,24 @@
         dc = dc + nt(faded, start[0, :, col(p)])
         outs = []
         for h in (2 * p, 2 * p + 1):
-            gap = across[h : h + 1, :] - log_decay[:, h : h + 1]
-            fall = jnp.exp(jnp.where(causal, gap, NEVER))
-            weights = (scores * fall).astype(BF16)
-            outs.append(nn(weights, dyp))
+            above = jnp.concatenate([falls(h, first, first, True), falls(h, first, second, False)], axis=1)
+            below = falls(h, second, second, True)
+            outs.append(
+                jnp.concatenate(
+                    [
+                        nn((scores[:half] * above).astype(BF16), dyp),
+                        nn((scores[half:, half:] * below).astype(BF16), dyp[half:]),
+                    ],
+                    axis=0,
+                )
+            )
             mine = low_lanes if h % 2 == 0 else jnp.logical_not(low_lanes)
-            score_grad = score_grad + fall * nt(jnp.where(mine, scaled, 0.0).astype(BF16), dyp)
+            own = jnp.where(mine, scaled, 0.0).astype(BF16)
+            above_grad = above_grad + above * nt(own[:half], dyp)
+            below_grad = below_grad + below * nt(own[half:], dyp[half:])
         dxs_out[:, col(p)] = jnp.where(low_lanes, outs[0], outs[1])
+    below_grad = jnp.concatenate([jnp.zeros((half, half), F32), below_grad], axis=1)
+    score_grad = jnp.concatenate([above_grad, below_grad], axis=0)
     dbc_out[:, col(0)] = nn_fine(*split(score_grad), c_rows)
     dbc_out[:, col(1)] = dc + nn_fine(*split(score_grad.T), b_rows)
 
@@ -425,7 +446,7 @@
     dext[pl.ds(PAD + rows, PAD), :] = jnp.zeros((PAD, LANES), F32)
 
     def through_conv(p, grad):
-        ext[0:PAD, :] = halo[0, :, col(p)]
+        ext[0:PAD, :] = halo[0, :, col(p)].astype(F32)[MARK - PAD :]
         ext[pl.ds(PAD, rows), :] = proj[:, col(p)].astype(F32)
         taps = [ext[pl.ds(PAD - 3 + k, rows), :] for k in range(KCONV)]
         z = cb[:, col(p)] + cw[0:1, col(p)] * taps[0]
@@ -481,20 +502,21 @@
     out[...] = product(left[...], right[...]).astype(BF16)
 
 
-def gathered_kernel(product, own, one, two, low, high, right, out, left):
-    half = low.shape[0]
-    for j, block in enumerate((own, one, two)):
+def gathered_kernel(product, count, *refs):
+    blocks, (right, out, left, *last) = refs[:count], refs[count:]
+    for j in range(4):
 
         @pl.when(pl.program_id(0) == j)
         def _():
-            left[...] = block[...]
-
-    @pl.when(pl.program_id(0) == 3)
-    def _():
-        left[:half, :] = low[...]
-        left[half:, :] = high[...]
+            first = 0
+            for block in blocks[j : j + 1] if j < 3 else blocks[3:]:
+                value = block[...].reshape(block.shape[-2:])
+                left[first : first + value.shape[0], :] = value
+                first += value.shape[0]
 
     out[...] = product(left[...], right[...]).astype(BF16)
+    for tail in last:
+        tail[0] = out[out.shape[0] - tail.shape[1] :, : tail.shape[2]]
 
 
 def weight_kernel(*refs):
@@ -517,13 +539,15 @@
         out[0, rows + part * half : rows + (part + 1) * half] = back[:, part * width : (part + 1) * width].astype(BF16)
 
 
-def branch_kernel(left, right, *outs):
-    value = nn(left[...], right[...]).astype(BF16)
+def branch_kernel(count, *refs):
+    lefts, right, outs = refs[:count], refs[count], refs[count + 1 :]
+    values = [nn(left[...], right[...]).astype(BF16) for left in lefts]
     for q, out in enumerate(outs):
 
         @pl.when(pl.program_id(0) == q)
         def _():
-            out[...] = value
+            for m, value in enumerate(values):
+                out[m] = value
 
 
 def grad_kernel(mix, gate, w_mix, w_gate, normed, o0, o1, o2, o3, pre):
@@ -654,7 +678,7 @@
         scratch_shapes=scratch,
         input_output_aliases=alias or {},
         compiler_params=pltpu.CompilerParams(
-            dimension_semantics=("arbitrary",), vmem_limit_bytes=56 * 1024 * 1024
+            dimension_semantics=("arbitrary",), vmem_limit_bytes=48 * 1024 * 1024
         ),
         cost_estimate=pl.CostEstimate(
             flops=int(us * slots * 1.1e9 * COST), bytes_accessed=int(us * slots * 1e6 * COST), transcendentals=0
@@ -681,15 +705,19 @@
     return out
 
 
-def gathered_times(parts, right, product, held):
-    rows, depth = parts[0].shape
+def gathered_times(parts, right, product, held, batch=None, last=()):
+    rows, depth = parts[0].shape[-2:]
+    if batch is None:
+        ins = [(v, whole(*v.shape)) for v in parts]
+    else:
+        ins = [(v, pl.BlockSpec((1, rows, depth), lambda i: (batch, 0, 0))) for v in parts]
     width = right.shape[1] if product is nn else right.shape[0]
     block = lambda w: (sds((4 * rows, w), BF16), pl.BlockSpec((rows, w), lambda i: (i, 0)))
     return call(
-        functools.partial(gathered_kernel, product),
+        functools.partial(gathered_kernel, product, len(parts)),
         4,
-        [(v, whole(*v.shape)) for v in parts] + [(right, whole(*right.shape))],
-        [block(width), block(depth)],
+        ins + [(right, whole(*right.shape))],
+        [block(width), block(depth)] + [(sds((4, MARK, w), BF16), each(MARK, w)) for w in last],
         [],
         2.7,
         held,
@@ -825,12 +853,10 @@
     forward_chain = [None] * micro
 
     def project(m, *others):
-        proj, normed_all[m] = gathered_times(normed_parts[m], w_mix, nn, held(*others))
+        proj, normed_all[m], tail = gathered_times(normed_parts[m], w_mix, nn, held(*others), last=(xbc,))
         ran(proj)
-        tail = proj.reshape(reps, length, cols)[:, length - (KCONV - 1) :, :xbc]
         halo = lax.ppermute(tail, "seq", [(i, i + 1) for i in range(pieces - 1)])
-        halo = jnp.pad(halo.astype(F32), ((0, 0), (PAD - (KCONV - 1), 0), (0, 0)))
-        proj_in[m], halo_in[m] = (proj, row_spec(cols)), (halo, each(PAD, xbc))
+        proj_in[m], halo_in[m] = (proj, row_spec(cols)), (halo, each(MARK, xbc))
 
     def front(m, *others):
         x, bc, sl, part, message, fade = call(
@@ -864,7 +890,7 @@
         gate_in[m] = wide(ran(rows_times(normed_all[m], w_gate, nn, length, held(*others))))
 
     def grad_of(m, *others):
-        grad, cot_all[m] = gathered_times(later(cot_parts[m]), w_out, nt, held(*others))
+        grad, cot_all[m] = gathered_times(cot_blocks, w_out, nt, held(*others), m)
         grad_in[m] = wide(ran(grad))
 
     def gating(m, *others):
@@ -893,21 +919,15 @@
     far.append(to_far(near[1]))
     normed_parts.append(far_parts(near[1], far[1]))
     front(0, *far[1])
-    cot_near = [gather_near(after(masked[0], *line))]
-    project(1, cot_near[0][0])
+    cot_blocks = gather_direct(after(masked, *line))
+    project(1, cot_blocks[0])
     front(1, forward_chain[0].hop())
     gate_of(0)
-    cot_near[0] = later(cot_near[0])
-    cot_far = [to_far(cot_near[0])]
-    cot_near.append(gather_near(after(masked[1], *line, *cot_far[0])))
-    cot_parts = [far_parts(cot_near[0], cot_far[0])]
-    within(0, forward_chain[0].hop(), forward_chain[1].hop(), cot_near[1][0])
+    within(0, forward_chain[0].hop(), forward_chain[1].hop())
     gate_of(1)
     within(1, forward_chain[0].hop(), forward_chain[1].hop())
-    cot_near[1] = later(cot_near[1])
-    cot_far.append(to_far(cot_near[1]))
-    cot_parts.append(far_parts(cot_near[1], cot_far[1]))
-    grad_of(0, *cot_far[1])
+    cot_blocks = later(cot_blocks)
+    grad_of(0)
     forward_chain[0].rest()
     grad_of(1, forward_chain[0].back(), forward_chain[1].hop())
     forward_chain[1].rest()
@@ -992,7 +1012,7 @@
             + [(normed_all[m], row_spec(model))],
             [(sds((length, model), BF16), whole(length, model))] * reps + [(sds((PAD, model), F32), whole(PAD, model))],
             [],
-            40.0,
+            80.0 if m == 0 else 0.1,
             held(*others),
         )
         pre_parts[m] = ran(pre)[0]
@@ -1004,25 +1024,21 @@
     def over_seq(parts):
         return lax.psum_scatter(parts, "seq", scatter_dimension=0, tiled=True)
 
-    def project_out(m, *others):
-        blocks = call(
-            branch_kernel,
-            reps,
-            [wide(gated[m]), (w_out, whole(*w_out.shape))],
-            [(sds((length, model), BF16), whole(length, model))] * reps,
-            [],
-            1.9,
-            held(*others),
-        )
-        ran(blocks[0])
-        return list(blocks[:1]) + [swap(blocks[q], "rep", q) for q in (1, 2, 3)]
-
     normalise(0)
-    branch = [project_out(0)]
-    normalise(1, backward_chain[0].hop())
-    branch.append(project_out(1))
+    normalise(1)
+    branch = call(
+        functools.partial(branch_kernel, micro),
+        reps,
+        [wide(v) for v in gated] + [(w_out, whole(*w_out.shape))],
+        [(sds((micro, length, model), BF16), whole(micro, length, model))] * reps,
+        [],
+        3.8,
+        held(backward_chain[0].hop()),
+    )
+    ran(branch[0])
+    branch = [branch[0]] + [swap(branch[q], "rep", q) for q in (1, 2, 3)]
     within_back(0, backward_chain[0].hop(), backward_chain[1].hop())
-    within_back(1, backward_chain[0].hop(), backward_chain[1].hop(), *branch[0])
+    within_back(1, backward_chain[0].hop(), backward_chain[1].hop())
     backward_chain[0].rest()
     back(0, backward_chain[0].back(), backward_chain[1].hop())
     backward_chain[1].rest()
@@ -1051,9 +1067,10 @@
             lax.dynamic_update_slice(jnp.zeros((inner, model), BF16), out_part, (rep * width, 0))
         )
     complete(0)
-    back(1)
+    back(1, *branch[1:])
     grad_through(0)
     complete(1)
+    mix_part = ran(weight_sum(normed_all, pgs, held(), 0.1))
     grad_through(1)
     gain_part, skip_part = sum(g[0] for g in gains), sum(v[0] for v in skips)
     cw_part, cb_part, sb_part, dl_part = (sum(v) for v in zip(*smalls))
@@ -1061,24 +1078,43 @@
     packed = jnp.concatenate(
         [cw_part[:KCONV].reshape(-1), cb_part[0], gain_part, lanes_of(skip_heads), sb_part[0], dl_part[0]]
     )
-    branch = [later(b) for b in branch]
-    output = jnp.stack([sum(v.astype(F32) for v in b) for b in branch])
+    mix_sums = over_seq(after(mix_part, gate_sums, out_sums, *line, *normed_grad[0]))
+    output = sum(v.astype(F32) for v in later(branch))
     output = jnp.where(valid, token_rows + output, 0.0).astype(BF16)
-    mix_part = ran(weight_sum(normed_all, pgs, held(output), 0.1))
-    mix_sums = over_seq(after(mix_part, gate_sums, out_sums, *normed_grad[0], *normed_grad[1][3:]))
     normed_grad[0] = later(normed_grad[0])
     gate_near = gather_near(gate_sums)
-    normed_grad[1] = scatter_near(*normed_grad[1][:3], *after(tuple(normed_grad[1][3:]), *line, *gate_near[1:]))
+    far_sums = after(tuple(normed_grad[1][3:]), *line)
+    normed_grad[1], sent = scatter_near(*normed_grad[1][:3], *after(far_sums, *gate_near[1:], output))
     gate_rows = far_parts(gate_near, to_far(gate_near)) if strided else gather_direct(gate_sums)
     out_rows = gate_rows if strided else gather_direct(out_sums)
     pre_part = sum(pre_parts)
-    small_sums = SmallSums(jnp.concatenate([packed, pre_part]).reshape(-1, LANES)).rest()
+    small_sums = jnp.concatenate([packed, pre_part]).reshape(-1, LANES)
+    small_sums = SmallSums(after(small_sums, *far_sums))
+    small_sums.hop()
+    small_sums.value = after(small_sums.value, *sent)
+    small_sums = small_sums.rest()
 
     normed_grad = jnp.stack([sum(v.astype(F32) for v in n) for n in normed_grad])
     xhat = token_rows * inverse
     scaled = normed_grad * pre_gain
     rows_grad = inverse * (scaled - xhat * jnp.mean(scaled * xhat, axis=-1, keepdims=True))
     tokens_grad = jnp.where(valid, cotangent.astype(F32), 0.0) + rows_grad
+
+
+    ready = tuple(gate_rows) + (small_sums, tokens_grad)
+    if strided:
+        mix_near = gather_near(after(mix_sums, *ready))
+        mix_far = to_far(mix_near)
+        mix_rows = far_parts(mix_near, mix_far)
+    else:
+        mix_rows = gather_direct(mix_sums)
+        mix_far = mix_rows[1:]
+    gate_rows = list(after(tuple(gate_rows), *mix_far))
+    out_rows = gate_rows if strided else out_rows
+    small_sums = after(small_sums, *mix_far)
+    both_packed = jnp.stack([small_sums, swap(small_sums, "rep", 1)])
+    far_packed = swap(both_packed, "rep", 2)
+    packed = [both_packed[0], both_packed[1], far_packed[0], far_packed[1]]
 
     rep_scalar = rep.astype(jnp.int32).reshape(1)
     place_in = (rep_scalar, pl.BlockSpec(memory_space=pltpu.SMEM))
@@ -1094,7 +1130,6 @@
         sds(in_weight.shape[::-1], F32),
         pl.BlockSpec((reps * unit, k_rows), lambda i: (i + first, 0)),
     )
-    finished = []
     if strided:
         (out_weight_grad,) = call(
             functools.partial(out_grad_kernel, k_rows),
@@ -1112,11 +1147,6 @@
             [],
             0.8,
         )
-        finished = [out_weight_grad, gate_done]
-    mix_rows = (gather_halves if strided else gather_direct)(after(mix_sums, tokens_grad, *finished))
-    both_packed = jnp.stack([small_sums, swap(small_sums, "rep", 1)])
-    far_packed = swap(both_packed, "rep", 2)
-    packed = [both_packed[0], both_packed[1], far_packed[0], far_packed[1]]
     if strided:
         (in_weight_grad,) = call(
             functools.partial(mix_grad_kernel, groups, heads),

time: 690 us -> 669 us (0.970)
  Pallas kernels: 339 us -> 304 us
  waiting for transfers between devices: 87.1 us -> 115 us
  other arithmetic: 79.6 us -> 66.7 us
    pallas_call x28 -> x27, Pallas kernels: 339 us -> 304 us  [call(): pl.pallas_call(kernel, grid=(slots,), in_specs=[s for _, s in ins], out_s...]
    unnamed x137 -> x229, local copies, waits for them, and re-layouts: 7.58 us -> 27.8 us
    ppermute x48 -> x40, waiting for transfers between devices: 73.3 us -> 90.1 us  [swap(): lax.ppermute(value, axis, [(i, i ^ bit) for i in range(lax.axis_size(axis...]
    ppermute x4, waiting for transfers between devices: 0.01 us -> 7.33 us  [__init__(): lax.ppermute(message, 'seq', [(2 * c + first, 2 * c + lead) for c in chips])]
    ppermute x48 -> x40, starting transfers between devices: 62.2 us -> 58 us  [swap(): lax.ppermute(value, axis, [(i, i ^ bit) for i in range(lax.axis_size(axis...]
  transfers between devices with their start and end apart: 77 -> 69, of which waited for: 18 -> 21; matrix products, arithmetic and copies ran while one was open for 16% -> 12% of each run, Pallas kernels for 48% -> 44%
where the time goes in v3:
time: 669 us; the launch traced here: 656 us
  Pallas kernels  304 us (45%)
  waiting for transfers between devices  115 us (17%)
  starting transfers between devices  105 us (16%)
  other arithmetic  66.7 us (10%)
  local copies, waits for them, and re-layouts  49.8 us (7%)
  between operations  15.9 us (2%)
    pallas_call x27, Pallas kernels, call(): pl.pallas_call(kernel, grid=(slots,), in_specs=[s for _, s in ins], out_s...  304 us
    ppermute x40, waiting for transfers between devices, swap(): lax.ppermute(value, axis, [(i, i ^ bit) for i in range(lax.axis_size(axis...  90.1 us
    ppermute x40, starting transfers between devices, swap(): lax.ppermute(value, axis, [(i, i ^ bit) for i in range(lax.axis_size(axis...  58 us
    unnamed x229, local copies, waits for them, and re-layouts  27.8 us
    convert_element_type x8, other arithmetic, hop(): (self.total.astype(F32) + self.total_fade * self.enters.astype(F32)).asty...  19.1 us
    ppermute x4, starting transfers between devices, __init__(): lax.ppermute(message, 'seq', [(2 * c + first, 2 * c + lead) for c in chips])  16.2 us
    ppermute x12, starting transfers between devices, hop(): self.enters = self.enters + lax.ppermute(onto, 'seq', [self.onward.pop(0)])  14.5 us
  transfers between devices with their start and end apart: 69, of which 21 were waited for; matrix products, arithmetic and copies ran while one was open for 12% of the time, Pallas kernels for 44%

profile of v3, /device:TPU:0, one launch (start us, length us, event | category | flops | bytes accessed | tf_op | source)
XLA Modules:
  0.0 656.0 jit_solution(15986708339544660851)
XLA Ops:
  27.8 20.4 %collective-permute-done.2.refs_2_ = bf16[256,2048]{1,0:T(8,128)(2,1)} collective-permute-done((bf16[256,2048]{1,0:T(8,128)(2,1)}, bf16[256,2048]{1,0:T(8,128)(2,1)}, u32[]{:S(2)}, u32[]{:S(2)}) %collective-permute-start.2) | collective-permute-done | bytes 1048608 | tf_op jit(solution)/shard_map/ppermute | solution.py:26
  67.5 12.2 %all-gather.4.cloned.1.call-done.refs_5_.w_mix = bf16[2048,1408]{1,0:T(8,128)(2,1)} async-done(((bf16[256,1408]{1,0:T(8,128)(2,1)}), bf16[2048,1408]{1,0:T(8,128)(2,1)}) %all-gather.4.cloned.1.call-update) | async-done | bytes 5767184 | tf_op jit(solution)/shard_map/all_gather | solution.py:794
  81.8 12.1 %shard_map.203 = (bf16[1024,1408]{1,0:T(8,128)(2,1)}, bf16[1024,2048]{1,0:T(8,128)(2,1)}, bf16[4,16,1280]{2,1,0:T(8,128)(2,1)}) custom-call(bf16[256,2048]{1,0:T(8,128)(2,1)} %get-tuple-element.145.refs_0_, bf16[256,2048]{1,0:T(8,128)(2,1)} %collective-permute-done.refs_1_, bf16[256,2048]{1,0:T(8,128)(2,1)} %collective-permute-done.2.refs_2_, ...), custom_call_target="tpu_custom_call" | custom-call | flops 11879999488 | bytes 10800000 | tf_op jit(solution)/shard_map/pallas_call | solution.py:672
  102.6 8.7 %shard_map.204 = (f32[1024,1024]{1,0:T(8,128)}, bf16[1024,512]{1,0:T(8,128)(2,1)S(1)}, f32[1024,256]{1,0:T(8,128)S(1)}, f32[4,128,1024]{2,1,0:T(8,128)S(1)}, bf1...) custom-call(bf16[1024,1408]{1,0:T(8,128)(2,1)} %get-tuple-element.210.proj, ...), custom_call_target="tpu_custom_call" | custom-call | flops 10119999488 | bytes 9200000 | tf_op jit(solution)/shard_map/pallas_call | solution.py:672
  119.1 11.8 %shard_map.205 = (bf16[1024,1408]{1,0:T(8,128)(2,1)}, bf16[1024,2048]{1,0:T(8,128)(2,1)}, bf16[4,16,1280]{2,1,0:T(8,128)(2,1)S(1)}) custom-call(bf16[256,2048]{1,0:T(8,128)(2,1)S(1)} %get-tuple-element.156.refs_0_, bf16[256,2048]{1,0:T(8,128)(2,1)} %collective-permute-done.4.refs_1_, bf16[256,2048]{1,0:T(8,128)(2,1)} %collective-permute-done.5.refs_2_, ...), custom_call_target="tpu_custom_call" | custom-call | flops 11879999488 | bytes 10800000 | tf_op jit(solution)/shard_map/pallas_call | solution.py:672
  135.3 8.9 %shard_map.206 = (f32[1024,1024]{1,0:T(8,128)}, bf16[1024,512]{1,0:T(8,128)(2,1)S(1)}, f32[1024,256]{1,0:T(8,128)S(1)}, f32[4,128,1024]{2,1,0:T(8,128)S(1)}, bf1...) custom-call(bf16[1024,1408]{1,0:T(8,128)(2,1)} %get-tuple-element.218.proj, ...), custom_call_target="tpu_custom_call" | custom-call | flops 10119999488 | bytes 9200000 | tf_op jit(solution)/shard_map/pallas_call | solution.py:672
  147.6 12.1 %collective-permute-start.12 = (bf16[4,144,1024]{2,1,0:T(8,128)(2,1)}, bf16[4,144,1024]{2,1,0:T(8,128)(2,1)}, u32[]{:S(2)}, u32[]{:S(2)}) collective-permute-start(bf16[4,144,1024]{2,1,0:T(8,128)(2,1)} %get-tuple-element.165), channel_id=1, source_target_pairs={{0,1},{2,3},{4,5},{6,7},{8,9},{10,11},{12,13},{14,15},{16,17},{18,... | collective-permute-start | bytes 3538952 | tf_op jit(solution)/shard_map/ppermute | solution.py:121
  173.5 9.9 %shard_map.208.y = f32[1024,1024]{1,0:T(8,128)} custom-call(f32[1024,1024]{1,0:T(8,128)} %get-tuple-element.204.x, bf16[1024,512]{1,0:T(8,128)(2,1)S(1)} %copy-done.70, f32[1024,256]{1,0:T(8,128)S(1)} %copy-done.74, bf16[128,1024]{1,0:T(8,128)(2,1)S(1)} %and_convert_fusion.spread), custom_call_target="tpu_custom_call" | custom-call | flops 9680000000 | bytes 8800000 | tf_op jit(solution)/shard_map/pallas_call | solution.py:672
  201.3 9.9 %shard_map.210.y = f32[1024,1024]{1,0:T(8,128)} custom-call(f32[1024,1024]{1,0:T(8,128)} %get-tuple-element.207.x, bf16[1024,512]{1,0:T(8,128)(2,1)S(1)} %copy-done.60, f32[1024,256]{1,0:T(8,128)S(1)} %copy-done.65, bf16[128,1024]{1,0:T(8,128)(2,1)S(1)} %and_convert_fusion.spread), custom_call_target="tpu_custom_call" | custom-call | flops 9680000000 | bytes 8800000 | tf_op jit(solution)/shard_map/pallas_call | solution.py:672
  211.3 8.7 %shard_map.211 = (bf16[1024,1024]{1,0:T(8,128)(2,1)S(1)}, bf16[1024,2048]{1,0:T(8,128)(2,1)}) custom-call(bf16[2,256,2048]{2,1,0:T(8,128)(2,1)S(1)} %broadcast_select_fusion.refs_0_, bf16[2,256,2048]{2,1,0:T(8,128)(2,1)} %collective-permute-done.13.refs_1_, bf16[2,256,2048]{2,1,0:T(8,128)(2,1)} %collective-permute-done.14.refs_2_, ...), custom_call_target="tpu_custom_call" | custom-call | flops 11879999488 | bytes 10800000 | tf_op jit(solution)/shard_map/pallas_call | solution.py:672
  228.2 8.8 %shard_map.212 = (bf16[1024,1024]{1,0:T(8,128)(2,1)S(1)}, bf16[1024,2048]{1,0:T(8,128)(2,1)}) custom-call(bf16[2,256,2048]{2,1,0:T(8,128)(2,1)S(1)} %broadcast_select_fusion.refs_0_, bf16[2,256,2048]{2,1,0:T(8,128)(2,1)} %collective-permute-done.13.refs_1_, bf16[2,256,2048]{2,1,0:T(8,128)(2,1)} %collective-permute-done.14.refs_2_, ...), custom_call_target="tpu_custom_call" | custom-call | flops 11879999488 | bytes 10800000 | tf_op jit(solution)/shard_map/pallas_call | solution.py:672
  271.3 10.4 %shard_map.215 = (bf16[1024,1024]{1,0:T(8,128)(2,1)S(1)}, bf16[1024,1024]{1,0:T(8,128)(2,1)}, bf16[1024,1024]{1,0:T(8,128)(2,1)}, f32[4,128,1024]{2,1,0:T(8,128)...) custom-call(f32[1024,1024]{1,0:T(8,128)} %get-tuple-element.188.y, ...), custom_call_target="tpu_custom_call" | custom-call | flops 13639999488 | bytes 12400000 | tf_op jit(solution)/shard_map/pallas_call | solution.py:672
  283.2 10.9 %shard_map.216 = (bf16[1024,1024]{1,0:T(8,128)(2,1)S(1)}, bf16[1024,1024]{1,0:T(8,128)(2,1)}, bf16[1024,1024]{1,0:T(8,128)(2,1)}, f32[4,128,1024]{2,1,0:T(8,128)...) custom-call(f32[1024,1024]{1,0:T(8,128)} %get-tuple-element.192.y, ...), custom_call_target="tpu_custom_call" | custom-call | flops 13639999488 | bytes 12400000 | tf_op jit(solution)/shard_map/pallas_call | solution.py:672
  313.0 15.4 %shard_map.217 = (bf16[2,256,2048]{2,1,0:T(8,128)(2,1)S(1)}, bf16[2,256,2048]{2,1,0:T(8,128)(2,1)}, bf16[2,256,2048]{2,1,0:T(8,128)(2,1)}, bf16[2,256,2048]{2,1,0:T(8,128)(2,1)}) custom-call(bf16[1024,1024]{1,0:T(8,128)(2,1)} %copy-done.78, bf16[1024,1024]{1,0:T(8,128)(2,1)} %copy-done.79, bf16[1024,2048]{1,0:T(8,128)(2,1)} %all-gather.8.cloned.1.call-done.refs_4_.refs_2_), custom_call_target="tpu_custom_call" | custom-call | flops 16720000000 | bytes 15200000 | tf_op jit(solution)/shard_map/pallas_call | solution.py:672
  338.9 13.4 %shard_map.218 = (f32[1024,1024]{1,0:T(8,128)}, f32[1024,256]{1,0:T(8,128)S(1)}) custom-call(f32[1024,1024]{1,0:T(8,128)} %get-tuple-element.204.x, bf16[1024,512]{1,0:T(8,128)(2,1)S(1)} %copy-done.72, f32[1024,256]{1,0:T(8,128)S(1)} %copy-done.76, bf16[1024,1024]{1,0:T(8,128)(2,1)} %get-tuple-element.205.dy, bf16[4,128,1024]{2,1,0:T(8,128)(2,1)S(1)} %fusion.35.start, ...), custom_call_target="tpu_custom_call" | custom-call | flops 15840000000 | bytes 14400000 | tf_op jit(solution)/shard_map/pallas_call | solution.py:672
  359.4 13.3 %shard_map.219 = (f32[1024,1024]{1,0:T(8,128)}, f32[1024,256]{1,0:T(8,128)S(1)}) custom-call(f32[1024,1024]{1,0:T(8,128)} %get-tuple-element.207.x, bf16[1024,512]{1,0:T(8,128)(2,1)S(1)} %copy-done.62, f32[1024,256]{1,0:T(8,128)S(1)} %copy-done.67, bf16[1024,1024]{1,0:T(8,128)(2,1)} %get-tuple-element.208.dy, bf16[4,128,1024]{2,1,0:T(8,128)(2,1)S(1)} %fusion.34.start, ...), custom_call_target="tpu_custom_call" | custom-call | flops 15840000000 | bytes 14400000 | tf_op jit(solution)/shard_map/pallas_call | solution.py:672
  380.5 20.4 %shard_map.220 = (bf16[1024,1408]{1,0:T(8,128)(2,1)}, f32[4,8,1280]{2,1,0:T(8,128)S(1)}, f32[4,8,1280]{2,1,0:T(8,128)S(1)}, f32[8,1280]{1,0:T(8,128)S(1)}, f32[8...) custom-call(bf16[1024,1408]{1,0:T(8,128)(2,1)} %get-tuple-element.210.proj, ...), custom_call_target="tpu_custom_call" | custom-call | flops 22439999488 | bytes 20400000 | tf_op jit(solution)/shard_map/pallas_call | solution.py:672
  400.9 24.4 %shard_map.221 = bf16[8,512,1024]{2,1,0:T(8,128)(2,1)} custom-call(bf16[1024,2048]{1,0:T(8,128)(2,1)} %get-tuple-element.231.left.refs_0_.normed, bf16[1024,2048]{1,0:T(8,128)(2,1)} %get-tuple-element.171.left.refs_1_.normed, bf16[1024,1024]{1,0:T(8,128)(2,1)S(1)} %copy-done.77, bf16[1024,1024]{1,0:T(8,128)(2,1)S(1)} %copy-done.7, ...), custom_call_target="tpu_custom_call" | custom-call | flops 28160000000 | bytes 25600000 | tf_op jit(solution)/shard_map/pallas_call | solution.py:672
  430.1 20.3 %shard_map.222 = (bf16[1024,1408]{1,0:T(8,128)(2,1)}, f32[4,8,1280]{2,1,0:T(8,128)S(1)}, f32[4,8,1280]{2,1,0:T(8,128)S(1)}, f32[8,1280]{1,0:T(8,128)S(1)}, f32[8...) custom-call(bf16[1024,1408]{1,0:T(8,128)(2,1)} %get-tuple-element.218.proj, ...), custom_call_target="tpu_custom_call" | custom-call | flops 22439999488 | bytes 20400000 | tf_op jit(solution)/shard_map/pallas_call | solution.py:672
  452.9 18.8 %shard_map.223 = (bf16[256,2048]{1,0:T(8,128)(2,1)S(1)}, bf16[256,2048]{1,0:T(8,128)(2,1)}, bf16[256,2048]{1,0:T(8,128)(2,1)}, bf16[256,2048]{1,0:T(8,128)(2,1)}, f32[8,2048]{1,0:T(8,128)S(1)}) custom-call(bf16[1024,1408]{1,0:T(8,128)(2,1)} %bitcast.97, bf16[1024,1024]{1,0:T(8,128)(2,1)} %get-tuple-element.214.refs_2_.gate, ...), custom_call_target="tpu_custom_call" | custom-call | flops 352000016384 | bytes 320000000 | tf_op jit(solution)/shard_map/pallas_call | solution.py:672
  484.0 16.8 %shard_map.224 = bf16[2048,1408]{1,0:T(8,128)(2,1)} custom-call(bf16[1024,2048]{1,0:T(8,128)(2,1)} %get-tuple-element.231.left.refs_0_.normed, bf16[1024,2048]{1,0:T(8,128)(2,1)} %get-tuple-element.171.left.refs_1_.normed, bf16[1024,1408]{1,0:T(8,128)(2,1)S(1)} %bitcast.98, bf16[1024,1408]{1,0:T(8,128)(2,1)S(1)} %bitcast.94), custom_call_target="tpu_custom_call" | custom-call | flops 880000000 | bytes 800000 | tf_op jit(solution)/shard_map/pallas_call | solution.py:672
  500.8 17.1 %shard_map.225 = (bf16[256,2048]{1,0:T(8,128)(2,1)S(1)}, bf16[256,2048]{1,0:T(8,128)(2,1)S(1)}, bf16[256,2048]{1,0:T(8,128)(2,1)S(1)}, bf16[256,2048]{1,0:T(8,128)(2,1)S(1)}, f32[8,2048]{1,0:T(8,128)S(1)}) custom-call(bf16[1024,1408]{1,0:T(8,128)(2,1)} %bitcast.95, bf16[1024,1024]{1,0:T(8,128)(2,1)} %get-tuple-element.215.refs_3_.gate, ...), custom_call_target="tpu_custom_call" | custom-call | flops 440000000 | bytes 400000 | tf_op jit(solution)/shard_map/pallas_call | solution.py:672
  537.4 22.1 %collective-permute-done.48 = bf16[128,2048]{1,0:T(8,128)(2,1)S(1)} collective-permute-done((bf16[128,2048]{1,0:T(8,128)(2,1)S(1)}, bf16[128,2048]{1,0:T(8,128)(2,1)S(1)}, u32[]{:S(2)}, u32[]{:S(2)}) %collective-permute-start.48) | collective-permute-done | bytes 524320 | tf_op jit(solution)/shard_map/ppermute | solution.py:26
  604.5 15.0 %collective-permute-done.59.m2 = bf16[256,1408]{1,0:T(8,128)(2,1)S(1)} collective-permute-done((bf16[256,1408]{1,0:T(8,128)(2,1)}, bf16[256,1408]{1,0:T(8,128)(2,1)S(1)}, u32[]{:S(2)}, u32[]{:S(2)}) %collective-permute-start.59) | collective-permute-done | bytes 720928 | tf_op jit(solution)/shard_map/ppermute | solution.py:26
  (512 shorter events, 298.5 us)
Async XLA Ops:
  7.2 72.6 %all-gather.4.cloned.1.call-start = ((), (), s32[]{:S(2)}) async-start(), calls=%async_computation.2 | async-start | bytes 6488064 | tf_op jit(solution)/shard_map/all_gather | solution.py:794
  16.5 143.3 %all-gather.6.cloned.1.call-start = ((), (), s32[]{:S(2)}) async-start(), calls=%async_computation.3 | async-start | bytes 4718592 | tf_op jit(solution)/shard_map/all_gather | solution.py:795
  17.6 193.7 %all-gather.8.cloned.1.call-start = ((), (), s32[]{:S(2)}) async-start(), calls=%async_computation.4 | async-start | bytes 4718592 | tf_op jit(solution)/shard_map/all_gather | solution.py:799
  21.7 26.4 %collective-permute-start.2 = (bf16[256,2048]{1,0:T(8,128)(2,1)}, bf16[256,2048]{1,0:T(8,128)(2,1)}, u32[]{:S(2)}, u32[]{:S(2)}) collective-permute-start(bf16[256,2048]{1,0:T(8,128)(2,1)} %get-tuple-element.145.refs_0_), channel_id=1, source_target_pairs={{0,16},{8,24},{16,0},{24,8},{1,17},{9,25},{17,1},{25,9},{2,18},{10... | collective-permute-start | bytes 3145736 | tf_op jit(solution)/shard_map/ppermute | solution.py:26
  24.7 26.3 %collective-permute-start = (bf16[256,2048]{1,0:T(8,128)(2,1)}, bf16[256,2048]{1,0:T(8,128)(2,1)}, u32[]{:S(2)}, u32[]{:S(2)}) collective-permute-start(bf16[256,2048]{1,0:T(8,128)(2,1)} %get-tuple-element.145.refs_0_), channel_id=1, source_target_pairs={{0,8},{8,0},{16,24},{24,16},{1,9},{9,1},{17,25},{25,17},{2,10},{10... | collective-permute-start | bytes 3145736 | tf_op jit(solution)/shard_map/ppermute | solution.py:26
  27.0 495.1 %reduce-scatter.3.cloned.1.call-start = ((), (), s32[]{:S(2)}) async-start(), calls=%async_computation.5 | async-start | bytes 9437184 | tf_op jit(solution)/shard_map/reduce_scatter | solution.py:1025
  65.5 31.9 %collective-permute-start.5 = (bf16[256,2048]{1,0:T(8,128)(2,1)S(1)}, bf16[256,2048]{1,0:T(8,128)(2,1)}, u32[]{:S(2)}, u32[]{:S(2)}) collective-permute-start(bf16[256,2048]{1,0:T(8,128)(2,1)S(1)} %get-tuple-element.156.refs_0_), channel_id=1, source_target_pairs={{0,16},{8,24},{16,0},{24,8},{1,17},{9,25},{17,1},{25,9},{2,18},{10... | collective-permute-start | bytes 3145736 | tf_op jit(solution)/shard_map/ppermute | solution.py:26
  67.0 30.4 %collective-permute-start.4 = (bf16[256,2048]{1,0:T(8,128)(2,1)S(1)}, bf16[256,2048]{1,0:T(8,128)(2,1)}, u32[]{:S(2)}, u32[]{:S(2)}) collective-permute-start(bf16[256,2048]{1,0:T(8,128)(2,1)S(1)} %get-tuple-element.156.refs_0_), channel_id=1, source_target_pairs={{0,8},{8,0},{16,24},{24,16},{1,9},{9,1},{17,25},{25,17},{2,10},{10... | collective-permute-start | bytes 3145736 | tf_op jit(solution)/shard_map/ppermute | solution.py:26
  115.6 95.7 %collective-permute-start.15 = (bf16[2,256,2048]{2,1,0:T(8,128)(2,1)S(1)}, bf16[2,256,2048]{2,1,0:T(8,128)(2,1)}, u32[]{:S(2)}, u32[]{:S(2)}) collective-permute-start(bf16[2,256,2048]{2,1,0:T(8,128)(2,1)S(1)} %broadcast_select_fusion.refs_0_), channel_id=1, source_target_pairs={{0,24},{8,16},{16,8},{24,0},{1,25},{9,17},{17,9},{25,1},{2,26},{10... | collective-permute-start | bytes 6291464 | tf_op jit(solution)/shard_map/ppermute | solution.py:26
  118.0 93.2 %collective-permute-start.14 = (bf16[2,256,2048]{2,1,0:T(8,128)(2,1)S(1)}, bf16[2,256,2048]{2,1,0:T(8,128)(2,1)}, u32[]{:S(2)}, u32[]{:S(2)}) collective-permute-start(bf16[2,256,2048]{2,1,0:T(8,128)(2,1)S(1)} %broadcast_select_fusion.refs_0_), channel_id=1, source_target_pairs={{0,16},{8,24},{16,0},{24,8},{1,17},{9,25},{17,1},{25,9},{2,18},{10... | collective-permute-start | bytes 6291464 | tf_op jit(solution)/shard_map/ppermute | solution.py:26
  118.6 92.7 %collective-permute-start.13 = (bf16[2,256,2048]{2,1,0:T(8,128)(2,1)S(1)}, bf16[2,256,2048]{2,1,0:T(8,128)(2,1)}, u32[]{:S(2)}, u32[]{:S(2)}) collective-permute-start(bf16[2,256,2048]{2,1,0:T(8,128)(2,1)S(1)} %broadcast_select_fusion.refs_0_), channel_id=1, source_target_pairs={{0,8},{8,0},{16,24},{24,16},{1,9},{9,1},{17,25},{25,17},{2,10},{10... | collective-permute-start | bytes 6291464 | tf_op jit(solution)/shard_map/ppermute | solution.py:26
  133.6 33.8 %collective-permute-start.11 = (bf16[4,128,1024]{2,1,0:T(8,128)(2,1)}, bf16[4,128,1024]{2,1,0:T(8,128)(2,1)}, u32[]{:S(2)}, u32[]{:S(2)}) collective-permute-start(bf16[4,128,1024]{2,1,0:T(8,128)(2,1)} %fusion.12), channel_id=1, source_target_pairs={{1,3},{9,11},{17,19},{25,27}} | collective-permute-start | bytes 3145736 | tf_op jit(solution)/shard_map/ppermute | solution.py:134
  328.4 97.0 %collective-permute-start.30 = (bf16[2,256,2048]{2,1,0:T(8,128)(2,1)}, bf16[2,256,2048]{2,1,0:T(8,128)(2,1)}, u32[]{:S(2)}, u32[]{:S(2)}) collective-permute-start(bf16[2,256,2048]{2,1,0:T(8,128)(2,1)} %get-tuple-element.199), channel_id=1, source_target_pairs={{0,8},{8,0},{16,24},{24,16},{1,9},{9,1},{17,25},{25,17},{2,10},{10... | collective-permute-start | bytes 6291464 | tf_op jit(solution)/shard_map/ppermute | solution.py:26
  329.0 96.4 %collective-permute-start.31 = (bf16[2,256,2048]{2,1,0:T(8,128)(2,1)}, bf16[2,256,2048]{2,1,0:T(8,128)(2,1)}, u32[]{:S(2)}, u32[]{:S(2)}) collective-permute-start(bf16[2,256,2048]{2,1,0:T(8,128)(2,1)} %get-tuple-element.200), channel_id=1, source_target_pairs={{0,16},{8,24},{16,0},{24,8},{1,17},{9,25},{17,1},{25,9},{2,18},{10... | collective-permute-start | bytes 6291464 | tf_op jit(solution)/shard_map/ppermute | solution.py:26
  330.5 94.9 %collective-permute-start.32 = (bf16[2,256,2048]{2,1,0:T(8,128)(2,1)}, bf16[2,256,2048]{2,1,0:T(8,128)(2,1)}, u32[]{:S(2)}, u32[]{:S(2)}) collective-permute-start(bf16[2,256,2048]{2,1,0:T(8,128)(2,1)} %get-tuple-element.201), channel_id=1, source_target_pairs={{0,24},{8,16},{16,8},{24,0},{1,25},{9,17},{17,9},{25,1},{2,26},{10... | collective-permute-start | bytes 6291464 | tf_op jit(solution)/shard_map/ppermute | solution.py:26
  376.1 50.6 %collective-permute-start.41 = (bf16[4,128,1024]{2,1,0:T(8,128)(2,1)}, bf16[4,128,1024]{2,1,0:T(8,128)(2,1)}, u32[]{:S(2)}, u32[]{:S(2)}) collective-permute-start(bf16[4,128,1024]{2,1,0:T(8,128)(2,1)} %add.393), channel_id=1, source_target_pairs={{0,1},{2,3},{4,5},{6,7},{8,9},{10,11},{12,13},{14,15},{16,17},{18,... | collective-permute-start | bytes 3145736 | tf_op jit(solution)/shard_map/ppermute | solution.py:142
  425.3 174.9 %reduce-scatter.5.cloned.1.call-start = ((), (), s32[]{:S(2)}) async-start(), calls=%async_computation.6 | async-start | bytes 6488064 | tf_op jit(solution)/shard_map/reduce_scatter | solution.py:1025
  472.7 46.1 %collective-permute-start.44 = (bf16[256,2048]{1,0:T(8,128)(2,1)}, bf16[256,2048]{1,0:T(8,128)(2,1)}, u32[]{:S(2)}, u32[]{:S(2)}) collective-permute-start(bf16[256,2048]{1,0:T(8,128)(2,1)} %get-tuple-element.239), channel_id=1, source_target_pairs={{0,8},{8,0},{16,24},{24,16},{1,9},{9,1},{17,25},{25,17},{2,10},{10... | collective-permute-start | bytes 3145736 | tf_op jit(solution)/shard_map/ppermute | solution.py:26
  473.4 47.5 %collective-permute-start.45 = (bf16[256,2048]{1,0:T(8,128)(2,1)}, bf16[256,2048]{1,0:T(8,128)(2,1)}, u32[]{:S(2)}, u32[]{:S(2)}) collective-permute-start(bf16[256,2048]{1,0:T(8,128)(2,1)} %get-tuple-element.240), channel_id=1, source_target_pairs={{0,16},{8,24},{16,0},{24,8},{1,17},{9,25},{17,1},{25,9},{2,18},{10... | collective-permute-start | bytes 3145736 | tf_op jit(solution)/shard_map/ppermute | solution.py:26
  474.9 47.2 %collective-permute-start.46 = (bf16[256,2048]{1,0:T(8,128)(2,1)}, bf16[256,2048]{1,0:T(8,128)(2,1)}, u32[]{:S(2)}, u32[]{:S(2)}) collective-permute-start(bf16[256,2048]{1,0:T(8,128)(2,1)} %get-tuple-element.241), channel_id=1, source_target_pairs={{0,24},{8,16},{16,8},{24,0},{1,25},{9,17},{17,9},{25,1},{2,26},{10... | collective-permute-start | bytes 3145736 | tf_op jit(solution)/shard_map/ppermute | solution.py:26
  525.2 35.8 %collective-permute-start.50 = (bf16[512,1024]{1,0:T(8,128)(2,1)S(1)}, bf16[512,1024]{1,0:T(8,128)(2,1)S(1)}, u32[]{:S(2)}, u32[]{:S(2)}) collective-permute-start(bf16[512,1024]{1,0:T(8,128)(2,1)S(1)} %bitcast.102), channel_id=1, source_target_pairs={{0,16},{8,24},{16,0},{24,8},{1,17},{9,25},{17,1},{25,9},{2,18},{10... | collective-permute-start | bytes 3145736 | tf_op jit(solution)/shard_map/ppermute | solution.py:26
  526.6 34.4 %collective-permute-start.49 = (bf16[512,1024]{1,0:T(8,128)(2,1)S(1)}, bf16[512,1024]{1,0:T(8,128)(2,1)S(1)}, u32[]{:S(2)}, u32[]{:S(2)}) collective-permute-start(bf16[512,1024]{1,0:T(8,128)(2,1)S(1)} %bitcast.103), channel_id=1, source_target_pairs={{0,8},{8,0},{16,24},{24,16},{1,9},{9,1},{17,25},{25,17},{2,10},{10... | collective-permute-start | bytes 3145736 | tf_op jit(solution)/shard_map/ppermute | solution.py:26
  528.1 31.3 %collective-permute-start.48 = (bf16[128,2048]{1,0:T(8,128)(2,1)S(1)}, bf16[128,2048]{1,0:T(8,128)(2,1)S(1)}, u32[]{:S(2)}, u32[]{:S(2)}) collective-permute-start(bf16[128,2048]{1,0:T(8,128)(2,1)S(1)} %get-tuple-element.297), channel_id=1, source_target_pairs={{0,16},{8,24},{16,0},{24,8},{1,17},{9,25},{17,1},{25,9},{2,18},{10... | collective-permute-start | bytes 1572872 | tf_op jit(solution)/shard_map/ppermute | solution.py:26
  528.7 32.4 %collective-permute-start.47 = (bf16[128,2048]{1,0:T(8,128)(2,1)S(1)}, bf16[128,2048]{1,0:T(8,128)(2,1)S(1)}, u32[]{:S(2)}, u32[]{:S(2)}) collective-permute-start(bf16[128,2048]{1,0:T(8,128)(2,1)S(1)} %get-tuple-element.298), channel_id=1, source_target_pairs={{0,8},{8,0},{16,24},{24,16},{1,9},{9,1},{17,25},{25,17},{2,10},{10... | collective-permute-start | bytes 1572872 | tf_op jit(solution)/shard_map/ppermute | solution.py:26
  (156 other events, 1611.3 us)
Sparse Core Ops, SparseCore 0:
  16.6 63.1 all-gather.3
  81.3 45.8 all-gather.5
  128.8 55.2 all-gather.7
  425.4 92.5 reduce-scatter.2
  522.2 70.2 reduce-scatter.4

commit v4 on v3

--- a/solution.py
+++ b/solution.py
@@ -1019,7 +1019,7 @@
         if m == 0:
             normed_grad[m] = list(blocks[:1]) + [swap(blocks[q], "rep", q) for q in (1, 2, 3)]
         else:
-            normed_grad[m] = list(blocks[:3]) + list(scatter_far(blocks[3]))
+            normed_grad[m] = list(blocks[:3]) + list(scatter_far(after(blocks[3], *gate_near[1:])))
 
     def over_seq(parts):
         return lax.psum_scatter(parts, "seq", scatter_dimension=0, tiled=True)
@@ -1038,10 +1038,8 @@
     ran(branch[0])
     branch = [branch[0]] + [swap(branch[q], "rep", q) for q in (1, 2, 3)]
     within_back(0, backward_chain[0].hop(), backward_chain[1].hop())
-    within_back(1, backward_chain[0].hop(), backward_chain[1].hop())
+    onward = backward_chain[0].hop(), backward_chain[1].hop()
     backward_chain[0].rest()
-    back(0, backward_chain[0].back(), backward_chain[1].hop())
-    backward_chain[1].rest()
     if strided:
         k_rows, out_share = model // pieces, width // pieces
         both_rows = k_rows + out_share * model // width
@@ -1056,21 +1054,25 @@
             [(sds((pieces, both_rows, width), BF16), each(both_rows, width))],
             [],
             3.2,
-            held(backward_chain[1].back()),
+            held(*onward),
         )
         ran(both_part)
         gate_sums = out_sums = over_seq(both_part)[0]
     else:
-        gate_sums = over_seq(ran(weight_sum(normed_all, dgate, held(backward_chain[1].back()))))
+        gate_sums = over_seq(ran(weight_sum(normed_all, dgate, held(*onward))))
         out_part = ran(weight_sum(gated, cot_all, held()))
         out_sums = over_seq(
             lax.dynamic_update_slice(jnp.zeros((inner, model), BF16), out_part, (rep * width, 0))
         )
+    back(0, backward_chain[0].back())
+    within_back(1, backward_chain[1].hop())
+    backward_chain[1].rest()
     complete(0)
+    grad_through(0, backward_chain[1].back())
     back(1, *branch[1:])
-    grad_through(0)
     complete(1)
     mix_part = ran(weight_sum(normed_all, pgs, held(), 0.1))
+    gate_near = gather_near(after(gate_sums, *normed_grad[0]))
     grad_through(1)
     gain_part, skip_part = sum(g[0] for g in gains), sum(v[0] for v in skips)
     cw_part, cb_part, sb_part, dl_part = (sum(v) for v in zip(*smalls))
@@ -1078,13 +1080,12 @@
     packed = jnp.concatenate(
         [cw_part[:KCONV].reshape(-1), cb_part[0], gain_part, lanes_of(skip_heads), sb_part[0], dl_part[0]]
     )
-    mix_sums = over_seq(after(mix_part, gate_sums, out_sums, *line, *normed_grad[0]))
+    mix_sums = over_seq(after(mix_part, gate_sums, out_sums, *normed_grad[0]))
     output = sum(v.astype(F32) for v in later(branch))
     output = jnp.where(valid, token_rows + output, 0.0).astype(BF16)
     normed_grad[0] = later(normed_grad[0])
-    gate_near = gather_near(gate_sums)
     far_sums = after(tuple(normed_grad[1][3:]), *line)
-    normed_grad[1], sent = scatter_near(*normed_grad[1][:3], *after(far_sums, *gate_near[1:], output))
+    normed_grad[1], sent = scatter_near(*normed_grad[1][:3], *after(far_sums, output))
     gate_rows = far_parts(gate_near, to_far(gate_near)) if strided else gather_direct(gate_sums)
     out_rows = gate_rows if strided else gather_direct(out_sums)
     pre_part = sum(pre_parts)

time: 669 us -> 652 us (0.975)
  starting transfers between devices: 105 us -> 97.9 us
  waiting for transfers between devices: 115 us -> 108 us
    ppermute x40, starting transfers between devices: 58 us -> 51 us  [swap(): lax.ppermute(value, axis, [(i, i ^ bit) for i in range(lax.axis_size(axis...]
    unnamed x229 -> x227, local copies, waits for them, and re-layouts: 27.8 us -> 25 us
  transfers between devices with their start and end apart: 69 -> 69, of which waited for: 21 -> 21; matrix products, arithmetic and copies ran while one was open for 12% -> 12% of each run, Pallas kernels for 44% -> 46%
where the time goes in v4:
time: 652 us; the launch traced here: 641 us
  Pallas kernels  305 us (47%)
  waiting for transfers between devices  108 us (17%)
  starting transfers between devices  97.9 us (15%)
  other arithmetic  66.1 us (10%)
  local copies, waits for them, and re-layouts  47.3 us (7%)
  between operations  15.9 us (2%)
    pallas_call x27, Pallas kernels, call(): pl.pallas_call(kernel, grid=(slots,), in_specs=[s for _, s in ins], out_s...  305 us
    ppermute x40, waiting for transfers between devices, swap(): lax.ppermute(value, axis, [(i, i ^ bit) for i in range(lax.axis_size(axis...  83.6 us
    ppermute x40, starting transfers between devices, swap(): lax.ppermute(value, axis, [(i, i ^ bit) for i in range(lax.axis_size(axis...  51 us
    unnamed x227, local copies, waits for them, and re-layouts  25 us
    convert_element_type x8, other arithmetic, hop(): (self.total.astype(F32) + self.total_fade * self.enters.astype(F32)).asty...  18.6 us
    ppermute x4, starting transfers between devices, __init__(): lax.ppermute(message, 'seq', [(2 * c + first, 2 * c + lead) for c in chips])  16.3 us
    ppermute x12, starting transfers between devices, hop(): self.enters = self.enters + lax.ppermute(onto, 'seq', [self.onward.pop(0)])  14.5 us
  transfers between devices with their start and end apart: 69, of which 21 were waited for; matrix products, arithmetic and copies ran while one was open for 12% of the time, Pallas kernels for 46%

profile of v4, /device:TPU:0, one launch (start us, length us, event | category | flops | bytes accessed | tf_op | source)
XLA Modules:
  0.0 640.5 jit_solution(3474677174629163219)
XLA Ops:
  27.9 20.2 %collective-permute-done.refs_1_ = bf16[256,2048]{1,0:T(8,128)(2,1)} collective-permute-done((bf16[256,2048]{1,0:T(8,128)(2,1)}, bf16[256,2048]{1,0:T(8,128)(2,1)}, u32[]{:S(2)}, u32[]{:S(2)}) %collective-permute-start) | collective-permute-done | bytes 1048608 | tf_op jit(solution)/shard_map/ppermute | solution.py:26
  53.9 8.4 %collective-permute-done.1.refs_3_ = bf16[128,2048]{1,0:T(8,128)(2,1)S(1)} collective-permute-done((bf16[128,2048]{1,0:T(8,128)(2,1)S(1)}, bf16[128,2048]{1,0:T(8,128)(2,1)S(1)}, u32[]{:S(2)}, u32[]{:S(2)}) %collective-permute-start.1) | collective-permute-done | bytes 524320 | tf_op jit(solution)/shard_map/ppermute | solution.py:26
  67.5 12.3 %all-gather.4.cloned.1.call-done.refs_5_.w_mix = bf16[2048,1408]{1,0:T(8,128)(2,1)} async-done(((bf16[256,1408]{1,0:T(8,128)(2,1)}), bf16[2048,1408]{1,0:T(8,128)(2,1)}) %all-gather.4.cloned.1.call-update) | async-done | bytes 5767184 | tf_op jit(solution)/shard_map/all_gather | solution.py:794
  81.8 12.1 %shard_map.203 = (bf16[1024,1408]{1,0:T(8,128)(2,1)}, bf16[1024,2048]{1,0:T(8,128)(2,1)}, bf16[4,16,1280]{2,1,0:T(8,128)(2,1)}) custom-call(bf16[256,2048]{1,0:T(8,128)(2,1)} %get-tuple-element.147.refs_0_, bf16[256,2048]{1,0:T(8,128)(2,1)} %collective-permute-done.refs_1_, bf16[256,2048]{1,0:T(8,128)(2,1)} %collective-permute-done.2.refs_2_, ...), custom_call_target="tpu_custom_call" | custom-call | flops 11879999488 | bytes 10800000 | tf_op jit(solution)/shard_map/pallas_call | solution.py:672
  102.5 8.7 %shard_map.204 = (f32[1024,1024]{1,0:T(8,128)}, bf16[1024,512]{1,0:T(8,128)(2,1)S(1)}, f32[1024,256]{1,0:T(8,128)S(1)}, f32[4,128,1024]{2,1,0:T(8,128)S(1)}, bf1...) custom-call(bf16[1024,1408]{1,0:T(8,128)(2,1)} %get-tuple-element.214.proj, ...), custom_call_target="tpu_custom_call" | custom-call | flops 10119999488 | bytes 9200000 | tf_op jit(solution)/shard_map/pallas_call | solution.py:672
  119.1 11.8 %shard_map.205 = (bf16[1024,1408]{1,0:T(8,128)(2,1)}, bf16[1024,2048]{1,0:T(8,128)(2,1)}, bf16[4,16,1280]{2,1,0:T(8,128)(2,1)S(1)}) custom-call(bf16[256,2048]{1,0:T(8,128)(2,1)S(1)} %get-tuple-element.158.refs_0_, bf16[256,2048]{1,0:T(8,128)(2,1)} %collective-permute-done.4.refs_1_, bf16[256,2048]{1,0:T(8,128)(2,1)} %collective-permute-done.5.refs_2_, ...), custom_call_target="tpu_custom_call" | custom-call | flops 11879999488 | bytes 10800000 | tf_op jit(solution)/shard_map/pallas_call | solution.py:672
  135.1 8.9 %shard_map.206 = (f32[1024,1024]{1,0:T(8,128)}, bf16[1024,512]{1,0:T(8,128)(2,1)S(1)}, f32[1024,256]{1,0:T(8,128)S(1)}, f32[4,128,1024]{2,1,0:T(8,128)S(1)}, bf1...) custom-call(bf16[1024,1408]{1,0:T(8,128)(2,1)} %get-tuple-element.226.proj, ...), custom_call_target="tpu_custom_call" | custom-call | flops 10119999488 | bytes 9200000 | tf_op jit(solution)/shard_map/pallas_call | solution.py:672
  147.3 12.1 %collective-permute-start.12 = (bf16[4,144,1024]{2,1,0:T(8,128)(2,1)}, bf16[4,144,1024]{2,1,0:T(8,128)(2,1)}, u32[]{:S(2)}, u32[]{:S(2)}) collective-permute-start(bf16[4,144,1024]{2,1,0:T(8,128)(2,1)} %get-tuple-element.167), channel_id=1, source_target_pairs={{0,1},{2,3},{4,5},{6,7},{8,9},{10,11},{12,13},{14,15},{16,17},{18,... | collective-permute-start | bytes 3538952 | tf_op jit(solution)/shard_map/ppermute | solution.py:121
  173.3 9.9 %shard_map.208.y = f32[1024,1024]{1,0:T(8,128)} custom-call(f32[1024,1024]{1,0:T(8,128)} %get-tuple-element.206.x, bf16[1024,512]{1,0:T(8,128)(2,1)S(1)} %copy-done.65, f32[1024,256]{1,0:T(8,128)S(1)} %copy-done.70, bf16[128,1024]{1,0:T(8,128)(2,1)S(1)} %and_convert_fusion.spread), custom_call_target="tpu_custom_call" | custom-call | flops 9680000000 | bytes 8800000 | tf_op jit(solution)/shard_map/pallas_call | solution.py:672
  201.1 9.9 %shard_map.210.y = f32[1024,1024]{1,0:T(8,128)} custom-call(f32[1024,1024]{1,0:T(8,128)} %get-tuple-element.220.x, bf16[1024,512]{1,0:T(8,128)(2,1)S(1)} %copy-done.55, f32[1024,256]{1,0:T(8,128)S(1)} %copy-done.60, bf16[128,1024]{1,0:T(8,128)(2,1)S(1)} %and_convert_fusion.spread), custom_call_target="tpu_custom_call" | custom-call | flops 9680000000 | bytes 8800000 | tf_op jit(solution)/shard_map/pallas_call | solution.py:672
  211.0 8.7 %shard_map.211 = (bf16[1024,1024]{1,0:T(8,128)(2,1)S(1)}, bf16[1024,2048]{1,0:T(8,128)(2,1)}) custom-call(bf16[2,256,2048]{2,1,0:T(8,128)(2,1)S(1)} %broadcast_select_fusion.refs_0_, bf16[2,256,2048]{2,1,0:T(8,128)(2,1)} %collective-permute-done.13.refs_1_, bf16[2,256,2048]{2,1,0:T(8,128)(2,1)} %collective-permute-done.14.refs_2_, ...), custom_call_target="tpu_custom_call" | custom-call | flops 11879999488 | bytes 10800000 | tf_op jit(solution)/shard_map/pallas_call | solution.py:672
  228.0 8.8 %shard_map.212 = (bf16[1024,1024]{1,0:T(8,128)(2,1)S(1)}, bf16[1024,2048]{1,0:T(8,128)(2,1)}) custom-call(bf16[2,256,2048]{2,1,0:T(8,128)(2,1)S(1)} %broadcast_select_fusion.refs_0_, bf16[2,256,2048]{2,1,0:T(8,128)(2,1)} %collective-permute-done.13.refs_1_, bf16[2,256,2048]{2,1,0:T(8,128)(2,1)} %collective-permute-done.14.refs_2_, ...), custom_call_target="tpu_custom_call" | custom-call | flops 11879999488 | bytes 10800000 | tf_op jit(solution)/shard_map/pallas_call | solution.py:672
  271.4 10.4 %shard_map.215 = (bf16[1024,1024]{1,0:T(8,128)(2,1)S(1)}, bf16[1024,1024]{1,0:T(8,128)(2,1)}, bf16[1024,1024]{1,0:T(8,128)(2,1)}, f32[4,128,1024]{2,1,0:T(8,128)...) custom-call(f32[1024,1024]{1,0:T(8,128)} %get-tuple-element.190.y, ...), custom_call_target="tpu_custom_call" | custom-call | flops 13639999488 | bytes 12400000 | tf_op jit(solution)/shard_map/pallas_call | solution.py:672
  283.3 10.9 %shard_map.216 = (bf16[1024,1024]{1,0:T(8,128)(2,1)S(1)}, bf16[1024,1024]{1,0:T(8,128)(2,1)}, bf16[1024,1024]{1,0:T(8,128)(2,1)}, f32[4,128,1024]{2,1,0:T(8,128)...) custom-call(f32[1024,1024]{1,0:T(8,128)} %get-tuple-element.194.y, ...), custom_call_target="tpu_custom_call" | custom-call | flops 13639999488 | bytes 12400000 | tf_op jit(solution)/shard_map/pallas_call | solution.py:672
  313.1 15.5 %shard_map.217 = (bf16[2,256,2048]{2,1,0:T(8,128)(2,1)S(1)}, bf16[2,256,2048]{2,1,0:T(8,128)(2,1)}, bf16[2,256,2048]{2,1,0:T(8,128)(2,1)}, bf16[2,256,2048]{2,1,0:T(8,128)(2,1)}) custom-call(bf16[1024,1024]{1,0:T(8,128)(2,1)} %copy-done.75, bf16[1024,1024]{1,0:T(8,128)(2,1)} %copy-done.76, bf16[1024,2048]{1,0:T(8,128)(2,1)} %all-gather.8.cloned.1.call-done.refs_4_.refs_2_), custom_call_target="tpu_custom_call" | custom-call | flops 16720000000 | bytes 15200000 | tf_op jit(solution)/shard_map/pallas_call | solution.py:672
  338.2 13.3 %shard_map.218 = (f32[1024,1024]{1,0:T(8,128)}, f32[1024,256]{1,0:T(8,128)S(1)}) custom-call(f32[1024,1024]{1,0:T(8,128)} %get-tuple-element.206.x, bf16[1024,512]{1,0:T(8,128)(2,1)S(1)} %copy-done.67, f32[1024,256]{1,0:T(8,128)S(1)} %copy-done.72, bf16[1024,1024]{1,0:T(8,128)(2,1)} %get-tuple-element.207.dy, bf16[4,128,1024]{2,1,0:T(8,128)(2,1)S(1)} %fusion.35.start, ...), custom_call_target="tpu_custom_call" | custom-call | flops 15840000000 | bytes 14400000 | tf_op jit(solution)/shard_map/pallas_call | solution.py:672
  362.1 24.3 %shard_map.219 = bf16[8,512,1024]{2,1,0:T(8,128)(2,1)} custom-call(bf16[1024,2048]{1,0:T(8,128)(2,1)} %get-tuple-element.233.left.refs_0_.normed, bf16[1024,2048]{1,0:T(8,128)(2,1)} %get-tuple-element.173.left.refs_1_.normed, bf16[1024,1024]{1,0:T(8,128)(2,1)S(1)} %copy-done.74, bf16[1024,1024]{1,0:T(8,128)(2,1)S(1)} %copy-done.4, ...), custom_call_target="tpu_custom_call" | custom-call | flops 28160000000 | bytes 25600000 | tf_op jit(solution)/shard_map/pallas_call | solution.py:672
  393.5 21.2 %shard_map.220 = (bf16[1024,1408]{1,0:T(8,128)(2,1)}, f32[4,8,1280]{2,1,0:T(8,128)S(1)}, f32[4,8,1280]{2,1,0:T(8,128)S(1)}, f32[8,1280]{1,0:T(8,128)S(1)}, f32[8...) custom-call(bf16[1024,1408]{1,0:T(8,128)(2,1)} %get-tuple-element.214.proj, ...), custom_call_target="tpu_custom_call" | custom-call | flops 22439999488 | bytes 20400000 | tf_op jit(solution)/shard_map/pallas_call | solution.py:672
  416.0 13.5 %shard_map.221 = (f32[1024,1024]{1,0:T(8,128)}, f32[1024,256]{1,0:T(8,128)S(1)}) custom-call(f32[1024,1024]{1,0:T(8,128)} %get-tuple-element.220.x, bf16[1024,512]{1,0:T(8,128)(2,1)S(1)} %copy-done.57, f32[1024,256]{1,0:T(8,128)S(1)} %copy-done.62, bf16[1024,1024]{1,0:T(8,128)(2,1)} %get-tuple-element.221.dy, bf16[4,128,1024]{2,1,0:T(8,128)(2,1)S(1)} %fusion.34.start, ...), custom_call_target="tpu_custom_call" | custom-call | flops 15840000000 | bytes 14400000 | tf_op jit(solution)/shard_map/pallas_call | solution.py:672
  434.8 18.8 %shard_map.222 = (bf16[256,2048]{1,0:T(8,128)(2,1)S(1)}, bf16[256,2048]{1,0:T(8,128)(2,1)}, bf16[256,2048]{1,0:T(8,128)(2,1)}, bf16[256,2048]{1,0:T(8,128)(2,1)}, f32[8,2048]{1,0:T(8,128)S(1)}) custom-call(bf16[1024,1408]{1,0:T(8,128)(2,1)} %bitcast.97, bf16[1024,1024]{1,0:T(8,128)(2,1)} %get-tuple-element.210.refs_2_.gate, ...), custom_call_target="tpu_custom_call" | custom-call | flops 352000016384 | bytes 320000000 | tf_op jit(solution)/shard_map/pallas_call | solution.py:672
  458.2 20.6 %shard_map.223 = (bf16[1024,1408]{1,0:T(8,128)(2,1)}, f32[4,8,1280]{2,1,0:T(8,128)S(1)}, f32[4,8,1280]{2,1,0:T(8,128)S(1)}, f32[8,1280]{1,0:T(8,128)S(1)}, f32[8...) custom-call(bf16[1024,1408]{1,0:T(8,128)(2,1)} %get-tuple-element.226.proj, ...), custom_call_target="tpu_custom_call" | custom-call | flops 22439999488 | bytes 20400000 | tf_op jit(solution)/shard_map/pallas_call | solution.py:672
  485.7 16.7 %shard_map.224 = bf16[2048,1408]{1,0:T(8,128)(2,1)} custom-call(bf16[1024,2048]{1,0:T(8,128)(2,1)} %get-tuple-element.233.left.refs_0_.normed, bf16[1024,2048]{1,0:T(8,128)(2,1)} %get-tuple-element.173.left.refs_1_.normed, bf16[1024,1408]{1,0:T(8,128)(2,1)S(1)} %bitcast.98, bf16[1024,1408]{1,0:T(8,128)(2,1)S(1)} %bitcast.95), custom_call_target="tpu_custom_call" | custom-call | flops 880000000 | bytes 800000 | tf_op jit(solution)/shard_map/pallas_call | solution.py:672
  508.7 17.1 %shard_map.225 = (bf16[256,2048]{1,0:T(8,128)(2,1)S(1)}, bf16[256,2048]{1,0:T(8,128)(2,1)S(1)}, bf16[256,2048]{1,0:T(8,128)(2,1)S(1)}, bf16[256,2048]{1,0:T(8,128)(2,1)S(1)}, f32[8,2048]{1,0:T(8,128)S(1)}) custom-call(bf16[1024,1408]{1,0:T(8,128)(2,1)} %bitcast.94, bf16[1024,1024]{1,0:T(8,128)(2,1)} %get-tuple-element.211.refs_3_.gate, ...), custom_call_target="tpu_custom_call" | custom-call | flops 440000000 | bytes 400000 | tf_op jit(solution)/shard_map/pallas_call | solution.py:672
  589.4 14.4 %collective-permute-done.58.m1 = bf16[256,1408]{1,0:T(8,128)(2,1)S(1)} collective-permute-done((bf16[256,1408]{1,0:T(8,128)(2,1)}, bf16[256,1408]{1,0:T(8,128)(2,1)S(1)}, u32[]{:S(2)}, u32[]{:S(2)}) %collective-permute-start.58) | collective-permute-done | bytes 720928 | tf_op jit(solution)/shard_map/ppermute | solution.py:26
  (510 shorter events, 295.9 us)
Async XLA Ops:
  7.2 72.6 %all-gather.4.cloned.1.call-start = ((), (), s32[]{:S(2)}) async-start(), calls=%async_computation.2 | async-start | bytes 6488064 | tf_op jit(solution)/shard_map/all_gather | solution.py:794
  16.5 143.1 %all-gather.6.cloned.1.call-start = ((), (), s32[]{:S(2)}) async-start(), calls=%async_computation.3 | async-start | bytes 4718592 | tf_op jit(solution)/shard_map/all_gather | solution.py:795
  17.6 193.5 %all-gather.8.cloned.1.call-start = ((), (), s32[]{:S(2)}) async-start(), calls=%async_computation.4 | async-start | bytes 4718592 | tf_op jit(solution)/shard_map/all_gather | solution.py:799
  21.7 26.4 %collective-permute-start = (bf16[256,2048]{1,0:T(8,128)(2,1)}, bf16[256,2048]{1,0:T(8,128)(2,1)}, u32[]{:S(2)}, u32[]{:S(2)}) collective-permute-start(bf16[256,2048]{1,0:T(8,128)(2,1)} %get-tuple-element.147.refs_0_), channel_id=1, source_target_pairs={{0,8},{8,0},{16,24},{24,16},{1,9},{9,1},{17,25},{25,17},{2,10},{10... | collective-permute-start | bytes 3145736 | tf_op jit(solution)/shard_map/ppermute | solution.py:26
  24.6 26.4 %collective-permute-start.2 = (bf16[256,2048]{1,0:T(8,128)(2,1)}, bf16[256,2048]{1,0:T(8,128)(2,1)}, u32[]{:S(2)}, u32[]{:S(2)}) collective-permute-start(bf16[256,2048]{1,0:T(8,128)(2,1)} %get-tuple-element.147.refs_0_), channel_id=1, source_target_pairs={{0,16},{8,24},{16,0},{24,8},{1,17},{9,25},{17,1},{25,9},{2,18},{10... | collective-permute-start | bytes 3145736 | tf_op jit(solution)/shard_map/ppermute | solution.py:26
  27.0 477.0 %reduce-scatter.3.cloned.1.call-start = ((), (), s32[]{:S(2)}) async-start(), calls=%async_computation.5 | async-start | bytes 9437184 | tf_op jit(solution)/shard_map/reduce_scatter | solution.py:1025
  65.5 31.7 %collective-permute-start.4 = (bf16[256,2048]{1,0:T(8,128)(2,1)S(1)}, bf16[256,2048]{1,0:T(8,128)(2,1)}, u32[]{:S(2)}, u32[]{:S(2)}) collective-permute-start(bf16[256,2048]{1,0:T(8,128)(2,1)S(1)} %get-tuple-element.158.refs_0_), channel_id=1, source_target_pairs={{0,8},{8,0},{16,24},{24,16},{1,9},{9,1},{17,25},{25,17},{2,10},{10... | collective-permute-start | bytes 3145736 | tf_op jit(solution)/shard_map/ppermute | solution.py:26
  67.0 30.3 %collective-permute-start.5 = (bf16[256,2048]{1,0:T(8,128)(2,1)S(1)}, bf16[256,2048]{1,0:T(8,128)(2,1)}, u32[]{:S(2)}, u32[]{:S(2)}) collective-permute-start(bf16[256,2048]{1,0:T(8,128)(2,1)S(1)} %get-tuple-element.158.refs_0_), channel_id=1, source_target_pairs={{0,16},{8,24},{16,0},{24,8},{1,17},{9,25},{17,1},{25,9},{2,18},{10... | collective-permute-start | bytes 3145736 | tf_op jit(solution)/shard_map/ppermute | solution.py:26
  115.5 95.5 %collective-permute-start.13 = (bf16[2,256,2048]{2,1,0:T(8,128)(2,1)S(1)}, bf16[2,256,2048]{2,1,0:T(8,128)(2,1)}, u32[]{:S(2)}, u32[]{:S(2)}) collective-permute-start(bf16[2,256,2048]{2,1,0:T(8,128)(2,1)S(1)} %broadcast_select_fusion.refs_0_), channel_id=1, source_target_pairs={{0,8},{8,0},{16,24},{24,16},{1,9},{9,1},{17,25},{25,17},{2,10},{10... | collective-permute-start | bytes 6291464 | tf_op jit(solution)/shard_map/ppermute | solution.py:26
  117.1 93.9 %collective-permute-start.14 = (bf16[2,256,2048]{2,1,0:T(8,128)(2,1)S(1)}, bf16[2,256,2048]{2,1,0:T(8,128)(2,1)}, u32[]{:S(2)}, u32[]{:S(2)}) collective-permute-start(bf16[2,256,2048]{2,1,0:T(8,128)(2,1)S(1)} %broadcast_select_fusion.refs_0_), channel_id=1, source_target_pairs={{0,16},{8,24},{16,0},{24,8},{1,17},{9,25},{17,1},{25,9},{2,18},{10... | collective-permute-start | bytes 6291464 | tf_op jit(solution)/shard_map/ppermute | solution.py:26
  118.5 92.5 %collective-permute-start.15 = (bf16[2,256,2048]{2,1,0:T(8,128)(2,1)S(1)}, bf16[2,256,2048]{2,1,0:T(8,128)(2,1)}, u32[]{:S(2)}, u32[]{:S(2)}) collective-permute-start(bf16[2,256,2048]{2,1,0:T(8,128)(2,1)S(1)} %broadcast_select_fusion.refs_0_), channel_id=1, source_target_pairs={{0,24},{8,16},{16,8},{24,0},{1,25},{9,17},{17,9},{25,1},{2,26},{10... | collective-permute-start | bytes 6291464 | tf_op jit(solution)/shard_map/ppermute | solution.py:26
  133.5 33.7 %collective-permute-start.11 = (bf16[4,128,1024]{2,1,0:T(8,128)(2,1)}, bf16[4,128,1024]{2,1,0:T(8,128)(2,1)}, u32[]{:S(2)}, u32[]{:S(2)}) collective-permute-start(bf16[4,128,1024]{2,1,0:T(8,128)(2,1)} %fusion.12), channel_id=1, source_target_pairs={{1,3},{9,11},{17,19},{25,27}} | collective-permute-start | bytes 3145736 | tf_op jit(solution)/shard_map/ppermute | solution.py:134
  328.6 126.0 %collective-permute-start.30 = (bf16[2,256,2048]{2,1,0:T(8,128)(2,1)}, bf16[2,256,2048]{2,1,0:T(8,128)(2,1)}, u32[]{:S(2)}, u32[]{:S(2)}) collective-permute-start(bf16[2,256,2048]{2,1,0:T(8,128)(2,1)} %get-tuple-element.201), channel_id=1, source_target_pairs={{0,8},{8,0},{16,24},{24,16},{1,9},{9,1},{17,25},{25,17},{2,10},{10... | collective-permute-start | bytes 6291464 | tf_op jit(solution)/shard_map/ppermute | solution.py:26
  329.2 125.4 %collective-permute-start.31 = (bf16[2,256,2048]{2,1,0:T(8,128)(2,1)}, bf16[2,256,2048]{2,1,0:T(8,128)(2,1)}, u32[]{:S(2)}, u32[]{:S(2)}) collective-permute-start(bf16[2,256,2048]{2,1,0:T(8,128)(2,1)} %get-tuple-element.202), channel_id=1, source_target_pairs={{0,16},{8,24},{16,0},{24,8},{1,17},{9,25},{17,1},{25,9},{2,18},{10... | collective-permute-start | bytes 6291464 | tf_op jit(solution)/shard_map/ppermute | solution.py:26
  330.7 123.9 %collective-permute-start.32 = (bf16[2,256,2048]{2,1,0:T(8,128)(2,1)}, bf16[2,256,2048]{2,1,0:T(8,128)(2,1)}, u32[]{:S(2)}, u32[]{:S(2)}) collective-permute-start(bf16[2,256,2048]{2,1,0:T(8,128)(2,1)} %get-tuple-element.203), channel_id=1, source_target_pairs={{0,24},{8,16},{16,8},{24,0},{1,25},{9,17},{17,9},{25,1},{2,26},{10... | collective-permute-start | bytes 6291464 | tf_op jit(solution)/shard_map/ppermute | solution.py:26
  354.8 31.7 %collective-permute-start.41 = (bf16[4,128,1024]{2,1,0:T(8,128)(2,1)}, bf16[4,128,1024]{2,1,0:T(8,128)(2,1)}, u32[]{:S(2)}, u32[]{:S(2)}) collective-permute-start(bf16[4,128,1024]{2,1,0:T(8,128)(2,1)} %get-tuple-element.281), channel_id=1, source_target_pairs={{2,0},{10,8},{18,16},{26,24}} | collective-permute-start | bytes 3145736 | tf_op jit(solution)/shard_map/ppermute | solution.py:134
  357.6 32.7 %collective-permute-start.38 = (bf16[4,128,1024]{2,1,0:T(8,128)(2,1)}, bf16[4,128,1024]{2,1,0:T(8,128)(2,1)}, u32[]{:S(2)}, u32[]{:S(2)}) collective-permute-start(bf16[4,128,1024]{2,1,0:T(8,128)(2,1)} %add.389), channel_id=1, source_target_pairs={{0,1},{2,3},{4,5},{6,7},{8,9},{10,11},{12,13},{14,15},{16,17},{18,... | collective-permute-start | bytes 3145736 | tf_op jit(solution)/shard_map/ppermute | solution.py:142
  386.4 200.7 %reduce-scatter.5.cloned.1.call-start = ((), (), s32[]{:S(2)}) async-start(), calls=%async_computation.6 | async-start | bytes 6488064 | tf_op jit(solution)/shard_map/reduce_scatter | solution.py:1025
  388.6 41.0 %collective-permute-start.42 = (bf16[4,128,1024]{2,1,0:T(8,128)(2,1)S(1)}, bf16[4,128,1024]{2,1,0:T(8,128)(2,1)S(1)}, u32[]{:S(2)}, u32[]{:S(2)}) collective-permute-start(bf16[4,128,1024]{2,1,0:T(8,128)(2,1)S(1)} %add.394), channel_id=1, source_target_pairs={{0,1},{2,3},{4,5},{6,7},{8,9},{10,11},{12,13},{14,15},{16,17},{18,... | collective-permute-start | bytes 3145736 | tf_op jit(solution)/shard_map/ppermute | solution.py:142
  454.6 47.8 %collective-permute-start.44 = (bf16[256,2048]{1,0:T(8,128)(2,1)}, bf16[256,2048]{1,0:T(8,128)(2,1)}, u32[]{:S(2)}, u32[]{:S(2)}) collective-permute-start(bf16[256,2048]{1,0:T(8,128)(2,1)} %get-tuple-element.241), channel_id=1, source_target_pairs={{0,8},{8,0},{16,24},{24,16},{1,9},{9,1},{17,25},{25,17},{2,10},{10... | collective-permute-start | bytes 3145736 | tf_op jit(solution)/shard_map/ppermute | solution.py:26
  454.7 47.7 %collective-permute-start.45 = (bf16[256,2048]{1,0:T(8,128)(2,1)}, bf16[256,2048]{1,0:T(8,128)(2,1)}, u32[]{:S(2)}, u32[]{:S(2)}) collective-permute-start(bf16[256,2048]{1,0:T(8,128)(2,1)} %get-tuple-element.242), channel_id=1, source_target_pairs={{0,16},{8,24},{16,0},{24,8},{1,17},{9,25},{17,1},{25,9},{2,18},{10... | collective-permute-start | bytes 3145736 | tf_op jit(solution)/shard_map/ppermute | solution.py:26
  456.1 47.9 %collective-permute-start.46 = (bf16[256,2048]{1,0:T(8,128)(2,1)}, bf16[256,2048]{1,0:T(8,128)(2,1)}, u32[]{:S(2)}, u32[]{:S(2)}) collective-permute-start(bf16[256,2048]{1,0:T(8,128)(2,1)} %get-tuple-element.243), channel_id=1, source_target_pairs={{0,24},{8,16},{16,8},{24,0},{1,25},{9,17},{17,9},{25,1},{2,26},{10... | collective-permute-start | bytes 3145736 | tf_op jit(solution)/shard_map/ppermute | solution.py:26
  548.2 26.1 %collective-permute-start.51 = (bf16[256,2048]{1,0:T(8,128)(2,1)S(1)}, bf16[256,2048]{1,0:T(8,128)(2,1)S(1)}, u32[]{:S(2)}, u32[]{:S(2)}) collective-permute-start(bf16[256,2048]{1,0:T(8,128)(2,1)S(1)} %pad_maximum_fusion), channel_id=1, source_target_pairs={{0,8},{8,0},{16,24},{24,16},{1,9},{9,1},{17,25},{25,17},{2,10},{10... | collective-permute-start | bytes 3145736 | tf_op jit(solution)/shard_map/ppermute | solution.py:26
  549.9 26.2 %collective-permute-start.52 = (bf16[256,2048]{1,0:T(8,128)(2,1)S(1)}, bf16[256,2048]{1,0:T(8,128)(2,1)S(1)}, u32[]{:S(2)}, u32[]{:S(2)}) collective-permute-start(bf16[256,2048]{1,0:T(8,128)(2,1)S(1)} %pad_maximum_fusion.1), channel_id=1, source_target_pairs={{0,16},{8,24},{16,0},{24,8},{1,17},{9,25},{17,1},{25,9},{2,18},{10... | collective-permute-start | bytes 3145736 | tf_op jit(solution)/shard_map/ppermute | solution.py:26
  (155 other events, 2043.3 us)
Sparse Core Ops, SparseCore 0:
  16.6 63.1 all-gather.3
  81.3 45.8 all-gather.5
  128.8 55.2 all-gather.7
  386.6 92.8 reduce-scatter.2
  504.1 69.7 reduce-scatter.4

commit v5 on v4

--- a/solution.py
+++ b/solution.py
@@ -498,6 +498,29 @@
     dl_out[0:1, :] += -rate * jnp.sum(step_f * da, axis=0, keepdims=True)
 
 
+def share_kernel(heads, a_group, place, b0, b1, b2, b3, out):
+    last = pl.program_id(0) == pl.num_programs(0) - 1
+    for k, block in enumerate((b0, b1, b2, b3)):
+
+        @pl.when(jnp.logical_not(last) | (k < 2))
+        def _():
+            out[:, col(k)] = block[...].astype(F32).T.astype(BF16)
+
+    @pl.when(last)
+    def _():
+        rows = lax.broadcasted_iota(jnp.int32, b2.shape, 0)
+        inside = jnp.where(rows < HEADS, b2[...].astype(F32), 0.0).astype(BF16)
+        local = lax.broadcasted_iota(jnp.int32, (LANES, LANES), 0)
+        head = lax.broadcasted_iota(jnp.int32, (LANES, LANES), 1)
+        group = lax.div(local, a_group)
+        owner = (group * (HEADS // heads) + place[0]) * a_group + (local - group * a_group)
+        chosen = jnp.where((owner == head) & (local < heads), 1.0, 0.0).astype(BF16)
+        out[:, col(2)] = lax.dot_general(
+            inside, chosen, (((0,), (1,)), ((), ())), preferred_element_type=F32
+        ).astype(BF16)
+        out[:, col(3)] = jnp.zeros((out.shape[0], LANES), BF16)
+
+
 def rows_kernel(product, left, right, out):
     out[...] = product(left[...], right[...]).astype(BF16)
 
@@ -782,14 +805,39 @@
     normed = (token_rows * inverse * pre_gain).astype(BF16)
     masked = jnp.where(valid, cotangent, jnp.zeros_like(cotangent))
 
-    w_mix = jnp.concatenate(
-        [
-            pick(in_weight[:, inner : 2 * inner], HEAD_DIM),
-            in_weight[:, 2 * inner : 2 * inner + 2 * STATE],
-            lanes_of(pick(in_weight[:, 2 * inner + 2 * STATE :], 1)),
-        ],
-        axis=1,
-    )
+    rep_scalar = rep.astype(jnp.int32).reshape(1)
+    if strided and width == groups * LANES and groups % 4 == 0:
+        x_first = inner // LANES
+        x_blocks = x_first + groups * reps
+
+        def share_of(k):
+            def index(i, r):
+                at = 4 * i + k
+                return (jnp.where(at < groups, x_first + at * reps + r[0], jnp.minimum(x_blocks + at - groups, x_blocks + 2)), 0)
+
+            return pl.BlockSpec((LANES, in_weight.shape[0]), index)
+
+        w_mix = pl.pallas_call(
+            functools.partial(share_kernel, heads, heads // groups),
+            grid_spec=pltpu.PrefetchScalarGridSpec(
+                num_scalar_prefetch=1,
+                grid=(groups // 4 + 1,),
+                in_specs=[share_of(k) for k in range(4)],
+                out_specs=pl.BlockSpec((in_weight.shape[0], 4 * LANES), lambda i, r: (0, i)),
+            ),
+            out_shape=sds((in_weight.shape[0], cols), BF16),
+            compiler_params=pltpu.CompilerParams(dimension_semantics=("arbitrary",)),
+            cost_estimate=pl.CostEstimate(flops=int(4e9), bytes_accessed=int(4e6), transcendentals=0),
+        )(rep_scalar, *[in_weight.T] * 4)
+    else:
+        w_mix = jnp.concatenate(
+            [
+                pick(in_weight[:, inner : 2 * inner], HEAD_DIM),
+                in_weight[:, 2 * inner : 2 * inner + 2 * STATE],
+                lanes_of(pick(in_weight[:, 2 * inner + 2 * STATE :], 1)),
+            ],
+            axis=1,
+        )
     w_gate = pick(in_weight[:, :inner], HEAD_DIM)
     w_mix = lax.all_gather(w_mix, "seq", axis=0, tiled=True)
     w_gate = lax.all_gather(w_gate, "seq", axis=0, tiled=True)
@@ -1117,7 +1165,6 @@
     far_packed = swap(both_packed, "rep", 2)
     packed = [both_packed[0], both_packed[1], far_packed[0], far_packed[1]]
 
-    rep_scalar = rep.astype(jnp.int32).reshape(1)
     place_in = (rep_scalar, pl.BlockSpec(memory_space=pltpu.SMEM))
     local = jnp.arange(LANES, dtype=jnp.int32)
     a_group = heads // groups

time: 652 us -> 646 us (level)
    unnamed x227 -> x225, local copies, waits for them, and re-layouts: 25 us -> 24.9 us
  transfers between devices with their start and end apart: 69 -> 69, of which waited for: 21 -> 21; matrix products, arithmetic and copies ran while one was open for 12% -> 13% of each run, Pallas kernels for 46% -> 46%
where the time goes in v5:
time: 646 us; the launch traced here: 635 us
  Pallas kernels  308 us (48%)
  waiting for transfers between devices  104 us (16%)
  starting transfers between devices  98 us (15%)
  other arithmetic  64.1 us (10%)
  local copies, waits for them, and re-layouts  44.2 us (7%)
  between operations  15.9 us (2%)
    pallas_call x27, Pallas kernels, call(): pl.pallas_call(kernel, grid=(slots,), in_specs=[s for _, s in ins], out_s...  305 us
    ppermute x40, waiting for transfers between devices, swap(): lax.ppermute(value, axis, [(i, i ^ bit) for i in range(lax.axis_size(axis...  83.8 us
    ppermute x40, starting transfers between devices, swap(): lax.ppermute(value, axis, [(i, i ^ bit) for i in range(lax.axis_size(axis...  51 us
    unnamed x225, local copies, waits for them, and re-layouts  24.9 us
    convert_element_type x8, other arithmetic, hop(): (self.total.astype(F32) + self.total_fade * self.enters.astype(F32)).asty...  18.6 us
    ppermute x4, starting transfers between devices, __init__(): lax.ppermute(message, 'seq', [(2 * c + first, 2 * c + lead) for c in chips])  16.5 us
    ppermute x12, starting transfers between devices, hop(): self.enters = self.enters + lax.ppermute(onto, 'seq', [self.onward.pop(0)])  14.4 us
  transfers between devices with their start and end apart: 69, of which 21 were waited for; matrix products, arithmetic and copies ran while one was open for 13% of the time, Pallas kernels for 46%

profile of v5, /device:TPU:0, one launch (start us, length us, event | category | flops | bytes accessed | tf_op | source)
XLA Modules:
  0.0 634.7 jit_solution(1430009906340677546)
XLA Ops:
  26.2 20.2 %collective-permute-done.refs_1_ = bf16[256,2048]{1,0:T(8,128)(2,1)} collective-permute-done((bf16[256,2048]{1,0:T(8,128)(2,1)}, bf16[256,2048]{1,0:T(8,128)(2,1)}, u32[]{:S(2)}, u32[]{:S(2)}) %collective-permute-start) | collective-permute-done | bytes 1048608 | tf_op jit(solution)/shard_map/ppermute | solution.py:26
  52.1 8.5 %collective-permute-done.1.refs_3_ = bf16[128,2048]{1,0:T(8,128)(2,1)S(1)} collective-permute-done((bf16[128,2048]{1,0:T(8,128)(2,1)S(1)}, bf16[128,2048]{1,0:T(8,128)(2,1)S(1)}, u32[]{:S(2)}, u32[]{:S(2)}) %collective-permute-start.1) | collective-permute-done | bytes 524320 | tf_op jit(solution)/shard_map/ppermute | solution.py:26
  75.9 12.1 %shard_map.204 = (bf16[1024,1408]{1,0:T(8,128)(2,1)}, bf16[1024,2048]{1,0:T(8,128)(2,1)}, bf16[4,16,1280]{2,1,0:T(8,128)(2,1)}) custom-call(bf16[256,2048]{1,0:T(8,128)(2,1)} %get-tuple-element.147.refs_0_, bf16[256,2048]{1,0:T(8,128)(2,1)} %collective-permute-done.refs_1_, bf16[256,2048]{1,0:T(8,128)(2,1)} %collective-permute-done.2.refs_2_, ...), custom_call_target="tpu_custom_call" | custom-call | flops 11879999488 | bytes 10800000 | tf_op jit(solution)/shard_map/pallas_call | solution.py:695
  96.5 8.7 %shard_map.205 = (f32[1024,1024]{1,0:T(8,128)}, bf16[1024,512]{1,0:T(8,128)(2,1)S(1)}, f32[1024,256]{1,0:T(8,128)S(1)}, f32[4,128,1024]{2,1,0:T(8,128)S(1)}, bf1...) custom-call(bf16[1024,1408]{1,0:T(8,128)(2,1)} %get-tuple-element.214.proj, ...), custom_call_target="tpu_custom_call" | custom-call | flops 10119999488 | bytes 9200000 | tf_op jit(solution)/shard_map/pallas_call | solution.py:695
  113.2 11.8 %shard_map.206 = (bf16[1024,1408]{1,0:T(8,128)(2,1)}, bf16[1024,2048]{1,0:T(8,128)(2,1)}, bf16[4,16,1280]{2,1,0:T(8,128)(2,1)S(1)}) custom-call(bf16[256,2048]{1,0:T(8,128)(2,1)S(1)} %get-tuple-element.158.refs_0_, bf16[256,2048]{1,0:T(8,128)(2,1)} %collective-permute-done.4.refs_1_, bf16[256,2048]{1,0:T(8,128)(2,1)} %collective-permute-done.5.refs_2_, ...), custom_call_target="tpu_custom_call" | custom-call | flops 11879999488 | bytes 10800000 | tf_op jit(solution)/shard_map/pallas_call | solution.py:695
  129.2 8.9 %shard_map.207 = (f32[1024,1024]{1,0:T(8,128)}, bf16[1024,512]{1,0:T(8,128)(2,1)S(1)}, f32[1024,256]{1,0:T(8,128)S(1)}, f32[4,128,1024]{2,1,0:T(8,128)S(1)}, bf1...) custom-call(bf16[1024,1408]{1,0:T(8,128)(2,1)} %get-tuple-element.226.proj, ...), custom_call_target="tpu_custom_call" | custom-call | flops 10119999488 | bytes 9200000 | tf_op jit(solution)/shard_map/pallas_call | solution.py:695
  141.5 12.3 %collective-permute-start.12 = (bf16[4,144,1024]{2,1,0:T(8,128)(2,1)}, bf16[4,144,1024]{2,1,0:T(8,128)(2,1)}, u32[]{:S(2)}, u32[]{:S(2)}) collective-permute-start(bf16[4,144,1024]{2,1,0:T(8,128)(2,1)} %get-tuple-element.167), channel_id=1, source_target_pairs={{0,1},{2,3},{4,5},{6,7},{8,9},{10,11},{12,13},{14,15},{16,17},{18,... | collective-permute-start | bytes 3538952 | tf_op jit(solution)/shard_map/ppermute | solution.py:121
  167.6 9.9 %shard_map.209.y = f32[1024,1024]{1,0:T(8,128)} custom-call(f32[1024,1024]{1,0:T(8,128)} %get-tuple-element.206.x, bf16[1024,512]{1,0:T(8,128)(2,1)S(1)} %copy-done.65, f32[1024,256]{1,0:T(8,128)S(1)} %copy-done.70, bf16[128,1024]{1,0:T(8,128)(2,1)S(1)} %and_convert_fusion.spread), custom_call_target="tpu_custom_call" | custom-call | flops 9680000000 | bytes 8800000 | tf_op jit(solution)/shard_map/pallas_call | solution.py:695
  195.3 9.9 %shard_map.211.y = f32[1024,1024]{1,0:T(8,128)} custom-call(f32[1024,1024]{1,0:T(8,128)} %get-tuple-element.220.x, bf16[1024,512]{1,0:T(8,128)(2,1)S(1)} %copy-done.55, f32[1024,256]{1,0:T(8,128)S(1)} %copy-done.60, bf16[128,1024]{1,0:T(8,128)(2,1)S(1)} %and_convert_fusion.spread), custom_call_target="tpu_custom_call" | custom-call | flops 9680000000 | bytes 8800000 | tf_op jit(solution)/shard_map/pallas_call | solution.py:695
  205.3 8.7 %shard_map.212 = (bf16[1024,1024]{1,0:T(8,128)(2,1)S(1)}, bf16[1024,2048]{1,0:T(8,128)(2,1)}) custom-call(bf16[2,256,2048]{2,1,0:T(8,128)(2,1)S(1)} %broadcast_select_fusion.refs_0_, bf16[2,256,2048]{2,1,0:T(8,128)(2,1)} %collective-permute-done.13.refs_1_, bf16[2,256,2048]{2,1,0:T(8,128)(2,1)} %collective-permute-done.14.refs_2_, ...), custom_call_target="tpu_custom_call" | custom-call | flops 11879999488 | bytes 10800000 | tf_op jit(solution)/shard_map/pallas_call | solution.py:695
  222.2 8.8 %shard_map.213 = (bf16[1024,1024]{1,0:T(8,128)(2,1)S(1)}, bf16[1024,2048]{1,0:T(8,128)(2,1)}) custom-call(bf16[2,256,2048]{2,1,0:T(8,128)(2,1)S(1)} %broadcast_select_fusion.refs_0_, bf16[2,256,2048]{2,1,0:T(8,128)(2,1)} %collective-permute-done.13.refs_1_, bf16[2,256,2048]{2,1,0:T(8,128)(2,1)} %collective-permute-done.14.refs_2_, ...), custom_call_target="tpu_custom_call" | custom-call | flops 11879999488 | bytes 10800000 | tf_op jit(solution)/shard_map/pallas_call | solution.py:695
  253.7 8.3 %shard_map.215 = (f32[1024,1024]{1,0:T(8,128)}, f32[4,8,256]{2,1,0:T(8,128)S(1)}) custom-call(f32[1024,1024]{1,0:T(8,128)} %shard_map.211.y, f32[1024,1024]{1,0:T(8,128)} %get-tuple-element.220.x, bf16[1024,512]{1,0:T(8,128)(2,1)S(1)} %copy-done.56, f32[1024,256]{1,0:T(8,128)S(1)} %copy-done.61, bf16[4,128,1024]{2,1,0:T(8,128)(2,1)S(1)} %fusion.33.start, ...), custom_call_target="tpu_custom_call" | custom-call | flops 12320000000 | bytes 11200000 | tf_op jit(solution)/shard_map/pallas_call | solution.py:695
  265.5 10.4 %shard_map.216 = (bf16[1024,1024]{1,0:T(8,128)(2,1)S(1)}, bf16[1024,1024]{1,0:T(8,128)(2,1)}, bf16[1024,1024]{1,0:T(8,128)(2,1)}, f32[4,128,1024]{2,1,0:T(8,128)...) custom-call(f32[1024,1024]{1,0:T(8,128)} %get-tuple-element.190.y, ...), custom_call_target="tpu_custom_call" | custom-call | flops 13639999488 | bytes 12400000 | tf_op jit(solution)/shard_map/pallas_call | solution.py:695
  277.3 11.0 %shard_map.217 = (bf16[1024,1024]{1,0:T(8,128)(2,1)S(1)}, bf16[1024,1024]{1,0:T(8,128)(2,1)}, bf16[1024,1024]{1,0:T(8,128)(2,1)}, f32[4,128,1024]{2,1,0:T(8,128)...) custom-call(f32[1024,1024]{1,0:T(8,128)} %get-tuple-element.194.y, ...), custom_call_target="tpu_custom_call" | custom-call | flops 13639999488 | bytes 12400000 | tf_op jit(solution)/shard_map/pallas_call | solution.py:695
  307.1 15.5 %shard_map.218 = (bf16[2,256,2048]{2,1,0:T(8,128)(2,1)S(1)}, bf16[2,256,2048]{2,1,0:T(8,128)(2,1)}, bf16[2,256,2048]{2,1,0:T(8,128)(2,1)}, bf16[2,256,2048]{2,1,0:T(8,128)(2,1)}) custom-call(bf16[1024,1024]{1,0:T(8,128)(2,1)} %copy-done.75, bf16[1024,1024]{1,0:T(8,128)(2,1)} %copy-done.76, bf16[1024,2048]{1,0:T(8,128)(2,1)} %all-gather.8.cloned.1.call-done.refs_4_.refs_2_), custom_call_target="tpu_custom_call" | custom-call | flops 16720000000 | bytes 15200000 | tf_op jit(solution)/shard_map/pallas_call | solution.py:695
  332.3 13.3 %shard_map.219 = (f32[1024,1024]{1,0:T(8,128)}, f32[1024,256]{1,0:T(8,128)S(1)}) custom-call(f32[1024,1024]{1,0:T(8,128)} %get-tuple-element.206.x, bf16[1024,512]{1,0:T(8,128)(2,1)S(1)} %copy-done.67, f32[1024,256]{1,0:T(8,128)S(1)} %copy-done.72, bf16[1024,1024]{1,0:T(8,128)(2,1)} %get-tuple-element.207.dy, bf16[4,128,1024]{2,1,0:T(8,128)(2,1)S(1)} %fusion.34.start, ...), custom_call_target="tpu_custom_call" | custom-call | flops 15840000000 | bytes 14400000 | tf_op jit(solution)/shard_map/pallas_call | solution.py:695
  356.1 24.4 %shard_map.220 = bf16[8,512,1024]{2,1,0:T(8,128)(2,1)} custom-call(bf16[1024,2048]{1,0:T(8,128)(2,1)} %get-tuple-element.233.left.refs_0_.normed, bf16[1024,2048]{1,0:T(8,128)(2,1)} %get-tuple-element.173.left.refs_1_.normed, bf16[1024,1024]{1,0:T(8,128)(2,1)S(1)} %copy-done.74, bf16[1024,1024]{1,0:T(8,128)(2,1)S(1)} %copy-done.4, ...), custom_call_target="tpu_custom_call" | custom-call | flops 28160000000 | bytes 25600000 | tf_op jit(solution)/shard_map/pallas_call | solution.py:695
  387.6 21.2 %shard_map.221 = (bf16[1024,1408]{1,0:T(8,128)(2,1)}, f32[4,8,1280]{2,1,0:T(8,128)S(1)}, f32[4,8,1280]{2,1,0:T(8,128)S(1)}, f32[8,1280]{1,0:T(8,128)S(1)}, f32[8...) custom-call(bf16[1024,1408]{1,0:T(8,128)(2,1)} %get-tuple-element.214.proj, ...), custom_call_target="tpu_custom_call" | custom-call | flops 22439999488 | bytes 20400000 | tf_op jit(solution)/shard_map/pallas_call | solution.py:695
  410.1 13.5 %shard_map.222 = (f32[1024,1024]{1,0:T(8,128)}, f32[1024,256]{1,0:T(8,128)S(1)}) custom-call(f32[1024,1024]{1,0:T(8,128)} %get-tuple-element.220.x, bf16[1024,512]{1,0:T(8,128)(2,1)S(1)} %copy-done.57, f32[1024,256]{1,0:T(8,128)S(1)} %copy-done.62, bf16[1024,1024]{1,0:T(8,128)(2,1)} %get-tuple-element.221.dy, bf16[4,128,1024]{2,1,0:T(8,128)(2,1)S(1)} %fusion.33.start, ...), custom_call_target="tpu_custom_call" | custom-call | flops 15840000000 | bytes 14400000 | tf_op jit(solution)/shard_map/pallas_call | solution.py:695
  428.9 18.8 %shard_map.223 = (bf16[256,2048]{1,0:T(8,128)(2,1)S(1)}, bf16[256,2048]{1,0:T(8,128)(2,1)}, bf16[256,2048]{1,0:T(8,128)(2,1)}, bf16[256,2048]{1,0:T(8,128)(2,1)}, f32[8,2048]{1,0:T(8,128)S(1)}) custom-call(bf16[1024,1408]{1,0:T(8,128)(2,1)} %bitcast.90, bf16[1024,1024]{1,0:T(8,128)(2,1)} %get-tuple-element.210.refs_2_.gate, ...), custom_call_target="tpu_custom_call" | custom-call | flops 352000016384 | bytes 320000000 | tf_op jit(solution)/shard_map/pallas_call | solution.py:695
  452.3 20.6 %shard_map.224 = (bf16[1024,1408]{1,0:T(8,128)(2,1)}, f32[4,8,1280]{2,1,0:T(8,128)S(1)}, f32[4,8,1280]{2,1,0:T(8,128)S(1)}, f32[8,1280]{1,0:T(8,128)S(1)}, f32[8...) custom-call(bf16[1024,1408]{1,0:T(8,128)(2,1)} %get-tuple-element.226.proj, ...), custom_call_target="tpu_custom_call" | custom-call | flops 22439999488 | bytes 20400000 | tf_op jit(solution)/shard_map/pallas_call | solution.py:695
  479.8 16.8 %shard_map.225 = bf16[2048,1408]{1,0:T(8,128)(2,1)} custom-call(bf16[1024,2048]{1,0:T(8,128)(2,1)} %get-tuple-element.233.left.refs_0_.normed, bf16[1024,2048]{1,0:T(8,128)(2,1)} %get-tuple-element.173.left.refs_1_.normed, bf16[1024,1408]{1,0:T(8,128)(2,1)S(1)} %bitcast.91, bf16[1024,1408]{1,0:T(8,128)(2,1)S(1)} %bitcast.88), custom_call_target="tpu_custom_call" | custom-call | flops 880000000 | bytes 800000 | tf_op jit(solution)/shard_map/pallas_call | solution.py:695
  502.7 17.0 %shard_map.226 = (bf16[256,2048]{1,0:T(8,128)(2,1)S(1)}, bf16[256,2048]{1,0:T(8,128)(2,1)S(1)}, bf16[256,2048]{1,0:T(8,128)(2,1)S(1)}, bf16[256,2048]{1,0:T(8,128)(2,1)S(1)}, f32[8,2048]{1,0:T(8,128)S(1)}) custom-call(bf16[1024,1408]{1,0:T(8,128)(2,1)} %bitcast.87, bf16[1024,1024]{1,0:T(8,128)(2,1)} %get-tuple-element.211.refs_3_.gate, ...), custom_call_target="tpu_custom_call" | custom-call | flops 440000000 | bytes 400000 | tf_op jit(solution)/shard_map/pallas_call | solution.py:695
  583.4 14.4 %collective-permute-done.58.m1 = bf16[256,1408]{1,0:T(8,128)(2,1)S(1)} collective-permute-done((bf16[256,1408]{1,0:T(8,128)(2,1)}, bf16[256,1408]{1,0:T(8,128)(2,1)S(1)}, u32[]{:S(2)}, u32[]{:S(2)}) %collective-permute-start.58) | collective-permute-done | bytes 720928 | tf_op jit(solution)/shard_map/ppermute | solution.py:26
  (500 shorter events, 293.9 us)
Async XLA Ops:
  7.2 66.7 %all-gather.4.cloned.1.call-start = ((), (), s32[]{:S(2)}) async-start(), calls=%async_computation.2 | async-start | bytes 6488064 | tf_op jit(solution)/shard_map/all_gather | solution.py:842
  10.6 143.3 %all-gather.6.cloned.1.call-start = ((), (), s32[]{:S(2)}) async-start(), calls=%async_computation.3 | async-start | bytes 4718592 | tf_op jit(solution)/shard_map/all_gather | solution.py:843
  15.8 189.5 %all-gather.8.cloned.1.call-start = ((), (), s32[]{:S(2)}) async-start(), calls=%async_computation.4 | async-start | bytes 4718592 | tf_op jit(solution)/shard_map/all_gather | solution.py:847
  19.9 26.4 %collective-permute-start = (bf16[256,2048]{1,0:T(8,128)(2,1)}, bf16[256,2048]{1,0:T(8,128)(2,1)}, u32[]{:S(2)}, u32[]{:S(2)}) collective-permute-start(bf16[256,2048]{1,0:T(8,128)(2,1)} %get-tuple-element.147.refs_0_), channel_id=1, source_target_pairs={{0,8},{8,0},{16,24},{24,16},{1,9},{9,1},{17,25},{25,17},{2,10},{10... | collective-permute-start | bytes 3145736 | tf_op jit(solution)/shard_map/ppermute | solution.py:26
  22.9 26.4 %collective-permute-start.2 = (bf16[256,2048]{1,0:T(8,128)(2,1)}, bf16[256,2048]{1,0:T(8,128)(2,1)}, u32[]{:S(2)}, u32[]{:S(2)}) collective-permute-start(bf16[256,2048]{1,0:T(8,128)(2,1)} %get-tuple-element.147.refs_0_), channel_id=1, source_target_pairs={{0,16},{8,24},{16,0},{24,8},{1,17},{9,25},{17,1},{25,9},{2,18},{10... | collective-permute-start | bytes 3145736 | tf_op jit(solution)/shard_map/ppermute | solution.py:26
  25.2 472.8 %reduce-scatter.3.cloned.1.call-start = ((), (), s32[]{:S(2)}) async-start(), calls=%async_computation.5 | async-start | bytes 9437184 | tf_op jit(solution)/shard_map/reduce_scatter | solution.py:1073
  63.7 27.6 %collective-permute-start.4 = (bf16[256,2048]{1,0:T(8,128)(2,1)S(1)}, bf16[256,2048]{1,0:T(8,128)(2,1)}, u32[]{:S(2)}, u32[]{:S(2)}) collective-permute-start(bf16[256,2048]{1,0:T(8,128)(2,1)S(1)} %get-tuple-element.158.refs_0_), channel_id=1, source_target_pairs={{0,8},{8,0},{16,24},{24,16},{1,9},{9,1},{17,25},{25,17},{2,10},{10... | collective-permute-start | bytes 3145736 | tf_op jit(solution)/shard_map/ppermute | solution.py:26
  65.2 26.1 %collective-permute-start.5 = (bf16[256,2048]{1,0:T(8,128)(2,1)S(1)}, bf16[256,2048]{1,0:T(8,128)(2,1)}, u32[]{:S(2)}, u32[]{:S(2)}) collective-permute-start(bf16[256,2048]{1,0:T(8,128)(2,1)S(1)} %get-tuple-element.158.refs_0_), channel_id=1, source_target_pairs={{0,16},{8,24},{16,0},{24,8},{1,17},{9,25},{17,1},{25,9},{2,18},{10... | collective-permute-start | bytes 3145736 | tf_op jit(solution)/shard_map/ppermute | solution.py:26
  109.6 95.6 %collective-permute-start.13 = (bf16[2,256,2048]{2,1,0:T(8,128)(2,1)S(1)}, bf16[2,256,2048]{2,1,0:T(8,128)(2,1)}, u32[]{:S(2)}, u32[]{:S(2)}) collective-permute-start(bf16[2,256,2048]{2,1,0:T(8,128)(2,1)S(1)} %broadcast_select_fusion.refs_0_), channel_id=1, source_target_pairs={{0,8},{8,0},{16,24},{24,16},{1,9},{9,1},{17,25},{25,17},{2,10},{10... | collective-permute-start | bytes 6291464 | tf_op jit(solution)/shard_map/ppermute | solution.py:26
  111.2 94.1 %collective-permute-start.14 = (bf16[2,256,2048]{2,1,0:T(8,128)(2,1)S(1)}, bf16[2,256,2048]{2,1,0:T(8,128)(2,1)}, u32[]{:S(2)}, u32[]{:S(2)}) collective-permute-start(bf16[2,256,2048]{2,1,0:T(8,128)(2,1)S(1)} %broadcast_select_fusion.refs_0_), channel_id=1, source_target_pairs={{0,16},{8,24},{16,0},{24,8},{1,17},{9,25},{17,1},{25,9},{2,18},{10... | collective-permute-start | bytes 6291464 | tf_op jit(solution)/shard_map/ppermute | solution.py:26
  112.7 92.6 %collective-permute-start.15 = (bf16[2,256,2048]{2,1,0:T(8,128)(2,1)S(1)}, bf16[2,256,2048]{2,1,0:T(8,128)(2,1)}, u32[]{:S(2)}, u32[]{:S(2)}) collective-permute-start(bf16[2,256,2048]{2,1,0:T(8,128)(2,1)S(1)} %broadcast_select_fusion.refs_0_), channel_id=1, source_target_pairs={{0,24},{8,16},{16,8},{24,0},{1,25},{9,17},{17,9},{25,1},{2,26},{10... | collective-permute-start | bytes 6291464 | tf_op jit(solution)/shard_map/ppermute | solution.py:26
  127.6 33.8 %collective-permute-start.11 = (bf16[4,128,1024]{2,1,0:T(8,128)(2,1)}, bf16[4,128,1024]{2,1,0:T(8,128)(2,1)}, u32[]{:S(2)}, u32[]{:S(2)}) collective-permute-start(bf16[4,128,1024]{2,1,0:T(8,128)(2,1)} %fusion.12), channel_id=1, source_target_pairs={{1,3},{9,11},{17,19},{25,27}} | collective-permute-start | bytes 3145736 | tf_op jit(solution)/shard_map/ppermute | solution.py:134
  322.7 126.0 %collective-permute-start.30 = (bf16[2,256,2048]{2,1,0:T(8,128)(2,1)}, bf16[2,256,2048]{2,1,0:T(8,128)(2,1)}, u32[]{:S(2)}, u32[]{:S(2)}) collective-permute-start(bf16[2,256,2048]{2,1,0:T(8,128)(2,1)} %get-tuple-element.201), channel_id=1, source_target_pairs={{0,8},{8,0},{16,24},{24,16},{1,9},{9,1},{17,25},{25,17},{2,10},{10... | collective-permute-start | bytes 6291464 | tf_op jit(solution)/shard_map/ppermute | solution.py:26
  323.2 125.4 %collective-permute-start.31 = (bf16[2,256,2048]{2,1,0:T(8,128)(2,1)}, bf16[2,256,2048]{2,1,0:T(8,128)(2,1)}, u32[]{:S(2)}, u32[]{:S(2)}) collective-permute-start(bf16[2,256,2048]{2,1,0:T(8,128)(2,1)} %get-tuple-element.202), channel_id=1, source_target_pairs={{0,16},{8,24},{16,0},{24,8},{1,17},{9,25},{17,1},{25,9},{2,18},{10... | collective-permute-start | bytes 6291464 | tf_op jit(solution)/shard_map/ppermute | solution.py:26
  324.8 123.9 %collective-permute-start.32 = (bf16[2,256,2048]{2,1,0:T(8,128)(2,1)}, bf16[2,256,2048]{2,1,0:T(8,128)(2,1)}, u32[]{:S(2)}, u32[]{:S(2)}) collective-permute-start(bf16[2,256,2048]{2,1,0:T(8,128)(2,1)} %get-tuple-element.203), channel_id=1, source_target_pairs={{0,24},{8,16},{16,8},{24,0},{1,25},{9,17},{17,9},{25,1},{2,26},{10... | collective-permute-start | bytes 6291464 | tf_op jit(solution)/shard_map/ppermute | solution.py:26
  348.8 31.8 %collective-permute-start.41 = (bf16[4,128,1024]{2,1,0:T(8,128)(2,1)}, bf16[4,128,1024]{2,1,0:T(8,128)(2,1)}, u32[]{:S(2)}, u32[]{:S(2)}) collective-permute-start(bf16[4,128,1024]{2,1,0:T(8,128)(2,1)} %get-tuple-element.281), channel_id=1, source_target_pairs={{2,0},{10,8},{18,16},{26,24}} | collective-permute-start | bytes 3145736 | tf_op jit(solution)/shard_map/ppermute | solution.py:134
  351.7 32.8 %collective-permute-start.38 = (bf16[4,128,1024]{2,1,0:T(8,128)(2,1)}, bf16[4,128,1024]{2,1,0:T(8,128)(2,1)}, u32[]{:S(2)}, u32[]{:S(2)}) collective-permute-start(bf16[4,128,1024]{2,1,0:T(8,128)(2,1)} %add.384), channel_id=1, source_target_pairs={{0,1},{2,3},{4,5},{6,7},{8,9},{10,11},{12,13},{14,15},{16,17},{18,... | collective-permute-start | bytes 3145736 | tf_op jit(solution)/shard_map/ppermute | solution.py:142
  380.5 200.7 %reduce-scatter.5.cloned.1.call-start = ((), (), s32[]{:S(2)}) async-start(), calls=%async_computation.6 | async-start | bytes 6488064 | tf_op jit(solution)/shard_map/reduce_scatter | solution.py:1073
  382.7 41.0 %collective-permute-start.42 = (bf16[4,128,1024]{2,1,0:T(8,128)(2,1)S(1)}, bf16[4,128,1024]{2,1,0:T(8,128)(2,1)S(1)}, u32[]{:S(2)}, u32[]{:S(2)}) collective-permute-start(bf16[4,128,1024]{2,1,0:T(8,128)(2,1)S(1)} %add.389), channel_id=1, source_target_pairs={{0,1},{2,3},{4,5},{6,7},{8,9},{10,11},{12,13},{14,15},{16,17},{18,... | collective-permute-start | bytes 3145736 | tf_op jit(solution)/shard_map/ppermute | solution.py:142
  448.7 47.8 %collective-permute-start.44 = (bf16[256,2048]{1,0:T(8,128)(2,1)}, bf16[256,2048]{1,0:T(8,128)(2,1)}, u32[]{:S(2)}, u32[]{:S(2)}) collective-permute-start(bf16[256,2048]{1,0:T(8,128)(2,1)} %get-tuple-element.241), channel_id=1, source_target_pairs={{0,8},{8,0},{16,24},{24,16},{1,9},{9,1},{17,25},{25,17},{2,10},{10... | collective-permute-start | bytes 3145736 | tf_op jit(solution)/shard_map/ppermute | solution.py:26
  448.8 47.8 %collective-permute-start.45 = (bf16[256,2048]{1,0:T(8,128)(2,1)}, bf16[256,2048]{1,0:T(8,128)(2,1)}, u32[]{:S(2)}, u32[]{:S(2)}) collective-permute-start(bf16[256,2048]{1,0:T(8,128)(2,1)} %get-tuple-element.242), channel_id=1, source_target_pairs={{0,16},{8,24},{16,0},{24,8},{1,17},{9,25},{17,1},{25,9},{2,18},{10... | collective-permute-start | bytes 3145736 | tf_op jit(solution)/shard_map/ppermute | solution.py:26
  450.1 47.9 %collective-permute-start.46 = (bf16[256,2048]{1,0:T(8,128)(2,1)}, bf16[256,2048]{1,0:T(8,128)(2,1)}, u32[]{:S(2)}, u32[]{:S(2)}) collective-permute-start(bf16[256,2048]{1,0:T(8,128)(2,1)} %get-tuple-element.243), channel_id=1, source_target_pairs={{0,24},{8,16},{16,8},{24,0},{1,25},{9,17},{17,9},{25,1},{2,26},{10... | collective-permute-start | bytes 3145736 | tf_op jit(solution)/shard_map/ppermute | solution.py:26
  542.2 26.1 %collective-permute-start.51 = (bf16[256,2048]{1,0:T(8,128)(2,1)S(1)}, bf16[256,2048]{1,0:T(8,128)(2,1)S(1)}, u32[]{:S(2)}, u32[]{:S(2)}) collective-permute-start(bf16[256,2048]{1,0:T(8,128)(2,1)S(1)} %pad_maximum_fusion), channel_id=1, source_target_pairs={{0,8},{8,0},{16,24},{24,16},{1,9},{9,1},{17,25},{25,17},{2,10},{10... | collective-permute-start | bytes 3145736 | tf_op jit(solution)/shard_map/ppermute | solution.py:26
  544.0 26.2 %collective-permute-start.52 = (bf16[256,2048]{1,0:T(8,128)(2,1)S(1)}, bf16[256,2048]{1,0:T(8,128)(2,1)S(1)}, u32[]{:S(2)}, u32[]{:S(2)}) collective-permute-start(bf16[256,2048]{1,0:T(8,128)(2,1)S(1)} %pad_maximum_fusion.1), channel_id=1, source_target_pairs={{0,16},{8,24},{16,0},{24,8},{1,17},{9,25},{17,1},{25,9},{2,18},{10... | collective-permute-start | bytes 3145736 | tf_op jit(solution)/shard_map/ppermute | solution.py:26
  (153 other events, 2038.0 us)
Sparse Core Ops, SparseCore 0:
  10.7 63.1 all-gather.3
  75.4 45.8 all-gather.5
  122.9 55.2 all-gather.7
  380.7 92.8 reduce-scatter.2
  498.2 69.7 reduce-scatter.4

commit v6 on v5

--- a/solution.py
+++ b/solution.py
@@ -701,7 +701,7 @@
         scratch_shapes=scratch,
         input_output_aliases=alias or {},
         compiler_params=pltpu.CompilerParams(
-            dimension_semantics=("arbitrary",), vmem_limit_bytes=48 * 1024 * 1024
+            dimension_semantics=("arbitrary",), vmem_limit_bytes=52 * 1024 * 1024
         ),
         cost_estimate=pl.CostEstimate(
             flops=int(us * slots * 1.1e9 * COST), bytes_accessed=int(us * slots * 1e6 * COST), transcendentals=0

time: 646 us -> 637 us (0.986)
  Pallas kernels: 308 us -> 327 us
  local copies, waits for them, and re-layouts: 44.2 us -> 29.9 us
  other arithmetic: 64.1 us -> 55.3 us
    pallas_call x27, Pallas kernels: 305 us -> 324 us  [call(): pl.pallas_call(kernel, grid=(slots,), in_specs=[s for _, s in ins], out_s...]
    unnamed x225 -> x153, local copies, waits for them, and re-layouts: 24.9 us -> 6.46 us
  transfers between devices with their start and end apart: 69 -> 69, of which waited for: 21 -> 23; matrix products, arithmetic and copies ran while one was open for 13% -> 12% of each run, Pallas kernels for 46% -> 49%
where the time goes in v6:
time: 637 us; the launch traced here: 627 us
  Pallas kernels  327 us (51%)
  waiting for transfers between devices  104 us (16%)
  starting transfers between devices  95.4 us (15%)
  other arithmetic  55.3 us (9%)
  local copies, waits for them, and re-layouts  29.9 us (5%)
  between operations  15.6 us (2%)
    pallas_call x27, Pallas kernels, call(): pl.pallas_call(kernel, grid=(slots,), in_specs=[s for _, s in ins], out_s...  324 us
    ppermute x40, waiting for transfers between devices, swap(): lax.ppermute(value, axis, [(i, i ^ bit) for i in range(lax.axis_size(axis...  79.4 us
    ppermute x40, starting transfers between devices, swap(): lax.ppermute(value, axis, [(i, i ^ bit) for i in range(lax.axis_size(axis...  51.6 us
    ppermute x4, starting transfers between devices, __init__(): lax.ppermute(message, 'seq', [(2 * c + first, 2 * c + lead) for c in chips])  16.4 us
    ppermute x12, starting transfers between devices, hop(): self.enters = self.enters + lax.ppermute(onto, 'seq', [self.onward.pop(0)])  13.2 us
    convert_element_type x8, other arithmetic, hop(): (self.total.astype(F32) + self.total_fade * self.enters.astype(F32)).asty...  12.8 us
  transfers between devices with their start and end apart: 69, of which 23 were waited for; matrix products, arithmetic and copies ran while one was open for 12% of the time, Pallas kernels for 49%

profile of v6, /device:TPU:0, one launch (start us, length us, event | category | flops | bytes accessed | tf_op | source)
XLA Modules:
  0.0 626.9 jit_solution(2037053110304522667)
XLA Ops:
  26.2 20.2 %collective-permute-done.refs_1_ = bf16[256,2048]{1,0:T(8,128)(2,1)} collective-permute-done((bf16[256,2048]{1,0:T(8,128)(2,1)}, bf16[256,2048]{1,0:T(8,128)(2,1)}, u32[]{:S(2)}, u32[]{:S(2)}) %collective-permute-start) | collective-permute-done | bytes 1048608 | tf_op jit(solution)/shard_map/ppermute | solution.py:26
  64.9 8.9 %all-gather.4.cloned.1.call-done.refs_5_.w_mix = bf16[2048,1408]{1,0:T(8,128)(2,1)} async-done(((bf16[256,1408]{1,0:T(8,128)(2,1)}), bf16[2048,1408]{1,0:T(8,128)(2,1)}) %all-gather.4.cloned.1.call-update) | async-done | bytes 5767184 | tf_op jit(solution)/shard_map/all_gather | solution.py:842
  73.8 12.1 %shard_map.204 = (bf16[1024,1408]{1,0:T(8,128)(2,1)}, bf16[1024,2048]{1,0:T(8,128)(2,1)}, bf16[4,16,1280]{2,1,0:T(8,128)(2,1)S(1)}) custom-call(bf16[256,2048]{1,0:T(8,128)(2,1)} %get-tuple-element.147.refs_0_, bf16[256,2048]{1,0:T(8,128)(2,1)} %collective-permute-done.refs_1_, bf16[256,2048]{1,0:T(8,128)(2,1)} %collective-permute-done.2.refs_2_, ...), custom_call_target="tpu_custom_call" | custom-call | flops 11879999488 | bytes 10800000 | tf_op jit(solution)/shard_map/pallas_call | solution.py:695
  93.8 9.2 %shard_map.205 = (f32[1024,1024]{1,0:T(8,128)}, bf16[1024,512]{1,0:T(8,128)(2,1)S(1)}, f32[1024,256]{1,0:T(8,128)}, f32[4,128,1024]{2,1,0:T(8,128)}, bf16[4,144,...) custom-call(bf16[1024,1408]{1,0:T(8,128)(2,1)} %get-tuple-element.214.proj, ...), custom_call_target="tpu_custom_call" | custom-call | flops 10119999488 | bytes 9200000 | tf_op jit(solution)/shard_map/pallas_call | solution.py:695
  109.3 12.1 %shard_map.206 = (bf16[1024,1408]{1,0:T(8,128)(2,1)}, bf16[1024,2048]{1,0:T(8,128)(2,1)}, bf16[4,16,1280]{2,1,0:T(8,128)(2,1)S(1)}) custom-call(bf16[256,2048]{1,0:T(8,128)(2,1)} %copy-done.55, bf16[256,2048]{1,0:T(8,128)(2,1)} %collective-permute-done.4.refs_1_, bf16[256,2048]{1,0:T(8,128)(2,1)} %collective-permute-done.5.refs_2_, ...), custom_call_target="tpu_custom_call" | custom-call | flops 11879999488 | bytes 10800000 | tf_op jit(solution)/shard_map/pallas_call | solution.py:695
  125.8 9.2 %shard_map.207 = (f32[1024,1024]{1,0:T(8,128)}, bf16[1024,512]{1,0:T(8,128)(2,1)S(1)}, f32[1024,256]{1,0:T(8,128)}, f32[4,128,1024]{2,1,0:T(8,128)}, bf16[4,144,...) custom-call(bf16[1024,1408]{1,0:T(8,128)(2,1)} %get-tuple-element.226.proj, ...), custom_call_target="tpu_custom_call" | custom-call | flops 10119999488 | bytes 9200000 | tf_op jit(solution)/shard_map/pallas_call | solution.py:695
  135.0 11.9 %collective-permute-start.12 = (bf16[4,144,1024]{2,1,0:T(8,128)(2,1)}, bf16[4,144,1024]{2,1,0:T(8,128)(2,1)}, u32[]{:S(2)}, u32[]{:S(2)}) collective-permute-start(bf16[4,144,1024]{2,1,0:T(8,128)(2,1)} %get-tuple-element.167), channel_id=1, source_target_pairs={{0,1},{2,3},{4,5},{6,7},{8,9},{10,11},{12,13},{14,15},{16,17},{18,... | collective-permute-start | bytes 3538952 | tf_op jit(solution)/shard_map/ppermute | solution.py:121
  161.0 10.0 %shard_map.209.y = f32[1024,1024]{1,0:T(8,128)} custom-call(f32[1024,1024]{1,0:T(8,128)} %get-tuple-element.206.x, bf16[1024,512]{1,0:T(8,128)(2,1)S(1)} %get-tuple-element.169.bc, f32[1024,256]{1,0:T(8,128)} %get-tuple-element.170.sl, bf16[128,1024]{1,0:T(8,128)(2,1)S(1)} %and_convert_fusion.spread), custom_call_target="tpu_custom_call" | custom-call | flops 9680000000 | bytes 8800000 | tf_op jit(solution)/shard_map/pallas_call | solution.py:695
  189.0 10.0 %shard_map.211.y = f32[1024,1024]{1,0:T(8,128)} custom-call(f32[1024,1024]{1,0:T(8,128)} %get-tuple-element.220.x, bf16[1024,512]{1,0:T(8,128)(2,1)S(1)} %get-tuple-element.175.bc, f32[1024,256]{1,0:T(8,128)} %get-tuple-element.176.sl, bf16[128,1024]{1,0:T(8,128)(2,1)S(1)} %and_convert_fusion.spread), custom_call_target="tpu_custom_call" | custom-call | flops 9680000000 | bytes 8800000 | tf_op jit(solution)/shard_map/pallas_call | solution.py:695
  199.1 9.8 %shard_map.212 = (bf16[1024,1024]{1,0:T(8,128)(2,1)}, bf16[1024,2048]{1,0:T(8,128)(2,1)}) custom-call(bf16[2,256,2048]{2,1,0:T(8,128)(2,1)} %broadcast_select_fusion.refs_0_, bf16[2,256,2048]{2,1,0:T(8,128)(2,1)} %collective-permute-done.13.refs_1_, bf16[2,256,2048]{2,1,0:T(8,128)(2,1)} %collective-permute-done.14.refs_2_, ...), custom_call_target="tpu_custom_call" | custom-call | flops 11879999488 | bytes 10800000 | tf_op jit(solution)/shard_map/pallas_call | solution.py:695
  215.5 9.9 %shard_map.213 = (bf16[1024,1024]{1,0:T(8,128)(2,1)}, bf16[1024,2048]{1,0:T(8,128)(2,1)}) custom-call(bf16[2,256,2048]{2,1,0:T(8,128)(2,1)} %broadcast_select_fusion.refs_0_, bf16[2,256,2048]{2,1,0:T(8,128)(2,1)} %collective-permute-done.13.refs_1_, bf16[2,256,2048]{2,1,0:T(8,128)(2,1)} %collective-permute-done.14.refs_2_, ...), custom_call_target="tpu_custom_call" | custom-call | flops 11879999488 | bytes 10800000 | tf_op jit(solution)/shard_map/pallas_call | solution.py:695
  252.7 8.9 %shard_map.215 = (f32[1024,1024]{1,0:T(8,128)}, f32[4,8,256]{2,1,0:T(8,128)S(1)}) custom-call(f32[1024,1024]{1,0:T(8,128)} %shard_map.211.y, f32[1024,1024]{1,0:T(8,128)} %get-tuple-element.220.x, bf16[1024,512]{1,0:T(8,128)(2,1)S(1)} %get-tuple-element.175.bc, f32[1024,256]{1,0:T(8,128)} %get-tuple-element.176.sl, bf16[4,128,1024]{2,1,0:T(8,128)(2,1)} %fusion.33.start, ...), custom_call_target="tpu_custom_call" | custom-call | flops 12320000000 | bytes 11200000 | tf_op jit(solution)/shard_map/pallas_call | solution.py:695
  265.2 11.3 %shard_map.216 = (bf16[1024,1024]{1,0:T(8,128)(2,1)}, bf16[1024,1024]{1,0:T(8,128)(2,1)}, bf16[1024,1024]{1,0:T(8,128)(2,1)}, f32[4,128,1024]{2,1,0:T(8,128)}, b...) custom-call(f32[1024,1024]{1,0:T(8,128)} %get-tuple-element.190.y, ...), custom_call_target="tpu_custom_call" | custom-call | flops 13639999488 | bytes 12400000 | tf_op jit(solution)/shard_map/pallas_call | solution.py:695
  277.9 11.5 %shard_map.217 = (bf16[1024,1024]{1,0:T(8,128)(2,1)}, bf16[1024,1024]{1,0:T(8,128)(2,1)}, bf16[1024,1024]{1,0:T(8,128)(2,1)}, f32[4,128,1024]{2,1,0:T(8,128)}, b...) custom-call(f32[1024,1024]{1,0:T(8,128)} %get-tuple-element.194.y, ...), custom_call_target="tpu_custom_call" | custom-call | flops 13639999488 | bytes 12400000 | tf_op jit(solution)/shard_map/pallas_call | solution.py:695
  306.4 16.1 %shard_map.218 = (bf16[2,256,2048]{2,1,0:T(8,128)(2,1)}, bf16[2,256,2048]{2,1,0:T(8,128)(2,1)}, bf16[2,256,2048]{2,1,0:T(8,128)(2,1)}, bf16[2,256,2048]{2,1,0:T(8,128)(2,1)}) custom-call(bf16[1024,1024]{1,0:T(8,128)(2,1)} %get-tuple-element.198.refs_0_.refs_4_, bf16[1024,1024]{1,0:T(8,128)(2,1)} %get-tuple-element.199.refs_1_.refs_5_, ...), custom_call_target="tpu_custom_call" | custom-call | flops 16720000000 | bytes 15200000 | tf_op jit(solution)/shard_map/pallas_call | solution.py:695
  330.3 13.6 %shard_map.219 = (f32[1024,1024]{1,0:T(8,128)}, f32[1024,256]{1,0:T(8,128)S(1)}) custom-call(f32[1024,1024]{1,0:T(8,128)} %get-tuple-element.206.x, bf16[1024,512]{1,0:T(8,128)(2,1)} %copy-done.28, f32[1024,256]{1,0:T(8,128)} %get-tuple-element.170.sl, bf16[1024,1024]{1,0:T(8,128)(2,1)} %get-tuple-element.207.dy, bf16[4,128,1024]{2,1,0:T(8,128)(2,1)} %fusion.34.start, ...), custom_call_target="tpu_custom_call" | custom-call | flops 15840000000 | bytes 14400000 | tf_op jit(solution)/shard_map/pallas_call | solution.py:695
  350.8 25.5 %shard_map.220 = bf16[8,512,1024]{2,1,0:T(8,128)(2,1)} custom-call(bf16[1024,2048]{1,0:T(8,128)(2,1)} %get-tuple-element.233.left.refs_0_.normed, bf16[1024,2048]{1,0:T(8,128)(2,1)} %get-tuple-element.173.left.refs_1_.normed, bf16[1024,1024]{1,0:T(8,128)(2,1)} %get-tuple-element.210.refs_2_.gate, bf16[1024,1024]{1,0:T(8,128)(2,1)} %get-tuple-element.211.refs_3_.gate, ...), custom_call_target="tpu_custom_call" | custom-call | flops 28160000000 | bytes 25600000 | tf_op jit(solution)/shard_map/pallas_call | solution.py:695
  381.7 20.7 %shard_map.221 = (bf16[1024,1408]{1,0:T(8,128)(2,1)}, f32[4,8,1280]{2,1,0:T(8,128)S(1)}, f32[4,8,1280]{2,1,0:T(8,128)S(1)}, f32[8,1280]{1,0:T(8,128)S(1)}, f32[8...) custom-call(bf16[1024,1408]{1,0:T(8,128)(2,1)} %get-tuple-element.214.proj, ...), custom_call_target="tpu_custom_call" | custom-call | flops 22439999488 | bytes 20400000 | tf_op jit(solution)/shard_map/pallas_call | solution.py:695
  403.8 13.6 %shard_map.222 = (f32[1024,1024]{1,0:T(8,128)}, f32[1024,256]{1,0:T(8,128)S(1)}) custom-call(f32[1024,1024]{1,0:T(8,128)} %get-tuple-element.220.x, bf16[1024,512]{1,0:T(8,128)(2,1)} %copy-done.27, f32[1024,256]{1,0:T(8,128)} %get-tuple-element.176.sl, bf16[1024,1024]{1,0:T(8,128)(2,1)} %get-tuple-element.221.dy, bf16[4,128,1024]{2,1,0:T(8,128)(2,1)} %fusion.33.start, ...), custom_call_target="tpu_custom_call" | custom-call | flops 15840000000 | bytes 14400000 | tf_op jit(solution)/shard_map/pallas_call | solution.py:695
  422.6 18.8 %shard_map.223 = (bf16[256,2048]{1,0:T(8,128)(2,1)S(1)}, bf16[256,2048]{1,0:T(8,128)(2,1)}, bf16[256,2048]{1,0:T(8,128)(2,1)}, bf16[256,2048]{1,0:T(8,128)(2,1)}, f32[8,2048]{1,0:T(8,128)S(1)}) custom-call(bf16[1024,1408]{1,0:T(8,128)(2,1)} %bitcast.103, bf16[1024,1024]{1,0:T(8,128)(2,1)} %get-tuple-element.210.refs_2_.gate, ...), custom_call_target="tpu_custom_call" | custom-call | flops 352000016384 | bytes 320000000 | tf_op jit(solution)/shard_map/pallas_call | solution.py:695
  445.1 20.3 %shard_map.224 = (bf16[1024,1408]{1,0:T(8,128)(2,1)}, f32[4,8,1280]{2,1,0:T(8,128)S(1)}, f32[4,8,1280]{2,1,0:T(8,128)S(1)}, f32[8,1280]{1,0:T(8,128)S(1)}, f32[8...) custom-call(bf16[1024,1408]{1,0:T(8,128)(2,1)} %get-tuple-element.226.proj, ...), custom_call_target="tpu_custom_call" | custom-call | flops 22439999488 | bytes 20400000 | tf_op jit(solution)/shard_map/pallas_call | solution.py:695
  470.4 18.7 %shard_map.225 = bf16[2048,1408]{1,0:T(8,128)(2,1)} custom-call(bf16[1024,2048]{1,0:T(8,128)(2,1)} %get-tuple-element.233.left.refs_0_.normed, bf16[1024,2048]{1,0:T(8,128)(2,1)} %get-tuple-element.173.left.refs_1_.normed, bf16[1024,1408]{1,0:T(8,128)(2,1)} %bitcast.104, bf16[1024,1408]{1,0:T(8,128)(2,1)} %bitcast.98), custom_call_target="tpu_custom_call" | custom-call | flops 880000000 | bytes 800000 | tf_op jit(solution)/shard_map/pallas_call | solution.py:695
  495.4 19.2 %shard_map.226 = (bf16[256,2048]{1,0:T(8,128)(2,1)S(1)}, bf16[256,2048]{1,0:T(8,128)(2,1)}, bf16[256,2048]{1,0:T(8,128)(2,1)}, bf16[256,2048]{1,0:T(8,128)(2,1)}, f32[8,2048]{1,0:T(8,128)S(1)}) custom-call(bf16[1024,1408]{1,0:T(8,128)(2,1)} %bitcast.99, bf16[1024,1024]{1,0:T(8,128)(2,1)} %get-tuple-element.211.refs_3_.gate, ...), custom_call_target="tpu_custom_call" | custom-call | flops 440000000 | bytes 400000 | tf_op jit(solution)/shard_map/pallas_call | solution.py:695
  576.9 15.6 %collective-permute-done.58.m1 = bf16[256,1408]{1,0:T(8,128)(2,1)S(1)} collective-permute-done((bf16[256,1408]{1,0:T(8,128)(2,1)}, bf16[256,1408]{1,0:T(8,128)(2,1)S(1)}, u32[]{:S(2)}, u32[]{:S(2)}) %collective-permute-start.58) | collective-permute-done | bytes 720928 | tf_op jit(solution)/shard_map/ppermute | solution.py:26
  (428 shorter events, 274.3 us)
Async XLA Ops:
  7.2 66.7 %all-gather.4.cloned.1.call-start = ((), (), s32[]{:S(2)}) async-start(), calls=%async_computation.2 | async-start | bytes 6488064 | tf_op jit(solution)/shard_map/all_gather | solution.py:842
  10.6 136.5 %all-gather.6.cloned.1.call-start = ((), (), s32[]{:S(2)}) async-start(), calls=%async_computation.3 | async-start | bytes 4718592 | tf_op jit(solution)/shard_map/all_gather | solution.py:843
  15.8 183.3 %all-gather.8.cloned.1.call-start = ((), (), s32[]{:S(2)}) async-start(), calls=%async_computation.4 | async-start | bytes 4718592 | tf_op jit(solution)/shard_map/all_gather | solution.py:847
  19.9 26.4 %collective-permute-start = (bf16[256,2048]{1,0:T(8,128)(2,1)}, bf16[256,2048]{1,0:T(8,128)(2,1)}, u32[]{:S(2)}, u32[]{:S(2)}) collective-permute-start(bf16[256,2048]{1,0:T(8,128)(2,1)} %get-tuple-element.147.refs_0_), channel_id=1, source_target_pairs={{0,8},{8,0},{16,24},{24,16},{1,9},{9,1},{17,25},{25,17},{2,10},{10... | collective-permute-start | bytes 3145736 | tf_op jit(solution)/shard_map/ppermute | solution.py:26
  22.9 26.4 %collective-permute-start.2 = (bf16[256,2048]{1,0:T(8,128)(2,1)}, bf16[256,2048]{1,0:T(8,128)(2,1)}, u32[]{:S(2)}, u32[]{:S(2)}) collective-permute-start(bf16[256,2048]{1,0:T(8,128)(2,1)} %get-tuple-element.147.refs_0_), channel_id=1, source_target_pairs={{0,16},{8,24},{16,0},{24,8},{1,17},{9,25},{17,1},{25,9},{2,18},{10... | collective-permute-start | bytes 3145736 | tf_op jit(solution)/shard_map/ppermute | solution.py:26
  25.3 466.1 %reduce-scatter.3.cloned.1.call-start = ((), (), s32[]{:S(2)}) async-start(), calls=%async_computation.5 | async-start | bytes 9437184 | tf_op jit(solution)/shard_map/reduce_scatter | solution.py:1073
  62.9 25.7 %collective-permute-start.4 = (bf16[256,2048]{1,0:T(8,128)(2,1)S(1)}, bf16[256,2048]{1,0:T(8,128)(2,1)}, u32[]{:S(2)}, u32[]{:S(2)}) collective-permute-start(bf16[256,2048]{1,0:T(8,128)(2,1)S(1)} %get-tuple-element.158.refs_0_), channel_id=1, source_target_pairs={{0,8},{8,0},{16,24},{24,16},{1,9},{9,1},{17,25},{25,17},{2,10},{10... | collective-permute-start | bytes 3145736 | tf_op jit(solution)/shard_map/ppermute | solution.py:26
  105.7 93.3 %collective-permute-start.13 = (bf16[2,256,2048]{2,1,0:T(8,128)(2,1)}, bf16[2,256,2048]{2,1,0:T(8,128)(2,1)}, u32[]{:S(2)}, u32[]{:S(2)}) collective-permute-start(bf16[2,256,2048]{2,1,0:T(8,128)(2,1)} %broadcast_select_fusion.refs_0_), channel_id=1, source_target_pairs={{0,8},{8,0},{16,24},{24,16},{1,9},{9,1},{17,25},{25,17},{2,10},{10... | collective-permute-start | bytes 6291464 | tf_op jit(solution)/shard_map/ppermute | solution.py:26
  107.2 91.8 %collective-permute-start.14 = (bf16[2,256,2048]{2,1,0:T(8,128)(2,1)}, bf16[2,256,2048]{2,1,0:T(8,128)(2,1)}, u32[]{:S(2)}, u32[]{:S(2)}) collective-permute-start(bf16[2,256,2048]{2,1,0:T(8,128)(2,1)} %broadcast_select_fusion.refs_0_), channel_id=1, source_target_pairs={{0,16},{8,24},{16,0},{24,8},{1,17},{9,25},{17,1},{25,9},{2,18},{10... | collective-permute-start | bytes 6291464 | tf_op jit(solution)/shard_map/ppermute | solution.py:26
  108.7 90.3 %collective-permute-start.15 = (bf16[2,256,2048]{2,1,0:T(8,128)(2,1)}, bf16[2,256,2048]{2,1,0:T(8,128)(2,1)}, u32[]{:S(2)}, u32[]{:S(2)}) collective-permute-start(bf16[2,256,2048]{2,1,0:T(8,128)(2,1)} %broadcast_select_fusion.refs_0_), channel_id=1, source_target_pairs={{0,24},{8,16},{16,8},{24,0},{1,25},{9,17},{17,9},{25,1},{2,26},{10... | collective-permute-start | bytes 6291464 | tf_op jit(solution)/shard_map/ppermute | solution.py:26
  124.1 31.6 %collective-permute-start.11 = (bf16[4,128,1024]{2,1,0:T(8,128)(2,1)}, bf16[4,128,1024]{2,1,0:T(8,128)(2,1)}, u32[]{:S(2)}, u32[]{:S(2)}) collective-permute-start(bf16[4,128,1024]{2,1,0:T(8,128)(2,1)} %fusion.12), channel_id=1, source_target_pairs={{1,3},{9,11},{17,19},{25,27}} | collective-permute-start | bytes 3145736 | tf_op jit(solution)/shard_map/ppermute | solution.py:134
  160.3 25.7 %collective-permute-start.17 = (bf16[4,128,1024]{2,1,0:T(8,128)(2,1)S(1)}, bf16[4,128,1024]{2,1,0:T(8,128)(2,1)S(1)}, u32[]{:S(2)}, u32[]{:S(2)}) collective-permute-start(bf16[4,128,1024]{2,1,0:T(8,128)(2,1)S(1)} %fusion.17), channel_id=1, source_target_pairs={{1,3},{9,11},{17,19},{25,27}} | collective-permute-start | bytes 3145736 | tf_op jit(solution)/shard_map/ppermute | solution.py:134
  322.4 119.0 %collective-permute-start.30 = (bf16[2,256,2048]{2,1,0:T(8,128)(2,1)}, bf16[2,256,2048]{2,1,0:T(8,128)(2,1)}, u32[]{:S(2)}, u32[]{:S(2)}) collective-permute-start(bf16[2,256,2048]{2,1,0:T(8,128)(2,1)} %get-tuple-element.201), channel_id=1, source_target_pairs={{0,8},{8,0},{16,24},{24,16},{1,9},{9,1},{17,25},{25,17},{2,10},{10... | collective-permute-start | bytes 6291464 | tf_op jit(solution)/shard_map/ppermute | solution.py:26
  322.9 118.5 %collective-permute-start.31 = (bf16[2,256,2048]{2,1,0:T(8,128)(2,1)}, bf16[2,256,2048]{2,1,0:T(8,128)(2,1)}, u32[]{:S(2)}, u32[]{:S(2)}) collective-permute-start(bf16[2,256,2048]{2,1,0:T(8,128)(2,1)} %get-tuple-element.202), channel_id=1, source_target_pairs={{0,16},{8,24},{16,0},{24,8},{1,17},{9,25},{17,1},{25,9},{2,18},{10... | collective-permute-start | bytes 6291464 | tf_op jit(solution)/shard_map/ppermute | solution.py:26
  324.5 116.9 %collective-permute-start.32 = (bf16[2,256,2048]{2,1,0:T(8,128)(2,1)}, bf16[2,256,2048]{2,1,0:T(8,128)(2,1)}, u32[]{:S(2)}, u32[]{:S(2)}) collective-permute-start(bf16[2,256,2048]{2,1,0:T(8,128)(2,1)} %get-tuple-element.203), channel_id=1, source_target_pairs={{0,24},{8,16},{16,8},{24,0},{1,25},{9,17},{17,9},{25,1},{2,26},{10... | collective-permute-start | bytes 6291464 | tf_op jit(solution)/shard_map/ppermute | solution.py:26
  345.7 30.7 %collective-permute-start.41 = (bf16[4,128,1024]{2,1,0:T(8,128)(2,1)}, bf16[4,128,1024]{2,1,0:T(8,128)(2,1)}, u32[]{:S(2)}, u32[]{:S(2)}) collective-permute-start(bf16[4,128,1024]{2,1,0:T(8,128)(2,1)} %get-tuple-element.281), channel_id=1, source_target_pairs={{2,0},{10,8},{18,16},{26,24}} | collective-permute-start | bytes 3145736 | tf_op jit(solution)/shard_map/ppermute | solution.py:134
  347.4 32.5 %collective-permute-start.38 = (bf16[4,128,1024]{2,1,0:T(8,128)(2,1)S(1)}, bf16[4,128,1024]{2,1,0:T(8,128)(2,1)}, u32[]{:S(2)}, u32[]{:S(2)}) collective-permute-start(bf16[4,128,1024]{2,1,0:T(8,128)(2,1)S(1)} %add.384), channel_id=1, source_target_pairs={{0,1},{2,3},{4,5},{6,7},{8,9},{10,11},{12,13},{14,15},{16,17},{18,... | collective-permute-start | bytes 3145736 | tf_op jit(solution)/shard_map/ppermute | solution.py:142
  376.3 198.4 %reduce-scatter.5.cloned.1.call-start = ((), (), s32[]{:S(2)}) async-start(), calls=%async_computation.6 | async-start | bytes 6488064 | tf_op jit(solution)/shard_map/reduce_scatter | solution.py:1073
  378.1 39.2 %collective-permute-start.42 = (bf16[4,128,1024]{2,1,0:T(8,128)(2,1)S(1)}, bf16[4,128,1024]{2,1,0:T(8,128)(2,1)S(1)}, u32[]{:S(2)}, u32[]{:S(2)}) collective-permute-start(bf16[4,128,1024]{2,1,0:T(8,128)(2,1)S(1)} %add.389), channel_id=1, source_target_pairs={{0,1},{2,3},{4,5},{6,7},{8,9},{10,11},{12,13},{14,15},{16,17},{18,... | collective-permute-start | bytes 3145736 | tf_op jit(solution)/shard_map/ppermute | solution.py:142
  441.5 47.7 %collective-permute-start.44 = (bf16[256,2048]{1,0:T(8,128)(2,1)}, bf16[256,2048]{1,0:T(8,128)(2,1)S(1)}, u32[]{:S(2)}, u32[]{:S(2)}) collective-permute-start(bf16[256,2048]{1,0:T(8,128)(2,1)} %get-tuple-element.241), channel_id=1, source_target_pairs={{0,8},{8,0},{16,24},{24,16},{1,9},{9,1},{17,25},{25,17},{2,10},{10... | collective-permute-start | bytes 3145736 | tf_op jit(solution)/shard_map/ppermute | solution.py:26
  442.3 47.8 %collective-permute-start.45 = (bf16[256,2048]{1,0:T(8,128)(2,1)}, bf16[256,2048]{1,0:T(8,128)(2,1)}, u32[]{:S(2)}, u32[]{:S(2)}) collective-permute-start(bf16[256,2048]{1,0:T(8,128)(2,1)} %get-tuple-element.242), channel_id=1, source_target_pairs={{0,16},{8,24},{16,0},{24,8},{1,17},{9,25},{17,1},{25,9},{2,18},{10... | collective-permute-start | bytes 3145736 | tf_op jit(solution)/shard_map/ppermute | solution.py:26
  443.9 47.4 %collective-permute-start.46 = (bf16[256,2048]{1,0:T(8,128)(2,1)}, bf16[256,2048]{1,0:T(8,128)(2,1)}, u32[]{:S(2)}, u32[]{:S(2)}) collective-permute-start(bf16[256,2048]{1,0:T(8,128)(2,1)} %get-tuple-element.243), channel_id=1, source_target_pairs={{0,24},{8,16},{16,8},{24,0},{1,25},{9,17},{17,9},{25,1},{2,26},{10... | collective-permute-start | bytes 3145736 | tf_op jit(solution)/shard_map/ppermute | solution.py:26
  535.5 26.1 %collective-permute-start.51 = (bf16[256,2048]{1,0:T(8,128)(2,1)S(1)}, bf16[256,2048]{1,0:T(8,128)(2,1)S(1)}, u32[]{:S(2)}, u32[]{:S(2)}) collective-permute-start(bf16[256,2048]{1,0:T(8,128)(2,1)S(1)} %pad_maximum_fusion), channel_id=1, source_target_pairs={{0,8},{8,0},{16,24},{24,16},{1,9},{9,1},{17,25},{25,17},{2,10},{10... | collective-permute-start | bytes 3145736 | tf_op jit(solution)/shard_map/ppermute | solution.py:26
  536.9 26.3 %collective-permute-start.52 = (bf16[256,2048]{1,0:T(8,128)(2,1)S(1)}, bf16[256,2048]{1,0:T(8,128)(2,1)S(1)}, u32[]{:S(2)}, u32[]{:S(2)}) collective-permute-start(bf16[256,2048]{1,0:T(8,128)(2,1)S(1)} %pad_maximum_fusion.1), channel_id=1, source_target_pairs={{0,16},{8,24},{16,0},{24,8},{1,17},{9,25},{17,1},{25,9},{2,18},{10... | collective-permute-start | bytes 3145736 | tf_op jit(solution)/shard_map/ppermute | solution.py:26
  (117 other events, 3442.0 us)
Sparse Core Ops, SparseCore 0:
  10.7 63.1 all-gather.3
  75.4 45.8 all-gather.5
  122.9 53.7 all-gather.7
  376.4 89.8 reduce-scatter.2
  491.5 68.0 reduce-scatter.4
